TPU v7x, 256 devices: a whole 4x4x8 slice. The times are simulated.
256 devices in a mesh: blk: 8 (over x, y_hi), rep: 8 (over z), feat: 4 (over y_lo, core).
Axes of the slice: x: 4, y: 4 (y_hi: 2, y_lo: 2; y = y_hi * 2 + y_lo), z: 8, core: 2. Of those that a mesh axis runs over, the one named last changes fastest.
Arguments:
- features: bfloat16 [16384, 128], P(('blk', 'rep')), may hold values from -6 to 6
- weight_in: bfloat16 [128, 512], P(None, 'feat'), may hold values from -0.5 to 0.5
- bias_in: float32 [512], P('feat'), may hold values from -3 to 3
- weight_mid: bfloat16 [512, 512], P(None, 'feat'), may hold values from -0.25 to 0.25
- bias_mid: float32 [512], P('feat'), may hold values from -3 to 3
- light_tiles: bfloat16 [64, 8, 36, 128, 128], P(('blk', 'rep')), may hold values from -0.046875 to 0.046875
- light_rows: int32 [64, 8, 36], P(('blk', 'rep')), may hold values from 0 to 1
- light_cols: int32 [64, 8, 36], P(('blk', 'rep')), may hold values from 0 to 15
- heavy_tiles: bfloat16 [64, 8, 8, 128, 128], P(('blk', 'rep')), may hold values from -0.0625 to 0.0625
- heavy_slots: int32 [64, 8, 8], P(('blk', 'rep')), may hold values from 0 to 63, all different within a row; in each aligned block of 8 rows (0 to 7, 8 to 15, ..., all dimensions but the last counted through in order) at most 2 rows name the same one
- heavy_cols: int32 [64, 8, 8], P(('blk', 'rep')), may hold values from 0 to 15
- owner_map: int32 [64], P(('blk', 'rep')), may hold values from 0 to 1
Outputs:
- output: bfloat16 [16384, 512], P(('blk', 'rep'), 'feat')
Inputs may be any that keep to these rules, and one draw needn't show every extreme that they name: `heavy_slots`: the 8 heavy tiles of one group and source step name distinct heavy tile rows; among the 64 heavy tiles of one group no heavy tile row is named more than 2 times, and some row is named exactly that often. How many heavy tiles add to one heavy tile row in all differs from row to row.
All inputs are finite; a program needn't handle non-finite values.
Results may differ from a plain program's by a relative error of at most 0.0065.
Values may be sent and summed in bfloat16 or wider, within the bound.
No kernel may reach another device: no remote copies, remote signals or barrier semaphores. Data moves between devices by JAX's collectives and lax.ppermute only.
A program may use at most 192 MiB of HBM per device.

v0:
```python
import jax
import jax.numpy as jnp
from jax import lax
from jax.sharding import PartitionSpec as P


def from_behind(block, axis, distance):
    devices = range(lax.axis_size(axis))
    route = [((i - distance) % len(devices), i) for i in devices]
    return lax.ppermute(block, axis, route)


def step_terms(held, step, graph, state):
    light_tiles, light_rows, light_cols, heavy_tiles, heavy_slots, heavy_cols, owner_map = graph
    light_sum, heavy_parts, picks, received = state
    tile = light_tiles.shape[-1]
    width = held.shape[1]
    stacked = held.reshape(-1, tile, width)
    picked = jnp.take(stacked, light_cols[0, step], axis=0)
    products = jnp.einsum(
        "kij,kjf->kif", light_tiles[0, step], picked, preferred_element_type=jnp.float32
    )
    row_ids = jnp.arange(light_sum.shape[0], dtype=jnp.int32)
    onehot = (light_rows[0, step][:, None] == row_ids[None, :]).astype(jnp.float32)
    light_sum = light_sum + jnp.einsum(
        "kt,kif->tif", onehot, products, precision=lax.Precision.HIGHEST
    )
    hpicked = jnp.take(stacked, heavy_cols[0, step], axis=0)
    hproducts = jnp.einsum(
        "kij,kjf->kif", heavy_tiles[0, step], hpicked, preferred_element_type=jnp.float32
    )
    heavy_parts = heavy_parts + [(step, hproducts)]
    return (light_sum, heavy_parts, picks, received)


def aggregate(values, graph, received):
    light_tiles, light_rows, light_cols, heavy_tiles, heavy_slots, heavy_cols, owner_map = graph
    tile = light_tiles.shape[-1]
    width = values.shape[1]
    row_tiles = values.shape[0] // tile
    nblk = lax.axis_size("blk")
    groups = nblk * lax.axis_size("rep")
    light_sum = jnp.zeros((row_tiles, tile, width), jnp.float32)
    picks = None
    state = (light_sum, [], picks, received)
    block = lax.all_gather(values, "rep", axis=0, tiled=True)
    state = step_terms(block, 0, graph, state)
    forward_steps = nblk - 1
    held = block
    for step in range(1, forward_steps + 1):
        held = from_behind(held, "blk", 1)
        state = step_terms(held, step, graph, state)
    light_sum, heavy_parts, picks, received = state
    ordered = sorted(heavy_parts, key=lambda entry: entry[0])
    all_products = jnp.concatenate([entry[1] for entry in ordered], axis=0)
    slots = heavy_slots[0].reshape(-1)
    honehot = (slots[:, None] == jnp.arange(groups, dtype=jnp.int32)[None, :]).astype(jnp.float32)
    heavy_sum = jnp.einsum("kq,kif->qif", honehot, all_products, precision=lax.Precision.HIGHEST)
    heavy_own = lax.psum_scatter(heavy_sum, ("blk", "rep"), scatter_dimension=0, tiled=True)[0]
    owners = (owner_map[0] == jnp.arange(row_tiles, dtype=jnp.int32)).astype(jnp.float32)
    total = light_sum + owners[:, None, None] * heavy_own[None, :, :]
    return total.reshape(-1, width)


def per_device(
    features,
    weight_in,
    bias_in,
    weight_mid,
    bias_mid,
    light_tiles,
    light_rows,
    light_cols,
    heavy_tiles,
    heavy_slots,
    heavy_cols,
    owner_map,
):
    graph = (light_tiles, light_rows, light_cols, heavy_tiles, heavy_slots, heavy_cols, owner_map)
    received = None
    first = jnp.dot(features, weight_in, preferred_element_type=jnp.float32).astype(jnp.bfloat16)
    hidden = jnp.maximum(aggregate(first, graph, received) + bias_in, 0.0).astype(jnp.bfloat16)
    second = jnp.dot(
        lax.all_gather(hidden, "feat", axis=1, tiled=True),
        weight_mid,
        preferred_element_type=jnp.float32,
    ).astype(jnp.bfloat16)
    return (aggregate(second, graph, received) + bias_mid).astype(jnp.bfloat16)


def solution(mesh):
    in_specs = (
        P(("blk", "rep"), None),
        P(None, "feat"),
        P("feat"),
        P(None, "feat"),
        P("feat"),
        P(("blk", "rep"), None, None, None, None),
        P(("blk", "rep"), None, None),
        P(("blk", "rep"), None, None),
        P(("blk", "rep"), None, None, None, None),
        P(("blk", "rep"), None, None),
        P(("blk", "rep"), None, None),
        P(("blk", "rep")),
    )
    out_specs = P(("blk", "rep"), "feat")
    return jax.shard_map(
        per_device, mesh=mesh, in_specs=in_specs, out_specs=out_specs, check_vma=False
    )
```

profile of v0, /device:TPU:8, one launch (start us, length us, event | category | flops | bytes accessed | tf_op | source)
XLA Modules:
  0.0 1062.7 jit_solution(6890467355461804285)
XLA Ops:
  7.7 29.1 %all_gather.9 = bf16[2048,128]{1,0:T(8,128)(2,1)S(1)} all-gather(bf16[256,128]{1,0:T(8,128)(2,1)S(1)} %convolution_convert_fusion.1), channel_id=1, replica_groups=mesh['blk'=8,'rep'=8,'feat'=4] {'rep'}, dimensions={0}, use_global_device_ids=true | all-gather | bytes 589824 | tf_op jit(solution)/shard_map/all_gather | solution.py:46
  39.1 11.7 %collective-permute-done = bf16[2048,128]{1,0:T(8,128)(2,1)S(1)} collective-permute-done((bf16[2048,128]{1,0:T(8,128)(2,1)S(1)}, bf16[2048,128]{1,0:T(8,128)(2,1)S(1)}, u32[]{:S(2)}, u32[]{:S(2)}) %collective-permute-start) | collective-permute-done | bytes 524320 | tf_op jit(solution)/shard_map/ppermute | solution.py:10
  53.0 12.9 %collective-permute-done.1 = bf16[2048,128]{1,0:T(8,128)(2,1)S(1)} collective-permute-done((bf16[2048,128]{1,0:T(8,128)(2,1)S(1)}, bf16[2048,128]{1,0:T(8,128)(2,1)S(1)}, u32[]{:S(2)}, u32[]{:S(2)}) %collective-permute-start.1) | collective-permute-done | bytes 524320 | tf_op jit(solution)/shard_map/ppermute | solution.py:10
  71.2 11.0 %collective-permute-done.2 = bf16[2048,128]{1,0:T(8,128)(2,1)S(1)} collective-permute-done((bf16[2048,128]{1,0:T(8,128)(2,1)S(1)}, bf16[2048,128]{1,0:T(8,128)(2,1)S(1)}, u32[]{:S(2)}, u32[]{:S(2)}) %collective-permute-start.2) | collective-permute-done | bytes 524320 | tf_op jit(solution)/shard_map/ppermute | solution.py:10
  87.0 12.2 %collective-permute-done.3 = bf16[2048,128]{1,0:T(8,128)(2,1)} collective-permute-done((bf16[2048,128]{1,0:T(8,128)(2,1)S(1)}, bf16[2048,128]{1,0:T(8,128)(2,1)}, u32[]{:S(2)}, u32[]{:S(2)}) %collective-permute-start.3) | collective-permute-done | bytes 524320 | tf_op jit(solution)/shard_map/ppermute | solution.py:10
  109.3 8.4 collective-permute-done.4
  127.5 8.2 collective-permute-done.5
  145.1 3.9 collective-permute-done.6
  152.6 5.4 copy.61
  158.0 4.6 fusion.184
  162.6 4.4 copy.62
  198.3 3.8 convolution_bitcast_fusion.12
  207.5 3.8 convolution_bitcast_fusion.11
  226.4 3.8 convolution_bitcast_fusion.9
  242.0 288.6 %reduce-scatter.3.cloned.1.call-done = f32[1,128,128]{2,1,0:T(8,128)} async-done(((f32[64,128,128]{2,1,0:T(8,128)}), f32[1,128,128]{2,1,0:T(8,128)}) %reduce-scatter.3.cloned.1.call-update) | async-done | bytes 65552 | tf_op jit(solution)/shard_map/reduce_scatter | solution.py:59
  532.6 6.1 all_gather.10
  539.0 25.3 %all_gather.11 = bf16[2048,128]{1,0:T(8,128)(2,1)S(1)} all-gather(bf16[256,128]{1,0:T(8,128)(2,1)S(1)} %convolution_convert_fusion), channel_id=1, replica_groups=mesh['blk'=8,'rep'=8,'feat'=4] {'rep'}, dimensions={0}, use_global_device_ids=true | all-gather | bytes 589824 | tf_op jit(solution)/shard_map/all_gather | solution.py:46
  564.3 13.3 %collective-permute-done.7 = bf16[2048,128]{1,0:T(8,128)(2,1)S(1)} collective-permute-done((bf16[2048,128]{1,0:T(8,128)(2,1)S(1)}, bf16[2048,128]{1,0:T(8,128)(2,1)S(1)}, u32[]{:S(2)}, u32[]{:S(2)}) %collective-permute-start.7) | collective-permute-done | bytes 524320 | tf_op jit(solution)/shard_map/ppermute | solution.py:10
  578.3 13.5 %collective-permute-done.8 = bf16[2048,128]{1,0:T(8,128)(2,1)S(1)} collective-permute-done((bf16[2048,128]{1,0:T(8,128)(2,1)S(1)}, bf16[2048,128]{1,0:T(8,128)(2,1)S(1)}, u32[]{:S(2)}, u32[]{:S(2)}) %collective-permute-start.8) | collective-permute-done | bytes 524320 | tf_op jit(solution)/shard_map/ppermute | solution.py:10
  591.9 15.4 %collective-permute-done.9 = bf16[2048,128]{1,0:T(8,128)(2,1)S(1)} collective-permute-done((bf16[2048,128]{1,0:T(8,128)(2,1)S(1)}, bf16[2048,128]{1,0:T(8,128)(2,1)S(1)}, u32[]{:S(2)}, u32[]{:S(2)}) %collective-permute-start.9) | collective-permute-done | bytes 524320 | tf_op jit(solution)/shard_map/ppermute | solution.py:10
  608.1 15.5 %collective-permute-done.10 = bf16[2048,128]{1,0:T(8,128)(2,1)} collective-permute-done((bf16[2048,128]{1,0:T(8,128)(2,1)S(1)}, bf16[2048,128]{1,0:T(8,128)(2,1)}, u32[]{:S(2)}, u32[]{:S(2)}) %collective-permute-start.10) | collective-permute-done | bytes 524320 | tf_op jit(solution)/shard_map/ppermute | solution.py:10
  628.0 13.5 %collective-permute-done.11 = bf16[2048,128]{1,0:T(8,128)(2,1)S(1)} collective-permute-done((bf16[2048,128]{1,0:T(8,128)(2,1)}, bf16[2048,128]{1,0:T(8,128)(2,1)S(1)}, u32[]{:S(2)}, u32[]{:S(2)}) %collective-permute-start.11) | collective-permute-done | bytes 524320 | tf_op jit(solution)/shard_map/ppermute | solution.py:10
  651.1 8.8 collective-permute-done.12
  666.2 6.8 collective-permute-done.13
  676.0 5.6 copy.88
  681.6 4.6 fusion.182
  686.2 4.4 copy.89
  700.9 3.8 convolution_bitcast_fusion.6
  710.2 3.8 convolution_bitcast_fusion.5
  729.0 3.8 convolution_bitcast_fusion.3
  737.2 3.8 convolution_bitcast_fusion.2
  762.3 290.8 %reduce-scatter.5.cloned.1.call-done = f32[1,128,128]{2,1,0:T(8,128)} async-done(((f32[64,128,128]{2,1,0:T(8,128)}), f32[1,128,128]{2,1,0:T(8,128)}) %reduce-scatter.5.cloned.1.call-update) | async-done | bytes 65552 | tf_op jit(solution)/shard_map/reduce_scatter | solution.py:59
  (232 shorter events, 196.6 us)
Async XLA Ops:
  6.5 532.2 %copy-start = (bf16[512,128]{1,0:T(8,128)(2,1)S(1)}, bf16[512,128]{1,0:T(8,128)(2,1)}, u32[]{:S(2)}) copy-start(bf16[512,128]{1,0:T(8,128)(2,1)} %param.19) | copy-start | bytes 393220
  6.5 111.1 %copy-start.2 = (bf16[1,8,8,128,128]{4,3,2,1,0:T(8,128)(2,1)S(1)}, bf16[1,8,8,128,128]{4,3,2,1,0:T(8,128)(2,1)}, u32[]{:S(2)}) copy-start(bf16[1,8,8,128,128]{4,3,2,1,0:T(8,128)(2,1)} %param.24) | copy-start | bytes 6291460
  6.5 524.1 %reduce-scatter.3.cloned.1.call-start = ((), (), s32[]{:S(2)}) async-start(), calls=%async_computation.2 | async-start | bytes 4259840 | tf_op jit(solution)/shard_map/reduce_scatter | solution.py:59
  36.8 14.0 %collective-permute-start = (bf16[2048,128]{1,0:T(8,128)(2,1)S(1)}, bf16[2048,128]{1,0:T(8,128)(2,1)S(1)}, u32[]{:S(2)}, u32[]{:S(2)}) collective-permute-start(bf16[2048,128]{1,0:T(8,128)(2,1)S(1)} %all_gather.9), channel_id=1, source_target_pairs={{224,0},{0,32},{32,64},{64,96},{96,128},{128,160},{160,192},{192,2... | collective-permute-start | bytes 1572872 | tf_op jit(solution)/shard_map/ppermute | solution.py:10
  50.8 15.1 %collective-permute-start.1 = (bf16[2048,128]{1,0:T(8,128)(2,1)S(1)}, bf16[2048,128]{1,0:T(8,128)(2,1)S(1)}, u32[]{:S(2)}, u32[]{:S(2)}) collective-permute-start(bf16[2048,128]{1,0:T(8,128)(2,1)S(1)} %collective-permute-done), channel_id=1, source_target_pairs={{224,0},{0,32},{32,64},{64,96},{96,128},{128,160},{160,192},{192,2... | collective-permute-start | bytes 1572872 | tf_op jit(solution)/shard_map/ppermute | solution.py:10
  66.0 33.3 %copy-start.4 = (bf16[2048,128]{1,0:T(8,128)(2,1)}, bf16[2048,128]{1,0:T(8,128)(2,1)S(1)}, u32[]{:S(2)}) copy-start(bf16[2048,128]{1,0:T(8,128)(2,1)S(1)} %collective-permute-done.1) | copy-start | bytes 1572868
  66.0 16.2 %collective-permute-start.2 = (bf16[2048,128]{1,0:T(8,128)(2,1)S(1)}, bf16[2048,128]{1,0:T(8,128)(2,1)S(1)}, u32[]{:S(2)}, u32[]{:S(2)}) collective-permute-start(bf16[2048,128]{1,0:T(8,128)(2,1)S(1)} %collective-permute-done.1), channel_id=1, source_target_pairs={{224,0},{0,32},{32,64},{64,96},{96,128},{128,160},{160,192},{192,2... | collective-permute-start | bytes 1572872 | tf_op jit(solution)/shard_map/ppermute | solution.py:10
  82.2 17.1 %collective-permute-start.3 = (bf16[2048,128]{1,0:T(8,128)(2,1)S(1)}, bf16[2048,128]{1,0:T(8,128)(2,1)}, u32[]{:S(2)}, u32[]{:S(2)}) collective-permute-start(bf16[2048,128]{1,0:T(8,128)(2,1)S(1)} %collective-permute-done.2), channel_id=1, source_target_pairs={{224,0},{0,32},{32,64},{64,96},{96,128},{128,160},{160,192},{192,2... | collective-permute-start | bytes 1572872 | tf_op jit(solution)/shard_map/ppermute | solution.py:10
  84.6 19.4 %copy-start.9 = (s32[1024]{0:T(1024)}, s32[1024]{0:T(1024)S(1)}, u32[]{:S(2)}) copy-start(s32[1024]{0:T(1024)S(1)} %get-tuple-element.89) | copy-start | bytes 12292
  99.2 18.4 %collective-permute-start.4 = (bf16[2048,128]{1,0:T(8,128)(2,1)}, bf16[2048,128]{1,0:T(8,128)(2,1)}, u32[]{:S(2)}, u32[]{:S(2)}) collective-permute-start(bf16[2048,128]{1,0:T(8,128)(2,1)} %collective-permute-done.3), channel_id=1, source_target_pairs={{224,0},{0,32},{32,64},{64,96},{96,128},{128,160},{160,192},{192,2... | collective-permute-start | bytes 1572872 | tf_op jit(solution)/shard_map/ppermute | solution.py:10
  117.7 18.0 %collective-permute-start.5 = (bf16[2048,128]{1,0:T(8,128)(2,1)}, bf16[2048,128]{1,0:T(8,128)(2,1)}, u32[]{:S(2)}, u32[]{:S(2)}) collective-permute-start(bf16[2048,128]{1,0:T(8,128)(2,1)} %collective-permute-done.4), channel_id=1, source_target_pairs={{224,0},{0,32},{32,64},{64,96},{96,128},{128,160},{160,192},{192,2... | collective-permute-start | bytes 1572872 | tf_op jit(solution)/shard_map/ppermute | solution.py:10
  135.7 13.3 %collective-permute-start.6 = (bf16[2048,128]{1,0:T(8,128)(2,1)}, bf16[2048,128]{1,0:T(8,128)(2,1)}, u32[]{:S(2)}, u32[]{:S(2)}) collective-permute-start(bf16[2048,128]{1,0:T(8,128)(2,1)} %collective-permute-done.5), channel_id=1, source_target_pairs={{224,0},{0,32},{32,64},{64,96},{96,128},{128,160},{160,192},{192,2... | collective-permute-start | bytes 1572872 | tf_op jit(solution)/shard_map/ppermute | solution.py:10
  167.0 886.1 %reduce-scatter.5.cloned.1.call-start = ((), (), s32[]{:S(2)}) async-start(), calls=%async_computation.3 | async-start | bytes 4259840 | tf_op jit(solution)/shard_map/reduce_scatter | solution.py:59
  239.5 291.2 %copy-start.46 = (s32[36]{0:T(128)S(1)}, s32[36]{0:T(128)}, u32[]{:S(2)}) copy-start(s32[36]{0:T(128)} %get-tuple-element.39) | copy-start | bytes 436
  239.5 291.2 %copy-start.49 = (f32[2]{0:T(128)S(1)}, f32[2]{0:T(128)}, u32[]{:S(2)}) copy-start(f32[2]{0:T(128)} %compare_convert_fusion) | copy-start | bytes 28
  242.0 290.5 %copy-start.51 = (f32[128]{0:T(128)S(1)}, f32[128]{0:T(128)}, u32[]{:S(2)}) copy-start(f32[128]{0:T(128)} %param.18) | copy-start | bytes 1540
  532.5 91.8 %copy-start.3 = (bf16[1,8,8,128,128]{4,3,2,1,0:T(8,128)(2,1)S(1)}, bf16[1,8,8,128,128]{4,3,2,1,0:T(8,128)(2,1)}, u32[]{:S(2)}) copy-start(bf16[1,8,8,128,128]{4,3,2,1,0:T(8,128)(2,1)} %param.24) | copy-start | bytes 6291460
  538.9 106.2 %copy-start.31 = (pred[8]{0:T(512)(128)(4,1)S(1)}, pred[8]{0:T(512)(128)(4,1)}, u32[]{:S(2)}) copy-start(pred[8]{0:T(512)(128)(4,1)} %get-tuple-element.53) | copy-start | bytes 28
  564.3 13.3 %collective-permute-start.7 = (bf16[2048,128]{1,0:T(8,128)(2,1)S(1)}, bf16[2048,128]{1,0:T(8,128)(2,1)S(1)}, u32[]{:S(2)}, u32[]{:S(2)}) collective-permute-start(bf16[2048,128]{1,0:T(8,128)(2,1)S(1)} %all_gather.11), channel_id=1, source_target_pairs={{224,0},{0,32},{32,64},{64,96},{96,128},{128,160},{160,192},{192,2... | collective-permute-start | bytes 1572872 | tf_op jit(solution)/shard_map/ppermute | solution.py:10
  577.5 14.3 %collective-permute-start.8 = (bf16[2048,128]{1,0:T(8,128)(2,1)S(1)}, bf16[2048,128]{1,0:T(8,128)(2,1)S(1)}, u32[]{:S(2)}, u32[]{:S(2)}) collective-permute-start(bf16[2048,128]{1,0:T(8,128)(2,1)S(1)} %collective-permute-done.7), channel_id=1, source_target_pairs={{224,0},{0,32},{32,64},{64,96},{96,128},{128,160},{160,192},{192,2... | collective-permute-start | bytes 1572872 | tf_op jit(solution)/shard_map/ppermute | solution.py:10
  591.9 31.7 %copy-start.7 = (bf16[2048,128]{1,0:T(8,128)(2,1)}, bf16[2048,128]{1,0:T(8,128)(2,1)S(1)}, u32[]{:S(2)}) copy-start(bf16[2048,128]{1,0:T(8,128)(2,1)S(1)} %collective-permute-done.8) | copy-start | bytes 1572868
  591.9 15.4 %collective-permute-start.9 = (bf16[2048,128]{1,0:T(8,128)(2,1)S(1)}, bf16[2048,128]{1,0:T(8,128)(2,1)S(1)}, u32[]{:S(2)}, u32[]{:S(2)}) collective-permute-start(bf16[2048,128]{1,0:T(8,128)(2,1)S(1)} %collective-permute-done.8), channel_id=1, source_target_pairs={{224,0},{0,32},{32,64},{64,96},{96,128},{128,160},{160,192},{192,2... | collective-permute-start | bytes 1572872 | tf_op jit(solution)/shard_map/ppermute | solution.py:10
  607.3 16.3 %collective-permute-start.10 = (bf16[2048,128]{1,0:T(8,128)(2,1)S(1)}, bf16[2048,128]{1,0:T(8,128)(2,1)}, u32[]{:S(2)}, u32[]{:S(2)}) collective-permute-start(bf16[2048,128]{1,0:T(8,128)(2,1)S(1)} %collective-permute-done.9), channel_id=1, source_target_pairs={{224,0},{0,32},{32,64},{64,96},{96,128},{128,160},{160,192},{192,2... | collective-permute-start | bytes 1572872 | tf_op jit(solution)/shard_map/ppermute | solution.py:10
  623.6 17.9 %collective-permute-start.11 = (bf16[2048,128]{1,0:T(8,128)(2,1)}, bf16[2048,128]{1,0:T(8,128)(2,1)S(1)}, u32[]{:S(2)}, u32[]{:S(2)}) collective-permute-start(bf16[2048,128]{1,0:T(8,128)(2,1)} %collective-permute-done.10), channel_id=1, source_target_pairs={{224,0},{0,32},{32,64},{64,96},{96,128},{128,160},{160,192},{192,2... | collective-permute-start | bytes 1572872 | tf_op jit(solution)/shard_map/ppermute | solution.py:10
  626.2 21.9 %copy-start.30 = (pred[8]{0:T(512)(128)(4,1)S(1)}, pred[8]{0:T(512)(128)(4,1)}, u32[]{:S(2)}) copy-start(pred[8]{0:T(512)(128)(4,1)} %get-tuple-element.51) | copy-start | bytes 28
  641.5 18.4 %collective-permute-start.12 = (bf16[2048,128]{1,0:T(8,128)(2,1)S(1)}, bf16[2048,128]{1,0:T(8,128)(2,1)}, u32[]{:S(2)}, u32[]{:S(2)}) collective-permute-start(bf16[2048,128]{1,0:T(8,128)(2,1)S(1)} %collective-permute-done.11), channel_id=1, source_target_pairs={{224,0},{0,32},{32,64},{64,96},{96,128},{128,160},{160,192},{192,2... | collective-permute-start | bytes 1572872 | tf_op jit(solution)/shard_map/ppermute | solution.py:10
  643.3 16.6 %copy-start.29 = (pred[8]{0:T(512)(128)(4,1)S(1)}, pred[8]{0:T(512)(128)(4,1)}, u32[]{:S(2)}) copy-start(pred[8]{0:T(512)(128)(4,1)} %get-tuple-element.49) | copy-start | bytes 28
  659.9 13.1 %collective-permute-start.13 = (bf16[2048,128]{1,0:T(8,128)(2,1)}, bf16[2048,128]{1,0:T(8,128)(2,1)}, u32[]{:S(2)}, u32[]{:S(2)}) collective-permute-start(bf16[2048,128]{1,0:T(8,128)(2,1)} %collective-permute-done.12), channel_id=1, source_target_pairs={{224,0},{0,32},{32,64},{64,96},{96,128},{128,160},{160,192},{192,2... | collective-permute-start | bytes 1572872 | tf_op jit(solution)/shard_map/ppermute | solution.py:10
  759.7 293.4 %copy-start.47 = (s32[36]{0:T(128)S(1)}, s32[36]{0:T(128)}, u32[]{:S(2)}) copy-start(s32[36]{0:T(128)} %get-tuple-element.39) | copy-start | bytes 436
  759.7 293.4 %copy-start.50 = (f32[2]{0:T(128)S(1)}, f32[2]{0:T(128)}, u32[]{:S(2)}) copy-start(f32[2]{0:T(128)} %compare_convert_fusion) | copy-start | bytes 28
  759.7 295.9 %copy-start.1 = (bf16[512,128]{1,0:T(8,128)(2,1)S(1)}, bf16[512,128]{1,0:T(8,128)(2,1)}, u32[]{:S(2)}) copy-start(bf16[512,128]{1,0:T(8,128)(2,1)} %param.19) | copy-start | bytes 393220
  762.3 292.7 %copy-start.52 = (f32[128]{0:T(128)S(1)}, f32[128]{0:T(128)}, u32[]{:S(2)}) copy-start(f32[128]{0:T(128)} %param.20) | copy-start | bytes 1540
  (37 other events, 146.9 us)
Sparse Core Ops, SparseCore 0:
  167.1 363.5 reduce-scatter.2
  690.7 362.3 reduce-scatter.4
where the time goes:
time: 1070 us; the launch traced here: 1060 us
  waiting for transfers between devices  735 us (69%)
  matrix products  117 us (11%)
  local copies, waits for them, and re-layouts  115 us (11%)
  blocking collectives  60.6 us (6%)
  between operations  15.3 us (1%)
    reduce_scatter x2, waiting for transfers between devices, aggregate(): lax.psum_scatter(heavy_sum, ('blk', 'rep'), scatter_dimension=0, tiled=True)  579 us
    ppermute x14, waiting for transfers between devices, from_behind(): return lax.ppermute(block, axis, route)  155 us
    dot_general x16, matrix products, step_terms(): jnp.einsum('kij,kjf->kif', light_tiles[0, step], picked, preferred_elemen...  60.9 us
    all_gather x2, blocking collectives, aggregate(): block = lax.all_gather(values, 'rep', axis=0, tiled=True)  54.4 us
    dot_general x16, local copies, waits for them, and re-layouts, step_terms(): jnp.einsum('kij,kjf->kif', light_tiles[0, step], picked, preferred_elemen...  42.1 us
    dot_general x16, matrix products, step_terms(): jnp.einsum('kij,kjf->kif', heavy_tiles[0, step], hpicked, preferred_eleme...  26.3 us
    gather x16, local copies, waits for them, and re-layouts, step_terms(): picked = jnp.take(stacked, light_cols[0, step], axis=0)  25.9 us
    gather x16, local copies, waits for them, and re-layouts, step_terms(): hpicked = jnp.take(stacked, heavy_cols[0, step], axis=0)  24 us
  transfers between devices with their start and end apart: 16, of which 16 were waited for; matrix products, arithmetic and copies ran while one was open for 19% of the time, Pallas kernels for 0%

commit v1 on v0

v1 whole, which is shorter than its diff:
```python
import jax
import jax.numpy as jnp
from jax import lax
from jax.experimental import pallas as pl
from jax.experimental.pallas import tpu as pltpu
from jax.sharding import Mesh
from jax.sharding import PartitionSpec as P

BLK = ("x", "yh")
GROUP = ("x", "yh", "z")
FEAT = ("yl", "c")
PLANE = ("yh", "z")
T = 128
NB = 8
NR = 8
NG = NB * NR
NT = 2 * NG
LT = 36
HT = 8
NL = NB * LT
NH = NB * HT
SLOTS = 2 * NG
QR = T // 4
STEP = 16
NOTES = 8
CHUNKS = 4
CHUNK_STEPS = NB // CHUNKS
CHUNK = CHUNK_STEPS * LT
NX = 4
NPLANE = 2 * NR
HSTEP = 32
HELD = ((0, NPLANE), (NPLANE, NPLANE), (3 * NPLANE, NPLANE), (2 * NPLANE, NR), (2 * NPLANE + NR, NR))
BF16 = jnp.bfloat16
SMEM = pl.BlockSpec(memory_space=pltpu.SMEM)
VMEM = pl.BlockSpec(memory_space=pltpu.VMEM)
ANY = pl.BlockSpec(memory_space=pl.ANY)


def params(mib):
    return pltpu.CompilerParams(vmem_limit_bytes=mib * 1024 * 1024)


def turned(blk, source):
    return (((blk >> 1) - (source >> 1)) & 3) * 2 + (source & 1)


def around(axis, distance):
    n = lax.axis_size(axis)
    return [(i, (i + distance) % n) for i in range(n)]


def along_x(near):
    behind = lax.ppermute(near, "x", around("x", 1))
    ahead = lax.ppermute(near, "x", around("x", -1))
    far = near.shape[0] // 2
    return [
        near,
        behind,
        ahead,
        lax.ppermute(behind[:far], "x", around("x", 1)),
        lax.ppermute(ahead[far:], "x", around("x", -1)),
    ]


def swap(x, axis):
    return lax.ppermute(x, axis, around(axis, 1))


def everyone(x, axis, n):
    spread = jnp.broadcast_to(x[None], (n, *x.shape))
    return lax.all_to_all(spread, axis, 0, 0, tiled=True)


def pack_kernel(
    meta, slots, cols, rows, lcols, heavy, out, ids, places, need, trips, quarter, seats, taken, sem
):
    blk, feat = meta[0], meta[1]
    span = pl.ds(pl.multiple_of(feat * QR, QR), QR)
    copy = pltpu.make_async_copy(heavy.at[:, span, :], quarter.at[pl.ds(0, NH)], sem)
    copy.start()
    quarter[NH] = jnp.zeros((QR, T), BF16)

    def clear(q, carry):
        taken[q] = 0
        seats[2 * q] = NH
        seats[2 * q + 1] = NH
        return carry

    lax.fori_loop(0, NG, clear, 0, unroll=8)

    def seat(i, carry):
        q = slots[0, i // HT, i % HT]
        turn = taken[q]
        taken[q] = turn + 1
        seats[2 * q + turn] = i
        return carry

    lax.fori_loop(0, NH, seat, 0, unroll=8)
    lane = lax.broadcasted_iota(jnp.int32, (NOTES, T), 1)
    copy.wait()

    def node(i):
        j = jnp.minimum(i, NH - 1)
        tile = ((blk - (j >> 3)) & (NB - 1)) * 2 * NR + cols[0, j >> 3, j & (HT - 1)]
        return jnp.where(i < NH, tile, NT)

    def fill(q, carry):
        a, b = seats[2 * q], seats[2 * q + 1]
        notes = jnp.where(lane == 0, node(a), node(b)).astype(jnp.float32).astype(BF16)
        out[q] = jnp.concatenate([quarter[a], quarter[b], notes], axis=0)
        return carry

    lax.fori_loop(0, NG, fill, 0, unroll=4)

    def clear_lists(i, carry):
        for t in range(2):
            ids[t, i] = 0
            places[t, i] = NT
        return carry

    lax.fori_loop(0, NL, clear_lists, 0, unroll=8)
    for g in range(NL // STEP):
        need[g] = 0

    def put(k, carry, s, start):
        n0, n1 = carry
        row, col = rows[0, s, k], lcols[0, s, k]
        at = jnp.where(row == 0, n0, n1)
        ids[row, at] = s * LT + k
        places[row, at] = start + (col & 1) * NG + (col >> 1)
        need[at >> 4] = s // CHUNK_STEPS
        return n0 + 1 - row, n1 + row

    counts = (0, 0)
    for s in range(NB):
        start = turned(blk, (blk - s) & (NB - 1)) * NR
        counts = lax.fori_loop(0, LT, lambda k, c, s=s, v=start: put(k, c, s, v), counts, unroll=6)
    trips[0] = (jnp.maximum(counts[0], counts[1]) + STEP - 1) // STEP


def compact_kernel(hplaces, ids, places, htrips):
    def clear(i, carry):
        ids[i] = 0
        places[i] = NT
        return carry

    lax.fori_loop(0, NL, clear, 0, unroll=8)

    def put(i, n):
        place = hplaces[i]
        ids[n] = i
        places[n] = place
        return n + jnp.where(place < NT, 1, 0)

    n = lax.fori_loop(0, SLOTS, put, 0, unroll=8)
    ids[n] = 0
    places[n] = NT
    htrips[0] = (n + STEP - 1) // STEP


def dots(tile, value, count, ids, places, acc):
    for u in range(0, count, 2):
        left = jnp.concatenate([tile(ids(u)), tile(ids(u + 1))], axis=1)
        right = jnp.concatenate([value(places(u)), value(places(u + 1))], axis=0)
        acc = acc + jnp.dot(left, right, preferred_element_type=jnp.float32)
    return acc


def feature_copies(meta, parts, values, sems):
    core = meta[2]
    copies = []
    for which in range(2):
        c = core if which == 0 else 1 - core
        for (start, size), part in zip(HELD, parts[which * len(HELD) : (which + 1) * len(HELD)]):
            span = pl.ds(c * NG + start, size)
            copies.append(pltpu.make_async_copy(part, values.at[span], sems.at[len(copies)]))
    return copies


def first_kernel(meta, trips, ids, places, hplaces, light, heavy, *rest):
    parts, (out, values, tiles, htiles, sems) = rest[: 2 * len(HELD)], rest[2 * len(HELD) :]
    owner = meta[3]
    rows = pl.ds(pl.multiple_of(meta[1] * QR, QR), QR)
    copies = feature_copies(meta, parts, values, sems)
    copies.append(pltpu.make_async_copy(light.at[:, rows, :], tiles, sems.at[len(copies)]))
    for slot in range(2):
        rows, span = pl.ds(slot * QR, QR), pl.ds(slot * NG, NG)
        copies.append(
            pltpu.make_async_copy(heavy.at[:, rows, :], htiles.at[span], sems.at[len(copies)])
        )
    for copy in copies:
        copy.start()
    values[NT] = jnp.zeros((T, T), BF16)
    for copy in copies:
        copy.wait()
    value = lambda p: values[p]

    def body(g, carry):
        base = g * STEP
        return [
            dots(
                lambda i: tiles[i], value, STEP,
                lambda u: ids[t, base + u], lambda u: places[t, base + u], carry[t],
            )
            for t in range(2)
        ]

    zero = jnp.zeros((QR, T), jnp.float32)
    sums = lax.fori_loop(0, trips[0], body, [zero, zero])

    def heavy_body(g, acc):
        base = g * HSTEP
        return dots(
            lambda i: htiles[i], value, HSTEP,
            lambda u: base + u, lambda u: hplaces[base + u], acc,
        )

    hsum = lax.fori_loop(0, SLOTS // HSTEP, heavy_body, zero)
    for t in range(2):
        out[t] = (sums[t] + jnp.where(owner == t, hsum, 0.0)).astype(BF16)


def project_kernel(gathered, w_in, b_in, w_mid, mine, theirs):
    for rt in range(2):
        x = gathered[:, :, rt].reshape(-1, T)
        h = jnp.dot(x, w_in[...], preferred_element_type=jnp.float32) + b_in[...]
        h = jnp.maximum(h, 0.0).astype(BF16)
        s = jnp.dot(h, w_mid[...], preferred_element_type=jnp.float32).astype(BF16)
        mine[rt] = s[:, :T].reshape(mine.shape[1:])
        theirs[rt] = s[:, T:].reshape(theirs.shape[1:])


def second_kernel(meta, trips, htrips, need, ids, places, hids, hplaces, light, h0, h1, h2, h3, b_mid, *rest):
    parts, (out, values, tiles, htiles, sems, light_sems) = rest[: 2 * len(HELD)], rest[2 * len(HELD) :]
    core, feat, owner = meta[2], meta[1], meta[3]
    copies = []
    for which in range(2):
        c = core if which == 0 else 1 - core
        for (start, size), part in zip(HELD, parts[which * len(HELD) : (which + 1) * len(HELD)]):
            for rt in range(2):
                span = pl.ds(rt * NG + start, size)
                copies.append(
                    pltpu.make_async_copy(part.at[rt], values.at[span, :, c], sems.at[len(copies)])
                )
    first = len(copies)
    for k, h in enumerate((h0, h1, h2, h3)):
        rows = pl.ds(pl.multiple_of((feat ^ k) * QR, QR), QR)
        for slot in range(2):
            copies.append(
                pltpu.make_async_copy(
                    h.at[:, pl.ds(slot * QR, QR), :],
                    htiles.at[pl.ds(slot * NG, NG), rows, :],
                    sems.at[len(copies)],
                )
            )

    def chunk(n):
        span = pl.ds(n * CHUNK, CHUNK)
        return pltpu.make_async_copy(light.at[span], tiles.at[span], light_sems.at[n])

    for copy in copies[:first]:
        copy.start()
    for n in range(CHUNKS):
        chunk(n).start()
    for copy in copies[first:]:
        copy.start()
    values[NT] = jnp.zeros((2, 2, QR, T), BF16)
    for copy in copies[:first]:
        copy.wait()

    def wait_for(n):
        chunk(n).wait()
        return n + 1

    value = lambda p: values[p].reshape(T, T)

    def body(g, carry):
        here = lax.while_loop(lambda n: n <= need[g], wait_for, carry[2])
        base = g * STEP
        sums = [
            dots(
                lambda i: tiles[i], value, STEP,
                lambda u: ids[t, base + u], lambda u: places[t, base + u], carry[t],
            )
            for t in range(2)
        ]
        return (*sums, here)

    zero = jnp.zeros((T, T), jnp.float32)
    sum0, sum1, here = lax.fori_loop(0, trips[0], body, (zero, zero, 0))
    lax.while_loop(lambda n: n < CHUNKS, wait_for, here)
    for copy in copies[first:]:
        copy.wait()

    def heavy_body(g, acc):
        base = g * STEP
        return dots(
            lambda i: htiles[i], value, STEP, lambda u: hids[base + u], lambda u: hplaces[base + u], acc
        )

    hsum = lax.fori_loop(0, htrips[0], heavy_body, zero)
    out[:T] = (sum0 + jnp.where(owner == 0, hsum, 0.0) + b_mid[...]).astype(BF16)
    out[T:] = (sum1 + jnp.where(owner == 1, hsum, 0.0) + b_mid[...]).astype(BF16)


def per_device(
    features, weight_in, bias_in, weight_mid, bias_mid, light_tiles, light_rows, light_cols,
    heavy_tiles, heavy_slots, heavy_cols, owner_map,
):
    i32 = jnp.int32
    blk, core, feat = lax.axis_index(BLK), lax.axis_index("c"), lax.axis_index(FEAT)
    meta = jnp.stack([blk, feat, core, owner_map[0]]).astype(i32)
    light = light_tiles.reshape(NL, T, T)
    int_list = jax.ShapeDtypeStruct((NL,), i32)
    int_lists = jax.ShapeDtypeStruct((2, NL), i32)
    needs = jax.ShapeDtypeStruct((NL // STEP,), i32)
    one_int = jax.ShapeDtypeStruct((1,), i32)

    half = lax.dynamic_slice_in_dim(features, core * T, T, axis=0)
    plane = everyone(half, PLANE, NPLANE)

    packed, ids, places, need, trips = pl.pallas_call(
        pack_kernel,
        out_shape=(
            jax.ShapeDtypeStruct((NG, 2 * QR + NOTES, T), BF16), int_lists, int_lists, needs, one_int
        ),
        in_specs=[SMEM] * 5 + [ANY],
        out_specs=(VMEM, SMEM, SMEM, SMEM, SMEM),
        scratch_shapes=[
            pltpu.VMEM((NH + 1, QR, T), BF16),
            pltpu.SMEM((SLOTS,), i32),
            pltpu.SMEM((NG,), i32),
            pltpu.SemaphoreType.DMA(()),
        ],
        compiler_params=params(16),
        cost_estimate=pl.CostEstimate(flops=0, transcendentals=0, bytes_accessed=30_000_000),
        name="pack",
    )(meta, heavy_slots, heavy_cols, light_rows, light_cols, heavy_tiles.reshape(NH, T, T))
    arrived = lax.all_to_all(packed, GROUP, 0, 0, tiled=True)
    own = along_x(plane)
    held = own + [swap(part, "c") for part in own]

    nodes = arrived[:, 2 * QR, :2].T.reshape(SLOTS).astype(i32)
    hplaces = jnp.where(
        nodes < NT, (nodes & 1) * NG + turned(blk, nodes >> 4) * NR + ((nodes & 15) >> 1), NT
    )

    aggregated = pl.pallas_call(
        first_kernel,
        out_shape=jax.ShapeDtypeStruct((2, QR, T), BF16),
        in_specs=[SMEM] * 5 + [ANY] * (2 + len(held)),
        out_specs=VMEM,
        scratch_shapes=[
            pltpu.VMEM((NT + 1, T, T), BF16),
            pltpu.VMEM((NL, QR, T), BF16),
            pltpu.VMEM((SLOTS, QR, T), BF16),
            pltpu.SemaphoreType.DMA((len(held) + 3,)),
        ],
        compiler_params=params(54),
        name="aggregate_first",
    )(meta, trips, ids, places, hplaces, light, arrived, *held)

    aggregated, weight_in, bias_in, weight_mid = lax.optimization_barrier(
        (aggregated, weight_in, bias_in, weight_mid)
    )
    bias_rows = jnp.pad(bias_in.reshape(1, T), ((0, 7), (0, 0)))
    pieces = jnp.concatenate([weight_in.astype(jnp.float32), bias_rows], axis=0)
    pieces = jnp.stack([pieces, swap(pieces, "yl")])
    pieces = jnp.stack([pieces, swap(pieces, "c")], axis=1).reshape(4, T + 8, T)
    pieces = jnp.take(pieces, feat ^ jnp.arange(4), axis=0)
    w_in = jnp.moveaxis(pieces[:, :T], 0, 1).reshape(T, 4 * T).astype(BF16)
    b_in = pieces[:, T].reshape(1, 4 * T)
    w_mid = jnp.concatenate([weight_mid, swap(weight_mid, "c")], axis=1)

    rows = everyone(aggregated, (*PLANE, "yl"), 2 * NPLANE).reshape(NPLANE, 2, 2, QR, T)

    hids, hlist, htrips = pl.pallas_call(
        compact_kernel,
        out_shape=(int_list, int_list, one_int),
        in_specs=[SMEM],
        out_specs=(SMEM,) * 3,
        name="compact",
    )(hplaces)

    rows, arrived, w_in, b_in, w_mid, hids, hlist, htrips = lax.optimization_barrier(
        (rows, arrived, w_in, b_in, w_mid, hids, hlist, htrips)
    )
    hc = swap(arrived, "c")
    hy = swap(arrived, "yl")
    def project(part):
        half_values = jax.ShapeDtypeStruct((2, part.shape[0], 2, QR, T), BF16)
        return pl.pallas_call(
            project_kernel,
            out_shape=(half_values, half_values),
            in_specs=[VMEM] * 4,
            out_specs=(VMEM, VMEM),
            compiler_params=params(16),
            name="project",
        )(part, w_in, b_in, w_mid)

    behind = lax.ppermute(rows, "x", around("x", 1))
    ahead = lax.ppermute(rows, "x", around("x", -1))
    near = project(rows)
    behind, ahead, near = lax.optimization_barrier((behind, ahead, near))
    far = [
        lax.ppermute(behind[:NR], "x", around("x", 1)),
        lax.ppermute(ahead[NR:], "x", around("x", -1)),
    ]
    sides = [project(behind), project(ahead)]
    swapped = [swap(part[1], "c") for part in [near] + sides]
    far, sides, swapped = lax.optimization_barrier((far, sides, swapped))
    far = [project(part) for part in far]
    swapped += [swap(part[1], "c") for part in far]
    mine = [part[0] for part in [near] + sides + far]
    hy_late, _ = lax.optimization_barrier((hy, far))
    hyc = swap(hy_late, "c")
    return pl.pallas_call(
        second_kernel,
        out_shape=jax.ShapeDtypeStruct((2 * T, T), BF16),
        in_specs=[SMEM] * 8 + [ANY] * 5 + [VMEM] + [ANY] * len(held),
        out_specs=VMEM,
        scratch_shapes=[
            pltpu.VMEM((NT + 1, 2, 2, QR, T), BF16),
            pltpu.VMEM((NL, T, T), BF16),
            pltpu.VMEM((SLOTS, T, T), BF16),
            pltpu.SemaphoreType.DMA((2 * len(held) + 8,)),
            pltpu.SemaphoreType.DMA((CHUNKS,)),
        ],
        compiler_params=params(54),
        name="aggregate_second",
    )(
        meta, trips, htrips, need, ids, places, hids, hlist, light, arrived, hc, hy, hyc,
        bias_mid.reshape(1, T), *mine, *swapped,
    )


def solution(mesh):
    wide = Mesh(mesh.devices.reshape(4, 2, 8, 2, 2), ("x", "yh", "z", "yl", "c"))
    in_specs = (
        P(GROUP, None),
        P(None, FEAT),
        P(FEAT),
        P(None, FEAT),
        P(FEAT),
        P(GROUP, None, None, None, None),
        P(GROUP, None, None),
        P(GROUP, None, None),
        P(GROUP, None, None, None, None),
        P(GROUP, None, None),
        P(GROUP, None, None),
        P(GROUP),
    )
    return jax.shard_map(
        per_device, mesh=wide, in_specs=in_specs, out_specs=P(GROUP, FEAT), check_vma=False
    )
```

time: 1070 us -> 169 us (0.16)
  the two profiles are of different devices: /device:TPU:8 before, /device:TPU:1 now
where the time goes in v1:
time: 169 us; the launch traced here: 167 us
  starting transfers between devices  62 us (37%)
  waiting for transfers between devices  55.1 us (33%)
  Pallas kernels  37.6 us (22%)
  local copies, waits for them, and re-layouts  10.8 us (6%)
    all_to_all x2, starting transfers between devices, everyone(): return lax.all_to_all(spread, axis, 0, 0, tiled=True)  22 us
    ppermute x16, starting transfers between devices, swap(): return lax.ppermute(x, axis, around(axis, 1))  20.5 us
    all_to_all x2, waiting for transfers between devices, everyone(): return lax.all_to_all(spread, axis, 0, 0, tiled=True)  17.7 us
    ppermute x1, waiting for transfers between devices, along_x(): ahead = lax.ppermute(near, 'x', around('x', -1))  17.3 us
    pallas_call x1, Pallas kernels, per_device(): pl.pallas_call(second_kernel, out_shape=jax.ShapeDtypeStruct((2 * T, T),...  12.3 us
    pallas_call x1, Pallas kernels, per_device(): pl.pallas_call(first_kernel, out_shape=jax.ShapeDtypeStruct((2, QR, T), B...  9.46 us
    all_to_all x1, starting transfers between devices, per_device(): arrived = lax.all_to_all(packed, GROUP, 0, 0, tiled=True)  9.33 us
    pallas_call x1, Pallas kernels, per_device(): pl.pallas_call(pack_kernel, out_shape=(jax.ShapeDtypeStruct((NG, 2 * QR +...  7.89 us
  transfers between devices with their start and end apart: 27, of which 11 were waited for; matrix products, arithmetic and copies ran while one was open for 2% of the time, Pallas kernels for 9%

profile of v1, /device:TPU:1, one launch (start us, length us, event | category | flops | bytes accessed | tf_op | source)
XLA Modules:
  0.0 167.3 jit_solution(16386645194433600985)
XLA Ops:
  0.8 0.9 broadcast_in_dim.24
  1.8 11.7 %all-to-all-start.1 = ((bf16[16,128,128]{2,1,0:T(8,128)(2,1)}), bf16[16,128,128]{2,1,0:T(8,128)(2,1)S(1)}, u32[]{:S(2)}, u32[]{:S(2)}) async-start(bf16[16,128,128]{2,1,0:T(8,128)(2,1)} %broadcast_in_dim.24), calls=%async_computation.1 | async-start | bytes 1048576 | tf_op jit(solution)/shard_map/all_to_all | solution.py:71
  14.3 1.6 copy-done.1
  15.9 7.9 %pack.1 = (bf16[64,72,128]{2,1,0:T(8,128)(2,1)}, s32[2,288]{1,0:T(2,128)S(1)}, s32[2,288]{1,0:T(2,128)S(1)}, s32[18]{0:T(128)S(1)}, s32[1]{0:T(128)}) custom-call(s32[4]{0:T(128)S(1)} %pad_add_fusion.meta, s32[1,8,8]{2,1,0:T(8,128)S(1)} %copy-done.10, s32[1,8,8]{2,1,0:T(8,128)S(1)} %copy-done.11, s32[1,8,36]{2,1,0:T(8,128)S(1)} %copy-done.12, ...), custom_call_target="tpu_custom_call" | custom-call | bytes 30000000 | tf_op jit(solution)/shard_map/pack/pallas_call | solution.py:322
  25.5 3.2 %all-to-all-done.1.rest_0_ = bf16[16,128,128]{2,1,0:T(8,128)(2,1)S(1)} async-done(((bf16[16,128,128]{2,1,0:T(8,128)(2,1)}), bf16[16,128,128]{2,1,0:T(8,128)(2,1)S(1)}, u32[]{:S(2)}, u32[]{:S(2)}) %all-to-all-start.1) | async-done | bytes 524320 | tf_op jit(solution)/shard_map/all_to_all | solution.py:71
  28.8 9.3 %all-to-all-start = ((bf16[64,72,128]{2,1,0:T(8,128)(2,1)}), bf16[64,72,128]{2,1,0:T(8,128)(2,1)S(1)}, u32[]{:S(2)}, u32[]{:S(2)}) async-start(bf16[64,72,128]{2,1,0:T(8,128)(2,1)} %get-tuple-element.50), calls=%async_computation | async-start | bytes 2359296 | tf_op jit(solution)/shard_map/all_to_all | solution.py:339
  38.1 2.5 %collective-permute-start.1 = (bf16[16,128,128]{2,1,0:T(8,128)(2,1)S(1)}, bf16[16,128,128]{2,1,0:T(8,128)(2,1)S(1)}, u32[]{:S(2)}, u32[]{:S(2)}) collective-permute-start(bf16[16,128,128]{2,1,0:T(8,128)(2,1)S(1)} %all-to-all-done.1.rest_0_), channel_id=1, source_target_pairs={{0,192},{64,0},{128,64},{192,128},{1,193},{65,1},{129,65},{193,129... | collective-permute-start | bytes 1572872 | tf_op jit(solution)/shard_map/ppermute | solution.py:54
  40.6 17.3 %collective-permute-done.1.rest_2_ = bf16[16,128,128]{2,1,0:T(8,128)(2,1)S(1)} collective-permute-done((bf16[16,128,128]{2,1,0:T(8,128)(2,1)S(1)}, bf16[16,128,128]{2,1,0:T(8,128)(2,1)S(1)}, u32[]{:S(2)}, u32[]{:S(2)}) %collective-permute-start.1) | collective-permute-done | bytes 524320 | tf_op jit(solution)/shard_map/ppermute | solution.py:54
  58.0 4.2 %collective-permute-start.3 = (bf16[8,128,128]{2,1,0:T(8,128)(2,1)S(1)}, bf16[8,128,128]{2,1,0:T(8,128)(2,1)S(1)}, u32[]{:S(2)}, u32[]{:S(2)}) collective-permute-start(bf16[8,128,128]{2,1,0:T(8,128)(2,1)S(1)} %slice.33), channel_id=1, source_target_pairs={{0,192},{64,0},{128,64},{192,128},{1,193},{65,1},{129,65},{193,129... | collective-permute-start | bytes 786440 | tf_op jit(solution)/shard_map/ppermute | solution.py:61
  62.2 2.0 %collective-permute-done.rest_1_ = bf16[16,128,128]{2,1,0:T(8,128)(2,1)S(1)} collective-permute-done((bf16[16,128,128]{2,1,0:T(8,128)(2,1)S(1)}, bf16[16,128,128]{2,1,0:T(8,128)(2,1)S(1)}, u32[]{:S(2)}, u32[]{:S(2)}) %collective-permute-start) | collective-permute-done | bytes 524320 | tf_op jit(solution)/shard_map/ppermute | solution.py:53
  64.3 2.6 %collective-permute-start.4 = (bf16[16,128,128]{2,1,0:T(8,128)(2,1)S(1)}, bf16[16,128,128]{2,1,0:T(8,128)(2,1)}, u32[]{:S(2)}, u32[]{:S(2)}) collective-permute-start(bf16[16,128,128]{2,1,0:T(8,128)(2,1)S(1)} %all-to-all-done.1.rest_0_), channel_id=1, source_target_pairs={{0,1},{1,0},{2,3},{3,2},{4,5},{5,4},{6,7},{7,6},{8,9},{9,8},{10,11... | collective-permute-start | bytes 1572872 | tf_op jit(solution)/shard_map/ppermute | solution.py:66
  67.4 2.7 %collective-permute-start.8 = (bf16[8,128,128]{2,1,0:T(8,128)(2,1)S(1)}, bf16[8,128,128]{2,1,0:T(8,128)(2,1)}, u32[]{:S(2)}, u32[]{:S(2)}) collective-permute-start(bf16[8,128,128]{2,1,0:T(8,128)(2,1)S(1)} %collective-permute-done.3.rest_4_), channel_id=1, source_target_pairs={{0,1},{1,0},{2,3},{3,2},{4,5},{5,4},{6,7},{7,6},{8,9},{9,8},{10,11... | collective-permute-start | bytes 786440 | tf_op jit(solution)/shard_map/ppermute | solution.py:66
  70.1 1.1 collective-permute-done.2.rest_3_
  71.2 3.2 %collective-permute-start.7 = (bf16[8,128,128]{2,1,0:T(8,128)(2,1)S(1)}, bf16[8,128,128]{2,1,0:T(8,128)(2,1)}, u32[]{:S(2)}, u32[]{:S(2)}) collective-permute-start(bf16[8,128,128]{2,1,0:T(8,128)(2,1)S(1)} %collective-permute-done.2.rest_3_), channel_id=1, source_target_pairs={{0,1},{1,0},{2,3},{3,2},{4,5},{5,4},{6,7},{7,6},{8,9},{9,8},{10,11... | collective-permute-start | bytes 786440 | tf_op jit(solution)/shard_map/ppermute | solution.py:66
  75.8 9.5 %aggregate_first.1 = bf16[2,32,128]{2,1,0:T(8,128)(2,1)} custom-call(s32[4]{0:T(128)} %copy-done.9, s32[1]{0:T(128)} %get-tuple-element.47.trips, s32[2,288]{1,0:T(2,128)} %copy-done.7, s32[2,288]{1,0:T(2,128)} %copy-done.8, s32[128]{0:T(128)} %reshape.117.hplaces, bf16[288,128,128]{2,1,0:T(8,128)(2,1)} %bitcast.34, bf16[64,72,128]{2,1,0:T(8,128)(2,1)} %copy-done.15, ...), custom_call_target="tpu_custom_call" | custom-call | tf_op jit(solution)/shard_map/aggregate_first/pallas_call | solution.py:348
  86.6 1.6 broadcast_in_dim.25
  88.2 10.3 %all-to-all-start.2 = ((bf16[32,2,32,128]{3,2,1,0:T(8,128)(2,1)}), bf16[32,2,32,128]{3,2,1,0:T(8,128)(2,1)S(1)}, u32[]{:S(2)}, u32[]{:S(2)}) async-start(bf16[32,2,32,128]{3,2,1,0:T(8,128)(2,1)} %broadcast_in_dim.25), calls=%async_computation.2 | async-start | bytes 1048576 | tf_op jit(solution)/shard_map/all_to_all | solution.py:71
  98.9 2.2 %compact.1 = (s32[288]{0:T(512)}, s32[288]{0:T(512)}, s32[1]{0:T(128)}) custom-call(s32[128]{0:T(128)} %reshape.117.hplaces), custom_call_target="tpu_custom_call" | custom-call | tf_op jit(solution)/shard_map/compact/pallas_call | solution.py:377
  101.9 14.4 %all-to-all-done.2 = bf16[32,2,32,128]{3,2,1,0:T(8,128)(2,1)S(1)} async-done(((bf16[32,2,32,128]{3,2,1,0:T(8,128)(2,1)}), bf16[32,2,32,128]{3,2,1,0:T(8,128)(2,1)S(1)}, u32[]{:S(2)}, u32[]{:S(2)}) %all-to-all-start.2) | async-done | bytes 524320 | tf_op jit(solution)/shard_map/all_to_all | solution.py:71
  116.6 1.2 collective-permute-start.14
  117.8 1.4 project.5
  120.0 7.4 %collective-permute-done.15.gathered = bf16[16,2,2,32,128]{4,3,2,1,0:T(8,128)(2,1)S(1)} collective-permute-done((bf16[16,2,2,32,128]{4,3,2,1,0:T(8,128)(2,1)S(1)}, bf16[16,2,2,32,128]{4,3,2,1,0:T(8,128)(2,1)S(1)}, u32[]{:S(2)}, u32[]{:S(2)}) %collective-permute-start.15) | collective-permute-done | bytes 524320 | tf_op jit(solution)/shard_map/ppermute | solution.py:402
  127.4 1.2 collective-permute-done.14.gathered
  128.6 1.4 project.7
  130.3 1.4 project.6
  131.7 3.7 %collective-permute-start.19 = (bf16[2,16,2,32,128]{4,3,2,1,0:T(8,128)(2,1)S(1)}, bf16[2,16,2,32,128]{4,3,2,1,0:T(8,128)(2,1)S(1)}, u32[]{:S(2)}, u32[]{:S(2)}) collective-permute-start(bf16[2,16,2,32,128]{4,3,2,1,0:T(8,128)(2,1)S(1)} %get-tuple-element.72), channel_id=1, source_target_pairs={{0,1},{1,0},{2,3},{3,2},{4,5},{5,4},{6,7},{7,6},{8,9},{9,8},{10,11... | collective-permute-start | bytes 1572872 | tf_op jit(solution)/shard_map/ppermute | solution.py:66
  135.9 1.5 collective-permute-start.16
  137.5 5.0 %collective-permute-done.16.gathered = bf16[8,2,2,32,128]{4,3,2,1,0:T(8,128)(2,1)S(1)} collective-permute-done((bf16[8,2,2,32,128]{4,3,2,1,0:T(8,128)(2,1)S(1)}, bf16[8,2,2,32,128]{4,3,2,1,0:T(8,128)(2,1)S(1)}, u32[]{:S(2)}, u32[]{:S(2)}) %collective-permute-start.16) | collective-permute-done | bytes 262176 | tf_op jit(solution)/shard_map/ppermute | solution.py:406
  142.5 5.1 %collective-permute-start.12 = (bf16[64,72,128]{2,1,0:T(8,128)(2,1)S(1)}, bf16[64,72,128]{2,1,0:T(8,128)(2,1)S(1)}, u32[]{:S(2)}, u32[]{:S(2)}) collective-permute-start(bf16[64,72,128]{2,1,0:T(8,128)(2,1)S(1)} %copy-done.16), channel_id=1, source_target_pairs={{0,1},{1,0},{2,3},{3,2},{4,5},{5,4},{6,7},{7,6},{8,9},{9,8},{10,11... | collective-permute-start | bytes 3538952 | tf_op jit(solution)/shard_map/ppermute | solution.py:66
  147.6 0.8 project.8
  150.6 2.6 %collective-permute-done.22.rest_8_ = bf16[2,8,2,32,128]{4,3,2,1,0:T(8,128)(2,1)S(1)} collective-permute-done((bf16[2,8,2,32,128]{4,3,2,1,0:T(8,128)(2,1)S(1)}, bf16[2,8,2,32,128]{4,3,2,1,0:T(8,128)(2,1)S(1)}, u32[]{:S(2)}, u32[]{:S(2)}) %collective-permute-start.22) | collective-permute-done | bytes 262176 | tf_op jit(solution)/shard_map/ppermute | solution.py:66
  154.8 12.3 %aggregate_second.1 = bf16[256,128]{1,0:T(8,128)(2,1)} custom-call(s32[4]{0:T(128)} %copy-done.9, s32[1]{0:T(128)} %get-tuple-element.47.trips, s32[1]{0:T(128)} %get-tuple-element.58.htrips, s32[18]{0:T(128)} %copy-done.14, s32[2,288]{1,0:T(2,128)} %copy-done.7, s32[2,288]{1,0:T(2,128)} %copy-done.8, s32[288]{0:T(512)} %get-tuple-element.60.hids, ...), custom_call_target="tpu_custom_call" | custom-call | tf_op jit(solution)/shard_map/aggregate_second/pallas_call | solution.py:417
  (120 shorter events, 12.7 us)
Async XLA Ops:
  0.0 14.3 %copy-start.10 = (s32[1,8,8]{2,1,0:T(8,128)S(1)}, s32[1,8,8]{2,1,0:T(8,128)}, u32[]{:S(2)}) copy-start(s32[1,8,8]{2,1,0:T(8,128)} %slots.1) | copy-start | bytes 772
  1.8 27.0 %all-to-all-start.1 = ((bf16[16,128,128]{2,1,0:T(8,128)(2,1)}), bf16[16,128,128]{2,1,0:T(8,128)(2,1)S(1)}, u32[]{:S(2)}, u32[]{:S(2)}) async-start(bf16[16,128,128]{2,1,0:T(8,128)(2,1)} %broadcast_in_dim.24), calls=%async_computation.1 | async-start | bytes 1048576 | tf_op jit(solution)/shard_map/all_to_all | solution.py:71
  14.2 14.5 %copy-start.9 = (s32[4]{0:T(128)}, s32[4]{0:T(128)S(1)}, u32[]{:S(2)}) copy-start(s32[4]{0:T(128)S(1)} %pad_add_fusion.meta) | copy-start | bytes 52
  28.8 35.6 %copy-start.17 = (bf16[16,128,128]{2,1,0:T(8,128)(2,1)}, bf16[16,128,128]{2,1,0:T(8,128)(2,1)S(1)}, u32[]{:S(2)}) copy-start(bf16[16,128,128]{2,1,0:T(8,128)(2,1)S(1)} %all-to-all-done.1.rest_0_) | copy-start | bytes 1572868
  28.8 45.7 %all-to-all-start = ((bf16[64,72,128]{2,1,0:T(8,128)(2,1)}), bf16[64,72,128]{2,1,0:T(8,128)(2,1)S(1)}, u32[]{:S(2)}, u32[]{:S(2)}) async-start(bf16[64,72,128]{2,1,0:T(8,128)(2,1)} %get-tuple-element.50), calls=%async_computation | async-start | bytes 2359296 | tf_op jit(solution)/shard_map/all_to_all | solution.py:339
  38.1 19.8 %collective-permute-start.1 = (bf16[16,128,128]{2,1,0:T(8,128)(2,1)S(1)}, bf16[16,128,128]{2,1,0:T(8,128)(2,1)S(1)}, u32[]{:S(2)}, u32[]{:S(2)}) collective-permute-start(bf16[16,128,128]{2,1,0:T(8,128)(2,1)S(1)} %all-to-all-done.1.rest_0_), channel_id=1, source_target_pairs={{0,192},{64,0},{128,64},{192,128},{1,193},{65,1},{129,65},{193,129... | collective-permute-start | bytes 1572872 | tf_op jit(solution)/shard_map/ppermute | solution.py:54
  40.6 23.6 %collective-permute-start = (bf16[16,128,128]{2,1,0:T(8,128)(2,1)S(1)}, bf16[16,128,128]{2,1,0:T(8,128)(2,1)S(1)}, u32[]{:S(2)}, u32[]{:S(2)}) collective-permute-start(bf16[16,128,128]{2,1,0:T(8,128)(2,1)S(1)} %all-to-all-done.1.rest_0_), channel_id=1, source_target_pairs={{0,64},{64,128},{128,192},{192,0},{1,65},{65,129},{129,193},{193,1... | collective-permute-start | bytes 1572872 | tf_op jit(solution)/shard_map/ppermute | solution.py:53
  57.9 17.8 %copy-start.21 = (bf16[16,128,128]{2,1,0:T(8,128)(2,1)}, bf16[16,128,128]{2,1,0:T(8,128)(2,1)S(1)}, u32[]{:S(2)}) copy-start(bf16[16,128,128]{2,1,0:T(8,128)(2,1)S(1)} %collective-permute-done.1.rest_2_) | copy-start | bytes 1572868
  58.0 9.5 %collective-permute-start.3 = (bf16[8,128,128]{2,1,0:T(8,128)(2,1)S(1)}, bf16[8,128,128]{2,1,0:T(8,128)(2,1)S(1)}, u32[]{:S(2)}, u32[]{:S(2)}) collective-permute-start(bf16[8,128,128]{2,1,0:T(8,128)(2,1)S(1)} %slice.33), channel_id=1, source_target_pairs={{0,192},{64,0},{128,64},{192,128},{1,193},{65,1},{129,65},{193,129... | collective-permute-start | bytes 786440 | tf_op jit(solution)/shard_map/ppermute | solution.py:61
  64.2 7.0 %collective-permute-start.2 = (bf16[8,128,128]{2,1,0:T(8,128)(2,1)S(1)}, bf16[8,128,128]{2,1,0:T(8,128)(2,1)S(1)}, u32[]{:S(2)}, u32[]{:S(2)}) collective-permute-start(bf16[8,128,128]{2,1,0:T(8,128)(2,1)S(1)} %slice.32), channel_id=1, source_target_pairs={{0,64},{64,128},{128,192},{192,0},{1,65},{65,129},{129,193},{193,1... | collective-permute-start | bytes 786440 | tf_op jit(solution)/shard_map/ppermute | solution.py:60
  64.3 11.0 %collective-permute-start.4 = (bf16[16,128,128]{2,1,0:T(8,128)(2,1)S(1)}, bf16[16,128,128]{2,1,0:T(8,128)(2,1)}, u32[]{:S(2)}, u32[]{:S(2)}) collective-permute-start(bf16[16,128,128]{2,1,0:T(8,128)(2,1)S(1)} %all-to-all-done.1.rest_0_), channel_id=1, source_target_pairs={{0,1},{1,0},{2,3},{3,2},{4,5},{5,4},{6,7},{7,6},{8,9},{9,8},{10,11... | collective-permute-start | bytes 1572872 | tf_op jit(solution)/shard_map/ppermute | solution.py:66
  66.9 8.8 %collective-permute-start.6 = (bf16[16,128,128]{2,1,0:T(8,128)(2,1)S(1)}, bf16[16,128,128]{2,1,0:T(8,128)(2,1)}, u32[]{:S(2)}, u32[]{:S(2)}) collective-permute-start(bf16[16,128,128]{2,1,0:T(8,128)(2,1)S(1)} %collective-permute-done.1.rest_2_), channel_id=1, source_target_pairs={{0,1},{1,0},{2,3},{3,2},{4,5},{5,4},{6,7},{7,6},{8,9},{9,8},{10,11... | collective-permute-start | bytes 1572872 | tf_op jit(solution)/shard_map/ppermute | solution.py:66
  67.0 8.7 %collective-permute-start.5 = (bf16[16,128,128]{2,1,0:T(8,128)(2,1)S(1)}, bf16[16,128,128]{2,1,0:T(8,128)(2,1)}, u32[]{:S(2)}, u32[]{:S(2)}) collective-permute-start(bf16[16,128,128]{2,1,0:T(8,128)(2,1)S(1)} %collective-permute-done.rest_1_), channel_id=1, source_target_pairs={{0,1},{1,0},{2,3},{3,2},{4,5},{5,4},{6,7},{7,6},{8,9},{9,8},{10,11... | collective-permute-start | bytes 1572872 | tf_op jit(solution)/shard_map/ppermute | solution.py:66
  67.4 7.9 %collective-permute-start.8 = (bf16[8,128,128]{2,1,0:T(8,128)(2,1)S(1)}, bf16[8,128,128]{2,1,0:T(8,128)(2,1)}, u32[]{:S(2)}, u32[]{:S(2)}) collective-permute-start(bf16[8,128,128]{2,1,0:T(8,128)(2,1)S(1)} %collective-permute-done.3.rest_4_), channel_id=1, source_target_pairs={{0,1},{1,0},{2,3},{3,2},{4,5},{5,4},{6,7},{7,6},{8,9},{9,8},{10,11... | collective-permute-start | bytes 786440 | tf_op jit(solution)/shard_map/ppermute | solution.py:66
  71.2 4.5 %collective-permute-start.7 = (bf16[8,128,128]{2,1,0:T(8,128)(2,1)S(1)}, bf16[8,128,128]{2,1,0:T(8,128)(2,1)}, u32[]{:S(2)}, u32[]{:S(2)}) collective-permute-start(bf16[8,128,128]{2,1,0:T(8,128)(2,1)S(1)} %collective-permute-done.2.rest_3_), channel_id=1, source_target_pairs={{0,1},{1,0},{2,3},{3,2},{4,5},{5,4},{6,7},{7,6},{8,9},{9,8},{10,11... | collective-permute-start | bytes 786440 | tf_op jit(solution)/shard_map/ppermute | solution.py:66
  85.3 13.2 %collective-permute-start.9 = (f32[136,128]{1,0:T(8,128)S(1)}, f32[136,128]{1,0:T(8,128)S(1)}, u32[]{:S(2)}, u32[]{:S(2)}) collective-permute-start(f32[136,128]{1,0:T(8,128)S(1)} %get-tuple-element.92), channel_id=1, source_target_pairs={{0,2},{2,0},{1,3},{3,1},{4,6},{6,4},{5,7},{7,5},{8,10},{10,8},{9,1... | collective-permute-start | bytes 208904 | tf_op jit(solution)/shard_map/ppermute | solution.py:66
  85.9 15.2 %collective-permute-start.11 = (bf16[512,128]{1,0:T(8,128)(2,1)S(1)}, bf16[512,128]{1,0:T(8,128)(2,1)S(1)}, u32[]{:S(2)}, u32[]{:S(2)}) collective-permute-start(bf16[512,128]{1,0:T(8,128)(2,1)S(1)} %copy-done.30), channel_id=1, source_target_pairs={{0,1},{1,0},{2,3},{3,2},{4,5},{5,4},{6,7},{7,6},{8,9},{9,8},{10,11... | collective-permute-start | bytes 393224 | tf_op jit(solution)/shard_map/ppermute | solution.py:66
  88.2 28.1 %all-to-all-start.2 = ((bf16[32,2,32,128]{3,2,1,0:T(8,128)(2,1)}), bf16[32,2,32,128]{3,2,1,0:T(8,128)(2,1)S(1)}, u32[]{:S(2)}, u32[]{:S(2)}) async-start(bf16[32,2,32,128]{3,2,1,0:T(8,128)(2,1)} %broadcast_in_dim.25), calls=%async_computation.2 | async-start | bytes 1048576 | tf_op jit(solution)/shard_map/all_to_all | solution.py:71
  98.5 2.6 %collective-permute-start.10 = (f32[2,136,128]{2,1,0:T(8,128)S(1)}, f32[2,136,128]{2,1,0:T(8,128)S(1)}, u32[]{:S(2)}, u32[]{:S(2)}) collective-permute-start(f32[2,136,128]{2,1,0:T(8,128)S(1)} %get-tuple-element.90), channel_id=1, source_target_pairs={{0,1},{1,0},{2,3},{3,2},{4,5},{5,4},{6,7},{7,6},{8,9},{9,8},{10,11... | collective-permute-start | bytes 417800 | tf_op jit(solution)/shard_map/ppermute | solution.py:66
  101.1 15.2 %copy-start.16 = (bf16[64,72,128]{2,1,0:T(8,128)(2,1)S(1)}, bf16[64,72,128]{2,1,0:T(8,128)(2,1)}, u32[]{:S(2)}) copy-start(bf16[64,72,128]{2,1,0:T(8,128)(2,1)} %copy-done.15) | copy-start | bytes 3538948
  116.3 33.7 %collective-permute-start.13 = (bf16[64,72,128]{2,1,0:T(8,128)(2,1)S(1)}, bf16[64,72,128]{2,1,0:T(8,128)(2,1)S(1)}, u32[]{:S(2)}, u32[]{:S(2)}) collective-permute-start(bf16[64,72,128]{2,1,0:T(8,128)(2,1)S(1)} %copy-done.16), channel_id=1, source_target_pairs={{0,2},{2,0},{1,3},{3,1},{4,6},{6,4},{5,7},{7,5},{8,10},{10,8},{9,1... | collective-permute-start | bytes 3538952 | tf_op jit(solution)/shard_map/ppermute | solution.py:66
  116.3 11.0 %collective-permute-start.15 = (bf16[16,2,2,32,128]{4,3,2,1,0:T(8,128)(2,1)S(1)}, bf16[16,2,2,32,128]{4,3,2,1,0:T(8,128)(2,1)S(1)}, u32[]{:S(2)}, u32[]{:S(2)}) collective-permute-start(bf16[16,2,2,32,128]{4,3,2,1,0:T(8,128)(2,1)S(1)} %bitcast.31), channel_id=1, source_target_pairs={{0,192},{64,0},{128,64},{192,128},{1,193},{65,1},{129,65},{193,129... | collective-permute-start | bytes 1572872 | tf_op jit(solution)/shard_map/ppermute | solution.py:402
  116.6 12.0 %collective-permute-start.14 = (bf16[16,2,2,32,128]{4,3,2,1,0:T(8,128)(2,1)S(1)}, bf16[16,2,2,32,128]{4,3,2,1,0:T(8,128)(2,1)S(1)}, u32[]{:S(2)}, u32[]{:S(2)}) collective-permute-start(bf16[16,2,2,32,128]{4,3,2,1,0:T(8,128)(2,1)S(1)} %bitcast.32), channel_id=1, source_target_pairs={{0,64},{64,128},{128,192},{192,0},{1,65},{65,129},{129,193},{193,1... | collective-permute-start | bytes 1572872 | tf_op jit(solution)/shard_map/ppermute | solution.py:401
  130.0 6.0 %collective-permute-start.17 = (bf16[8,2,2,32,128]{4,3,2,1,0:T(8,128)(2,1)S(1)}, bf16[8,2,2,32,128]{4,3,2,1,0:T(8,128)(2,1)S(1)}, u32[]{:S(2)}, u32[]{:S(2)}) collective-permute-start(bf16[8,2,2,32,128]{4,3,2,1,0:T(8,128)(2,1)S(1)} %slice.28), channel_id=1, source_target_pairs={{0,192},{64,0},{128,64},{192,128},{1,193},{65,1},{129,65},{193,129... | collective-permute-start | bytes 786440 | tf_op jit(solution)/shard_map/ppermute | solution.py:407
  131.7 15.9 %collective-permute-start.19 = (bf16[2,16,2,32,128]{4,3,2,1,0:T(8,128)(2,1)S(1)}, bf16[2,16,2,32,128]{4,3,2,1,0:T(8,128)(2,1)S(1)}, u32[]{:S(2)}, u32[]{:S(2)}) collective-permute-start(bf16[2,16,2,32,128]{4,3,2,1,0:T(8,128)(2,1)S(1)} %get-tuple-element.72), channel_id=1, source_target_pairs={{0,1},{1,0},{2,3},{3,2},{4,5},{5,4},{6,7},{7,6},{8,9},{9,8},{10,11... | collective-permute-start | bytes 1572872 | tf_op jit(solution)/shard_map/ppermute | solution.py:66
  135.4 12.2 %collective-permute-start.20 = (bf16[2,16,2,32,128]{4,3,2,1,0:T(8,128)(2,1)S(1)}, bf16[2,16,2,32,128]{4,3,2,1,0:T(8,128)(2,1)S(1)}, u32[]{:S(2)}, u32[]{:S(2)}) collective-permute-start(bf16[2,16,2,32,128]{4,3,2,1,0:T(8,128)(2,1)S(1)} %get-tuple-element.74), channel_id=1, source_target_pairs={{0,1},{1,0},{2,3},{3,2},{4,5},{5,4},{6,7},{7,6},{8,9},{9,8},{10,11... | collective-permute-start | bytes 1572872 | tf_op jit(solution)/shard_map/ppermute | solution.py:66
  135.5 12.1 %collective-permute-start.18 = (bf16[2,16,2,32,128]{4,3,2,1,0:T(8,128)(2,1)S(1)}, bf16[2,16,2,32,128]{4,3,2,1,0:T(8,128)(2,1)S(1)}, u32[]{:S(2)}, u32[]{:S(2)}) collective-permute-start(bf16[2,16,2,32,128]{4,3,2,1,0:T(8,128)(2,1)S(1)} %get-tuple-element.75), channel_id=1, source_target_pairs={{0,1},{1,0},{2,3},{3,2},{4,5},{5,4},{6,7},{7,6},{8,9},{9,8},{10,11... | collective-permute-start | bytes 1572872 | tf_op jit(solution)/shard_map/ppermute | solution.py:66
  135.9 6.5 %collective-permute-start.16 = (bf16[8,2,2,32,128]{4,3,2,1,0:T(8,128)(2,1)S(1)}, bf16[8,2,2,32,128]{4,3,2,1,0:T(8,128)(2,1)S(1)}, u32[]{:S(2)}, u32[]{:S(2)}) collective-permute-start(bf16[8,2,2,32,128]{4,3,2,1,0:T(8,128)(2,1)S(1)} %slice.27), channel_id=1, source_target_pairs={{0,64},{64,128},{128,192},{192,0},{1,65},{65,129},{129,193},{193,1... | collective-permute-start | bytes 786440 | tf_op jit(solution)/shard_map/ppermute | solution.py:406
  142.5 8.2 %collective-permute-start.12 = (bf16[64,72,128]{2,1,0:T(8,128)(2,1)S(1)}, bf16[64,72,128]{2,1,0:T(8,128)(2,1)S(1)}, u32[]{:S(2)}, u32[]{:S(2)}) collective-permute-start(bf16[64,72,128]{2,1,0:T(8,128)(2,1)S(1)} %copy-done.16), channel_id=1, source_target_pairs={{0,1},{1,0},{2,3},{3,2},{4,5},{5,4},{6,7},{7,6},{8,9},{9,8},{10,11... | collective-permute-start | bytes 3538952 | tf_op jit(solution)/shard_map/ppermute | solution.py:66
  150.0 3.6 %collective-permute-start.21 = (bf16[64,72,128]{2,1,0:T(8,128)(2,1)S(1)}, bf16[64,72,128]{2,1,0:T(8,128)(2,1)S(1)}, u32[]{:S(2)}, u32[]{:S(2)}) collective-permute-start(bf16[64,72,128]{2,1,0:T(8,128)(2,1)S(1)} %collective-permute-done.13.h2), channel_id=1, source_target_pairs={{0,1},{1,0},{2,3},{3,2},{4,5},{5,4},{6,7},{7,6},{8,9},{9,8},{10,11... | collective-permute-start | bytes 3538952 | tf_op jit(solution)/shard_map/ppermute | solution.py:66
  150.0 3.2 %collective-permute-start.22 = (bf16[2,8,2,32,128]{4,3,2,1,0:T(8,128)(2,1)S(1)}, bf16[2,8,2,32,128]{4,3,2,1,0:T(8,128)(2,1)S(1)}, u32[]{:S(2)}, u32[]{:S(2)}) collective-permute-start(bf16[2,8,2,32,128]{4,3,2,1,0:T(8,128)(2,1)S(1)} %get-tuple-element.78), channel_id=1, source_target_pairs={{0,1},{1,0},{2,3},{3,2},{4,5},{5,4},{6,7},{7,6},{8,9},{9,8},{10,11... | collective-permute-start | bytes 786440 | tf_op jit(solution)/shard_map/ppermute | solution.py:66
  150.5 3.1 %collective-permute-start.23 = (bf16[2,8,2,32,128]{4,3,2,1,0:T(8,128)(2,1)S(1)}, bf16[2,8,2,32,128]{4,3,2,1,0:T(8,128)(2,1)S(1)}, u32[]{:S(2)}, u32[]{:S(2)}) collective-permute-start(bf16[2,8,2,32,128]{4,3,2,1,0:T(8,128)(2,1)S(1)} %get-tuple-element.81), channel_id=1, source_target_pairs={{0,1},{1,0},{2,3},{3,2},{4,5},{5,4},{6,7},{7,6},{8,9},{9,8},{10,11... | collective-permute-start | bytes 786440 | tf_op jit(solution)/shard_map/ppermute | solution.py:66
  (28 other events, 141.6 us)

commit v2 on v1

v2 whole, which is shorter than its diff:
```python
import functools

import jax
import jax.numpy as jnp
from jax import lax
from jax.experimental import pallas as pl
from jax.experimental.pallas import tpu as pltpu
from jax.sharding import Mesh
from jax.sharding import PartitionSpec as P

BLK = ("x", "yh")
GROUP = ("x", "yh", "z")
FEAT = ("yl", "c")
PLANE = ("yh", "z")
T = 128
NB = 8
NR = 8
NG = NB * NR
NT = 2 * NG
LT = 36
HT = 8
NL = NB * LT
NH = NB * HT
SLOTS = 2 * NG
QR = T // 4
STEP = 16
NOTES = 8
NX = 4
NPLANE = 2 * NR
HSTEP = 32
NEAR_STEPS = NB - 2
FAR_AT = -(-NEAR_STEPS * LT // STEP) * STEP
LIST = FAR_AT + -(-2 * LT // STEP) * STEP
HELD = ((0, NPLANE), (NPLANE, NPLANE), (3 * NPLANE, NPLANE), (2 * NPLANE, NR), (2 * NPLANE + NR, NR))
BF16 = jnp.bfloat16
SMEM = pl.BlockSpec(memory_space=pltpu.SMEM)
VMEM = pl.BlockSpec(memory_space=pltpu.VMEM)
ANY = pl.BlockSpec(memory_space=pl.ANY)


def params(mib):
    return pltpu.CompilerParams(vmem_limit_bytes=mib * 1024 * 1024)


def turned(blk, source):
    return (((blk >> 1) - (source >> 1)) & 3) * 2 + (source & 1)

PROJECTED = ((0, 0, 0, NPLANE), (1, 0, NPLANE, NPLANE), (1, NPLANE, 3 * NPLANE, NPLANE), (2, 0, 2 * NPLANE, NPLANE))


def step_of(blk, j):
    order = j if j < 4 else (j + 2 if j < NEAR_STEPS else j - 2)
    held, y = order >> 1, order & 1
    source = (((blk >> 1) - held) & 3) * 2 + y
    return (blk - source) & (NB - 1), order * NR


def around(axis, distance):
    n = lax.axis_size(axis)
    return [(i, (i + distance) % n) for i in range(n)]


def along_x(near):
    behind = lax.ppermute(near, "x", around("x", 1))
    ahead = lax.ppermute(near, "x", around("x", -1))
    far = near.shape[0] // 2
    return [
        near,
        behind,
        ahead,
        lax.ppermute(behind[:far], "x", around("x", 1)),
        lax.ppermute(ahead[far:], "x", around("x", -1)),
    ]


def swap(x, axis):
    return lax.ppermute(x, axis, around(axis, 1))


def everyone(x, axis, n):
    spread = jnp.broadcast_to(x[None], (n, *x.shape))
    return lax.all_to_all(spread, axis, 0, 0, tiled=True)


def pack_kernel(
    meta, slots, cols, rows, lcols, heavy, out, ids, places, need, trips, quarter, seats, taken, sem
):
    blk, feat = meta[0], meta[1]
    span = pl.ds(pl.multiple_of(feat * QR, QR), QR)
    copy = pltpu.make_async_copy(heavy.at[:, span, :], quarter.at[pl.ds(0, NH)], sem)
    copy.start()
    quarter[NH] = jnp.zeros((QR, T), BF16)

    def clear(q, carry):
        taken[q] = 0
        seats[2 * q] = NH
        seats[2 * q + 1] = NH
        return carry

    lax.fori_loop(0, NG, clear, 0, unroll=8)

    def seat(i, carry):
        q = slots[0, i // HT, i % HT]
        turn = taken[q]
        taken[q] = turn + 1
        seats[2 * q + turn] = i
        return carry

    lax.fori_loop(0, NH, seat, 0, unroll=8)
    lane = lax.broadcasted_iota(jnp.int32, (NOTES, T), 1)
    copy.wait()

    def node(i):
        j = jnp.minimum(i, NH - 1)
        tile = ((blk - (j >> 3)) & (NB - 1)) * 2 * NR + cols[0, j >> 3, j & (HT - 1)]
        return jnp.where(i < NH, tile, NT)

    def fill(q, carry):
        a, b = seats[2 * q], seats[2 * q + 1]
        notes = jnp.where(lane == 0, node(a), node(b)).astype(jnp.float32).astype(BF16)
        out[q] = jnp.concatenate([quarter[a], quarter[b], notes], axis=0)
        return carry

    lax.fori_loop(0, NG, fill, 0, unroll=4)

    for g in range(FAR_AT // STEP):
        need[g] = 0

    def put(k, carry, s, start, j, base):
        n0, n1 = carry
        row, col = rows[0, s, k], lcols[0, s, k]
        at = base + jnp.where(row == 0, n0, n1)
        ids[row, at] = j * LT + k
        places[row, at] = start + (col & 1) * NG + (col >> 1)
        if base == 0:
            need[at >> 4] = j
        return n0 + 1 - row, n1 + row

    def pad(i, carry, t):
        ids[t, i] = 0
        places[t, i] = NT
        return carry

    for which, (base, blocks) in enumerate(((0, range(NEAR_STEPS)), (FAR_AT, range(NEAR_STEPS, NB)))):
        counts = (0, 0)
        for j in blocks:
            s, start = step_of(blk, j)
            counts = lax.fori_loop(
                0, LT, lambda k, c, s=s, v=start, j=j, b=base: put(k, c, s, v, j, b), counts, unroll=6
            )
        count = (jnp.maximum(counts[0], counts[1]) + STEP - 1) // STEP
        trips[which] = count
        for t in range(2):
            lax.fori_loop(base + counts[t], base + count * STEP, lambda i, c, t=t: pad(i, c, t), 0)


def compact_kernel(hplaces, ids, places, htrips):
    def clear(i, carry):
        ids[i] = 0
        places[i] = NT
        return carry

    lax.fori_loop(0, NL, clear, 0, unroll=8)

    def put(i, n):
        place = hplaces[i]
        ids[n] = i
        places[n] = place
        return n + jnp.where(place < NT, 1, 0)

    n = lax.fori_loop(0, SLOTS, put, 0, unroll=8)
    ids[n] = 0
    places[n] = NT
    htrips[0] = (n + STEP - 1) // STEP


def dots(tile, value, count, ids, places, acc):
    for u in range(0, count, 2):
        left = jnp.concatenate([tile(ids(u)), tile(ids(u + 1))], axis=1)
        right = jnp.concatenate([value(places(u)), value(places(u + 1))], axis=0)
        acc = acc + jnp.dot(left, right, preferred_element_type=jnp.float32)
    return acc


def light_copy(meta, light, tiles, j, first, rows, sem):
    step, _ = step_of(meta[0], j)
    source = light.at[pl.ds(step * LT, LT)]
    if rows is not None:
        source = light.at[pl.ds(step * LT, LT), rows, :]
    return pltpu.make_async_copy(source, tiles.at[pl.ds((j - first) * LT, LT)], sem)


def light_dots(tiles, value, ids, places, first, base, carry):
    return [
        dots(
            lambda i: tiles[jnp.maximum(i - first * LT, 0)], value, STEP,
            lambda u: ids[t, base + u], lambda u: places[t, base + u], carry[t],
        )
        for t in range(2)
    ]


def feature_copies(meta, held, parts, values, sems):
    core = meta[2]
    copies = []
    for which in range(2):
        c = core if which == 0 else 1 - core
        for (start, size), part in zip(held, parts[which * len(held) : (which + 1) * len(held)]):
            span = pl.ds(c * NG + start, size)
            copies.append(pltpu.make_async_copy(part, values.at[span], sems.at[len(copies)]))
    return copies


def first_near_kernel(meta, trips, ids, places, light, *rest):
    held = HELD[:3]
    parts, (out, values, tiles, sems) = rest[: 2 * len(held)], rest[2 * len(held) :]
    rows = pl.ds(pl.multiple_of(meta[1] * QR, QR), QR)
    copies = feature_copies(meta, held, parts, values, sems)
    for j in range(NEAR_STEPS):
        copies.append(light_copy(meta, light, tiles, j, 0, rows, sems.at[len(copies)]))
    for copy in copies:
        copy.start()
    values[NT] = jnp.zeros((T, T), BF16)
    for copy in copies:
        copy.wait()
    zero = jnp.zeros((QR, T), jnp.float32)
    body = lambda g, c: light_dots(tiles, lambda p: values[p], ids, places, 0, g * STEP, c)
    out[0], out[1] = lax.fori_loop(0, trips[0], body, [zero, zero])


def first_kernel(meta, trips, ids, places, hplaces, light, heavy, near, *rest):
    parts, (out, values, tiles, htiles, sems) = rest[: 2 * len(HELD)], rest[2 * len(HELD) :]
    owner = meta[3]
    rows = pl.ds(pl.multiple_of(meta[1] * QR, QR), QR)
    copies = feature_copies(meta, HELD, parts, values, sems)
    for j in range(NEAR_STEPS, NB):
        copies.append(light_copy(meta, light, tiles, j, NEAR_STEPS, rows, sems.at[len(copies)]))
    for slot in range(2):
        rows, span = pl.ds(slot * QR, QR), pl.ds(slot * NG, NG)
        copies.append(
            pltpu.make_async_copy(heavy.at[:, rows, :], htiles.at[span], sems.at[len(copies)])
        )
    for copy in copies:
        copy.start()
    values[NT] = jnp.zeros((T, T), BF16)
    for copy in copies:
        copy.wait()
    value = lambda p: values[p]
    body = lambda g, c: light_dots(tiles, value, ids, places, NEAR_STEPS, FAR_AT + g * STEP, c)
    sums = lax.fori_loop(0, trips[1], body, [near[0], near[1]])

    def heavy_body(g, acc):
        base = g * HSTEP
        return dots(
            lambda i: htiles[i], value, HSTEP,
            lambda u: base + u, lambda u: hplaces[base + u], acc,
        )

    hsum = lax.fori_loop(0, SLOTS // HSTEP, heavy_body, jnp.zeros((QR, T), jnp.float32))
    for t in range(2):
        total = (sums[t] + jnp.where(owner == t, hsum, 0.0)).astype(BF16)
        for n in range(2 * NPLANE):
            out[n, t] = total


def project_kernel(n, *refs):
    parts, (w_in, b_in, w_mid, mine, theirs) = refs[:n], refs[n:]
    at = 0
    for part in parts:
        size = part.shape[0]
        for rt in range(2):
            x = part[:, :, rt].reshape(-1, T)
            h = jnp.dot(x, w_in[...], preferred_element_type=jnp.float32) + b_in[...]
            h = jnp.maximum(h, 0.0).astype(BF16)
            s = jnp.dot(h, w_mid[...], preferred_element_type=jnp.float32).astype(BF16)
            mine[rt, at : at + size] = s[:, :T].reshape(size, *mine.shape[2:])
            theirs[rt, at : at + size] = s[:, T:].reshape(size, *mine.shape[2:])
        at += size


def value_copies(meta, held, parts, values, sems):
    copies = []
    for which in range(2):
        c = meta[2] if which == 0 else 1 - meta[2]
        for k, at, start, size in held:
            part = parts[which * (held[-1][0] + 1) + k]
            for rt in range(2):
                span = pl.ds(rt * NG + start, size)
                copies.append(
                    pltpu.make_async_copy(
                        part.at[rt, pl.ds(at, size)], values.at[span, :, c], sems.at[len(copies)]
                    )
                )
    return copies


def second_near_kernel(meta, trips, need, ids, places, light, *rest):
    parts, (out, values, tiles, sems, light_sems) = rest[:4], rest[4:]
    copies = value_copies(meta, PROJECTED[:3], parts, values, sems)
    chunks = [light_copy(meta, light, tiles, j, 0, None, light_sems.at[j]) for j in range(NEAR_STEPS)]
    for copy in copies + chunks:
        copy.start()
    values[NT] = jnp.zeros((2, 2, QR, T), BF16)
    for copy in copies:
        copy.wait()

    def wait_for(n):
        span = pl.ds(n * LT, LT)
        pltpu.make_async_copy(light.at[span], tiles.at[span], light_sems.at[n]).wait()
        return n + 1

    value = lambda p: values[p].reshape(T, T)

    def body(g, carry):
        here = lax.while_loop(lambda n: n <= need[g], wait_for, carry[2])
        return (*light_dots(tiles, value, ids, places, 0, g * STEP, carry[:2]), here)

    zero = jnp.zeros((T, T), jnp.float32)
    sum0, sum1, here = lax.fori_loop(0, trips[0], body, (zero, zero, 0))
    lax.while_loop(lambda n: n < NEAR_STEPS, wait_for, here)
    out[0] = sum0
    out[1] = sum1


def second_kernel(
    meta, trips, htrips, ids, places, hids, hplaces, light, h0, h1, h2, h3, near, b_mid, *rest
):
    parts, (out, values, tiles, htiles, sems) = rest[:6], rest[6:]
    feat, owner = meta[1], meta[3]
    copies = value_copies(meta, PROJECTED, parts, values, sems)
    for j in range(NEAR_STEPS, NB):
        copies.append(light_copy(meta, light, tiles, j, NEAR_STEPS, None, sems.at[len(copies)]))
    first = len(copies)
    for k, h in enumerate((h0, h1, h2, h3)):
        rows = pl.ds(pl.multiple_of((feat ^ k) * QR, QR), QR)
        for slot in range(2):
            copies.append(
                pltpu.make_async_copy(
                    h.at[:, pl.ds(slot * QR, QR), :],
                    htiles.at[pl.ds(slot * NG, NG), rows, :],
                    sems.at[len(copies)],
                )
            )
    for copy in copies:
        copy.start()
    values[NT] = jnp.zeros((2, 2, QR, T), BF16)
    for copy in copies[:first]:
        copy.wait()
    value = lambda p: values[p].reshape(T, T)
    body = lambda g, c: light_dots(tiles, value, ids, places, NEAR_STEPS, FAR_AT + g * STEP, c)
    sums = lax.fori_loop(0, trips[1], body, [near[0], near[1]])
    for copy in copies[first:]:
        copy.wait()

    def heavy_body(g, acc):
        base = g * STEP
        return dots(
            lambda i: htiles[i], value, STEP, lambda u: hids[base + u], lambda u: hplaces[base + u], acc
        )

    hsum = lax.fori_loop(0, htrips[0], heavy_body, jnp.zeros((T, T), jnp.float32))
    for t in range(2):
        total = sums[t] + jnp.where(owner == t, hsum, 0.0) + b_mid[...]
        out[t * T : (t + 1) * T] = total.astype(BF16)


def per_device(
    features, weight_in, bias_in, weight_mid, bias_mid, light_tiles, light_rows, light_cols,
    heavy_tiles, heavy_slots, heavy_cols, owner_map,
):
    i32 = jnp.int32
    blk, core, feat = lax.axis_index(BLK), lax.axis_index("c"), lax.axis_index(FEAT)
    meta = jnp.stack([blk, feat, core, owner_map[0]]).astype(i32)
    light = light_tiles.reshape(NL, T, T)
    int_list = jax.ShapeDtypeStruct((NL,), i32)
    int_lists = jax.ShapeDtypeStruct((2, LIST), i32)
    needs = jax.ShapeDtypeStruct((FAR_AT // STEP,), i32)
    one_int = jax.ShapeDtypeStruct((1,), i32)
    two_ints = jax.ShapeDtypeStruct((2,), i32)

    half = lax.dynamic_slice_in_dim(features, core * T, T, axis=0)
    plane = everyone(half, PLANE, NPLANE)

    packed, ids, places, need, trips = pl.pallas_call(
        pack_kernel,
        out_shape=(
            jax.ShapeDtypeStruct((NG, 2 * QR + NOTES, T), BF16), int_lists, int_lists, needs, two_ints
        ),
        in_specs=[SMEM] * 5 + [ANY],
        out_specs=(VMEM, SMEM, SMEM, SMEM, SMEM),
        scratch_shapes=[
            pltpu.VMEM((NH + 1, QR, T), BF16),
            pltpu.SMEM((SLOTS,), i32),
            pltpu.SMEM((NG,), i32),
            pltpu.SemaphoreType.DMA(()),
        ],
        compiler_params=params(16),
        cost_estimate=pl.CostEstimate(flops=0, transcendentals=0, bytes_accessed=30_000_000),
        name="pack",
    )(meta, heavy_slots, heavy_cols, light_rows, light_cols, heavy_tiles.reshape(NH, T, T))
    arrived = lax.all_to_all(packed, GROUP, 0, 0, tiled=True)
    own = along_x(plane)
    own, far_parts = own[:3], own[3:]
    other = [swap(part, "c") for part in own]

    nodes = arrived[:, 2 * QR, :2].T.reshape(SLOTS).astype(i32)
    hplaces = jnp.where(
        nodes < NT, (nodes & 1) * NG + turned(blk, nodes >> 4) * NR + ((nodes & 15) >> 1), NT
    )

    first_near = pl.pallas_call(
        first_near_kernel,
        out_shape=jax.ShapeDtypeStruct((2, QR, T), jnp.float32),
        in_specs=[SMEM] * 4 + [ANY] * 7,
        out_specs=VMEM,
        scratch_shapes=[
            pltpu.VMEM((NT + 1, T, T), BF16),
            pltpu.VMEM((NEAR_STEPS * LT, QR, T), BF16),
            pltpu.SemaphoreType.DMA((6 + NEAR_STEPS,)),
        ],
        compiler_params=params(54),
        name="first_near",
    )(meta, trips, ids, places, light, *own, *other)
    first_near, far_parts = lax.optimization_barrier((first_near, far_parts))
    held = own + far_parts + other + [swap(part, "c") for part in far_parts]
    aggregated = pl.pallas_call(
        first_kernel,
        out_shape=jax.ShapeDtypeStruct((2 * NPLANE, 2, QR, T), BF16),
        in_specs=[SMEM] * 5 + [ANY] * 2 + [VMEM] + [ANY] * len(held),
        out_specs=VMEM,
        scratch_shapes=[
            pltpu.VMEM((NT + 1, T, T), BF16),
            pltpu.VMEM(((NB - NEAR_STEPS) * LT, QR, T), BF16),
            pltpu.VMEM((SLOTS, QR, T), BF16),
            pltpu.SemaphoreType.DMA((len(held) + 4,)),
        ],
        compiler_params=params(54),
        name="first",
    )(meta, trips, ids, places, hplaces, light, arrived, first_near, *held)

    aggregated, weight_in, bias_in, weight_mid = lax.optimization_barrier(
        (aggregated, weight_in, bias_in, weight_mid)
    )
    bias_rows = jnp.pad(bias_in.reshape(1, T), ((0, 7), (0, 0)))
    pieces = jnp.concatenate([weight_in.astype(jnp.float32), bias_rows], axis=0)
    pieces = jnp.stack([pieces, swap(pieces, "yl")])
    pieces = jnp.stack([pieces, swap(pieces, "c")], axis=1).reshape(4, T + 8, T)
    pieces = jnp.take(pieces, feat ^ jnp.arange(4), axis=0)
    w_in = jnp.moveaxis(pieces[:, :T], 0, 1).reshape(T, 4 * T).astype(BF16)
    b_in = pieces[:, T].reshape(1, 4 * T)
    w_mid = jnp.concatenate([weight_mid, swap(weight_mid, "c")], axis=1)

    rows = lax.all_to_all(aggregated, (*PLANE, "yl"), 0, 0, tiled=True).reshape(NPLANE, 2, 2, QR, T)

    hids, hlist, htrips = pl.pallas_call(
        compact_kernel,
        out_shape=(int_list, int_list, one_int),
        in_specs=[SMEM],
        out_specs=(SMEM,) * 3,
        name="compact",
    )(hplaces)

    rows, arrived, w_in, b_in, w_mid, hids, hlist, htrips = lax.optimization_barrier(
        (rows, arrived, w_in, b_in, w_mid, hids, hlist, htrips)
    )
    hc = swap(arrived, "c")
    hy = swap(arrived, "yl")
    def project(*parts):
        groups = sum(part.shape[0] for part in parts)
        half_values = jax.ShapeDtypeStruct((2, groups, 2, QR, T), BF16)
        return pl.pallas_call(
            functools.partial(project_kernel, len(parts)),
            out_shape=(half_values, half_values),
            in_specs=[VMEM] * (len(parts) + 3),
            out_specs=(VMEM, VMEM),
            compiler_params=params(24),
            name="project",
        )(*parts, w_in, b_in, w_mid)

    behind = lax.ppermute(rows, "x", around("x", 1))
    ahead = lax.ppermute(rows, "x", around("x", -1))
    near = project(rows)
    behind, ahead, near = lax.optimization_barrier((behind, ahead, near))
    far = [
        lax.ppermute(behind[:NR], "x", around("x", 1)),
        lax.ppermute(ahead[NR:], "x", around("x", -1)),
    ]
    sides = project(behind, ahead)
    mine = [near[0], sides[0]]
    swapped = [swap(near[1], "c"), swap(sides[1], "c")]
    second_near = pl.pallas_call(
        second_near_kernel,
        out_shape=jax.ShapeDtypeStruct((2, T, T), jnp.float32),
        in_specs=[SMEM] * 5 + [ANY] * 5,
        out_specs=VMEM,
        scratch_shapes=[
            pltpu.VMEM((NT + 1, 2, 2, QR, T), BF16),
            pltpu.VMEM((NEAR_STEPS * LT, T, T), BF16),
            pltpu.SemaphoreType.DMA((12,)),
            pltpu.SemaphoreType.DMA((NEAR_STEPS,)),
        ],
        compiler_params=params(54),
        name="second_near",
    )(meta, trips, need, ids, places, light, *mine, *swapped)
    far, second_near = lax.optimization_barrier((far, second_near))
    far = project(*far)
    mine.append(far[0])
    swapped.append(swap(far[1], "c"))
    hy_late, _ = lax.optimization_barrier((hy, far))
    hyc = swap(hy_late, "c")
    return pl.pallas_call(
        second_kernel,
        out_shape=jax.ShapeDtypeStruct((2 * T, T), BF16),
        in_specs=[SMEM] * 7 + [ANY] * 5 + [VMEM] * 2 + [ANY] * 6,
        out_specs=VMEM,
        scratch_shapes=[
            pltpu.VMEM((NT + 1, 2, 2, QR, T), BF16),
            pltpu.VMEM(((NB - NEAR_STEPS) * LT, T, T), BF16),
            pltpu.VMEM((SLOTS, T, T), BF16),
            pltpu.SemaphoreType.DMA((26,)),
        ],
        compiler_params=params(54),
        name="second",
    )(
        meta, trips, htrips, ids, places, hids, hlist, light, arrived, hc, hy, hyc, second_near,
        bias_mid.reshape(1, T), *mine, *swapped,
    )


def solution(mesh):
    wide = Mesh(mesh.devices.reshape(4, 2, 8, 2, 2), ("x", "yh", "z", "yl", "c"))
    in_specs = (
        P(GROUP, None),
        P(None, FEAT),
        P(FEAT),
        P(None, FEAT),
        P(FEAT),
        P(GROUP, None, None, None, None),
        P(GROUP, None, None),
        P(GROUP, None, None),
        P(GROUP, None, None, None, None),
        P(GROUP, None, None),
        P(GROUP, None, None),
        P(GROUP),
    )
    return jax.shard_map(
        per_device, mesh=wide, in_specs=in_specs, out_specs=P(GROUP, FEAT), check_vma=False
    )
```

time: 169 us -> 161 us (0.953)
  starting transfers between devices: 62 us -> 53.8 us
  waiting for transfers between devices: 55.1 us -> 48.9 us
  Pallas kernels: 37.6 us -> 42.3 us
  local copies, waits for them, and re-layouts: 10.8 us -> 14 us
    all_to_all x2 -> x1, waiting for transfers between devices: 17.7 us -> 3.65 us  [everyone(): return lax.all_to_all(spread, axis, 0, 0, tiled=True)]
    all_to_all x0 -> x1, waiting for transfers between devices: none -> 13 us  [per_device(): lax.all_to_all(aggregated, (*PLANE, 'yl'), 0, 0, tiled=True)]
    pallas_call x6, Pallas kernels: 15.2 us -> 25.5 us  [the longest x1 7.94 us: per_device(): pl.pallas_call(second_near_kernel, out_shape=jax.ShapeDtypeStruct((2, T,...]
    all_to_all x2 -> x1, starting transfers between devices: 22 us -> 11.7 us  [everyone(): return lax.all_to_all(spread, axis, 0, 0, tiled=True)]
    all_to_all x0 -> x1, starting transfers between devices: none -> 9.67 us  [per_device(): lax.all_to_all(aggregated, (*PLANE, 'yl'), 0, 0, tiled=True)]
    ppermute x1, waiting for transfers between devices: 4.97 us -> 0.01 us  [per_device(): lax.ppermute(behind[:NR], 'x', around('x', 1))]
    unnamed x66 -> x70, local copies, waits for them, and re-layouts: 6.83 us -> 11.7 us
    pallas_call x1, Pallas kernels: 12.3 us -> 7.74 us  [per_device(): pl.pallas_call(second_kernel, out_shape=jax.ShapeDtypeStruct((2 * T, T),...]
  transfers between devices with their start and end apart: 27 -> 25, of which waited for: 11 -> 11; matrix products, arithmetic and copies ran while one was open for 2% -> 1% of each run, Pallas kernels for 9% -> 17%
where the time goes in v2:
time: 161 us
  starting transfers between devices  53.8 us (33%)
  waiting for transfers between devices  48.9 us (30%)
  Pallas kernels  42.3 us (26%)
  local copies, waits for them, and re-layouts  14 us (9%)
    ppermute x14, starting transfers between devices, swap(): return lax.ppermute(x, axis, around(axis, 1))  15.9 us
    ppermute x1, waiting for transfers between devices, along_x(): ahead = lax.ppermute(near, 'x', around('x', -1))  15.3 us
    all_to_all x1, waiting for transfers between devices, per_device(): lax.all_to_all(aggregated, (*PLANE, 'yl'), 0, 0, tiled=True)  13 us
    all_to_all x1, starting transfers between devices, everyone(): return lax.all_to_all(spread, axis, 0, 0, tiled=True)  11.7 us
    unnamed x70, local copies, waits for them, and re-layouts  11.7 us
    all_to_all x1, starting transfers between devices, per_device(): lax.all_to_all(aggregated, (*PLANE, 'yl'), 0, 0, tiled=True)  9.67 us
    all_to_all x1, starting transfers between devices, per_device(): arrived = lax.all_to_all(packed, GROUP, 0, 0, tiled=True)  9.33 us
    pallas_call x1, Pallas kernels, per_device(): pl.pallas_call(second_near_kernel, out_shape=jax.ShapeDtypeStruct((2, T,...  7.94 us
  transfers between devices with their start and end apart: 25, of which 11 were waited for; matrix products, arithmetic and copies ran while one was open for 1% of the time, Pallas kernels for 17%

profile of v2, /device:TPU:1, one launch (start us, length us, event | category | flops | bytes accessed | tf_op | source)
XLA Modules:
  0.0 160.8 jit_solution(6310243240438147820)
XLA Ops:
  0.8 0.9 broadcast_in_dim.18
  1.7 11.7 %all-to-all-start.1 = ((bf16[16,128,128]{2,1,0:T(8,128)(2,1)}), bf16[16,128,128]{2,1,0:T(8,128)(2,1)S(1)}, u32[]{:S(2)}, u32[]{:S(2)}) async-start(bf16[16,128,128]{2,1,0:T(8,128)(2,1)} %broadcast_in_dim.18), calls=%async_computation.1 | async-start | bytes 1048576 | tf_op jit(solution)/shard_map/all_to_all | solution.py:82
  14.3 1.6 copy-done.2
  15.9 7.0 %pack.1 = (bf16[64,72,128]{2,1,0:T(8,128)(2,1)}, s32[2,304]{1,0:T(2,128)S(1)}, s32[2,304]{1,0:T(2,128)S(1)}, s32[14]{0:T(128)S(1)}, s32[2]{0:T(128)S(1)}) custom-call(s32[4]{0:T(128)S(1)} %pad_add_fusion.meta, s32[1,8,8]{2,1,0:T(8,128)S(1)} %copy-done.9, s32[1,8,8]{2,1,0:T(8,128)S(1)} %copy-done.10, s32[1,8,36]{2,1,0:T(8,128)S(1)} %copy-done.11, ...), custom_call_target="tpu_custom_call" | custom-call | bytes 30000000 | tf_op jit(solution)/shard_map/pack/pallas_call | solution.py:384
  25.1 3.7 %all-to-all-done.1.rest_0_ = bf16[16,128,128]{2,1,0:T(8,128)(2,1)S(1)} async-done(((bf16[16,128,128]{2,1,0:T(8,128)(2,1)}), bf16[16,128,128]{2,1,0:T(8,128)(2,1)S(1)}, u32[]{:S(2)}, u32[]{:S(2)}) %all-to-all-start.1) | async-done | bytes 524320 | tf_op jit(solution)/shard_map/all_to_all | solution.py:82
  28.8 9.3 %all-to-all-start = ((bf16[64,72,128]{2,1,0:T(8,128)(2,1)}), bf16[64,72,128]{2,1,0:T(8,128)(2,1)S(1)}, u32[]{:S(2)}, u32[]{:S(2)}) async-start(bf16[64,72,128]{2,1,0:T(8,128)(2,1)} %get-tuple-element.45), calls=%async_computation | async-start | bytes 2359296 | tf_op jit(solution)/shard_map/all_to_all | solution.py:401
  38.1 2.5 %collective-permute-start.1 = (bf16[16,128,128]{2,1,0:T(8,128)(2,1)S(1)}, bf16[16,128,128]{2,1,0:T(8,128)(2,1)S(1)}, u32[]{:S(2)}, u32[]{:S(2)}) collective-permute-start(bf16[16,128,128]{2,1,0:T(8,128)(2,1)S(1)} %all-to-all-done.1.rest_0_), channel_id=1, source_target_pairs={{0,192},{64,0},{128,64},{192,128},{1,193},{65,1},{129,65},{193,129... | collective-permute-start | bytes 1572872 | tf_op jit(solution)/shard_map/ppermute | solution.py:65
  40.6 2.1 %collective-permute-start.2 = (bf16[16,128,128]{2,1,0:T(8,128)(2,1)S(1)}, bf16[16,128,128]{2,1,0:T(8,128)(2,1)S(1)}, u32[]{:S(2)}, u32[]{:S(2)}) collective-permute-start(bf16[16,128,128]{2,1,0:T(8,128)(2,1)S(1)} %all-to-all-done.1.rest_0_), channel_id=1, source_target_pairs={{0,1},{1,0},{2,3},{3,2},{4,5},{5,4},{6,7},{7,6},{8,9},{9,8},{10,11... | collective-permute-start | bytes 1572872 | tf_op jit(solution)/shard_map/ppermute | solution.py:77
  42.7 15.3 %collective-permute-done.1.rest_2_ = bf16[16,128,128]{2,1,0:T(8,128)(2,1)S(1)} collective-permute-done((bf16[16,128,128]{2,1,0:T(8,128)(2,1)S(1)}, bf16[16,128,128]{2,1,0:T(8,128)(2,1)S(1)}, u32[]{:S(2)}, u32[]{:S(2)}) %collective-permute-start.1) | collective-permute-done | bytes 524320 | tf_op jit(solution)/shard_map/ppermute | solution.py:65
  57.9 4.0 %collective-permute-start.4 = (bf16[16,128,128]{2,1,0:T(8,128)(2,1)S(1)}, bf16[16,128,128]{2,1,0:T(8,128)(2,1)S(1)}, u32[]{:S(2)}, u32[]{:S(2)}) collective-permute-start(bf16[16,128,128]{2,1,0:T(8,128)(2,1)S(1)} %collective-permute-done.1.rest_2_), channel_id=1, source_target_pairs={{0,1},{1,0},{2,3},{3,2},{4,5},{5,4},{6,7},{7,6},{8,9},{9,8},{10,11... | collective-permute-start | bytes 1572872 | tf_op jit(solution)/shard_map/ppermute | solution.py:77
  61.9 2.3 %collective-permute-done.rest_1_ = bf16[16,128,128]{2,1,0:T(8,128)(2,1)S(1)} collective-permute-done((bf16[16,128,128]{2,1,0:T(8,128)(2,1)S(1)}, bf16[16,128,128]{2,1,0:T(8,128)(2,1)S(1)}, u32[]{:S(2)}, u32[]{:S(2)}) %collective-permute-start) | collective-permute-done | bytes 524320 | tf_op jit(solution)/shard_map/ppermute | solution.py:64
  64.2 2.5 %collective-permute-start.3 = (bf16[16,128,128]{2,1,0:T(8,128)(2,1)S(1)}, bf16[16,128,128]{2,1,0:T(8,128)(2,1)S(1)}, u32[]{:S(2)}, u32[]{:S(2)}) collective-permute-start(bf16[16,128,128]{2,1,0:T(8,128)(2,1)S(1)} %collective-permute-done.rest_1_), channel_id=1, source_target_pairs={{0,1},{1,0},{2,3},{3,2},{4,5},{5,4},{6,7},{7,6},{8,9},{9,8},{10,11... | collective-permute-start | bytes 1572872 | tf_op jit(solution)/shard_map/ppermute | solution.py:77
  66.9 1.5 collective-permute-start.5
  69.6 5.9 %first_near.1.near = f32[2,32,128]{2,1,0:T(8,128)} custom-call(s32[4]{0:T(128)} %copy-done.7, s32[2]{0:T(128)} %copy-done.8, s32[2,304]{1,0:T(2,128)} %copy-done.5, s32[2,304]{1,0:T(2,128)} %copy-done.6, bf16[288,128,128]{2,1,0:T(8,128)(2,1)} %bitcast.34, bf16[16,128,128]{2,1,0:T(8,128)(2,1)} %copy-done.16, bf16[16,128,128]{2,1,0:T(8,128)(2,1)} %copy-done.19, ...), custom_call_target="tpu_custom_call" | custom-call | tf_op jit(solution)/shard_map/first_near/pallas_call | solution.py:411
  79.4 6.5 %first.1 = bf16[32,2,32,128]{3,2,1,0:T(8,128)(2,1)} custom-call(s32[4]{0:T(128)} %copy-done.7, s32[2]{0:T(128)} %copy-done.8, s32[2,304]{1,0:T(2,128)} %copy-done.5, s32[2,304]{1,0:T(2,128)} %copy-done.6, s32[128]{0:T(128)} %reshape.116.hplaces, bf16[288,128,128]{2,1,0:T(8,128)(2,1)} %bitcast.35, bf16[64,72,128]{2,1,0:T(8,128)(2,1)} %copy-done.14, ...), custom_call_target="tpu_custom_call" | custom-call | tf_op jit(solution)/shard_map/first/pallas_call | solution.py:426
  86.5 9.7 %all-to-all-start.2 = ((bf16[32,2,32,128]{3,2,1,0:T(8,128)(2,1)}), bf16[32,2,32,128]{3,2,1,0:T(8,128)(2,1)S(1)}, u32[]{:S(2)}, u32[]{:S(2)}) async-start(bf16[32,2,32,128]{3,2,1,0:T(8,128)(2,1)} %first.1), calls=%async_computation.2 | async-start | bytes 1048576 | tf_op jit(solution)/shard_map/all_to_all | solution.py:453
  96.1 1.0 collective-permute-start.11
  97.3 2.2 %compact.1 = (s32[288]{0:T(512)}, s32[288]{0:T(512)}, s32[1]{0:T(128)}) custom-call(s32[128]{0:T(128)} %reshape.116.hplaces), custom_call_target="tpu_custom_call" | custom-call | tf_op jit(solution)/shard_map/compact/pallas_call | solution.py:455
  100.3 13.0 %all-to-all-done.2 = bf16[32,2,32,128]{3,2,1,0:T(8,128)(2,1)S(1)} async-done(((bf16[32,2,32,128]{3,2,1,0:T(8,128)(2,1)}), bf16[32,2,32,128]{3,2,1,0:T(8,128)(2,1)S(1)}, u32[]{:S(2)}, u32[]{:S(2)}) %all-to-all-start.2) | async-done | bytes 524320 | tf_op jit(solution)/shard_map/all_to_all | solution.py:453
  113.3 1.2 collective-permute-start.15
  114.7 1.4 project.3
  116.9 6.8 %collective-permute-done.15.refs_1_ = bf16[16,2,2,32,128]{4,3,2,1,0:T(8,128)(2,1)S(1)} collective-permute-done((bf16[16,2,2,32,128]{4,3,2,1,0:T(8,128)(2,1)S(1)}, bf16[16,2,2,32,128]{4,3,2,1,0:T(8,128)(2,1)S(1)}, u32[]{:S(2)}, u32[]{:S(2)}) %collective-permute-start.15) | collective-permute-done | bytes 524320 | tf_op jit(solution)/shard_map/ppermute | solution.py:481
  123.7 2.2 %collective-permute-done.14.refs_0_ = bf16[16,2,2,32,128]{4,3,2,1,0:T(8,128)(2,1)S(1)} collective-permute-done((bf16[16,2,2,32,128]{4,3,2,1,0:T(8,128)(2,1)S(1)}, bf16[16,2,2,32,128]{4,3,2,1,0:T(8,128)(2,1)S(1)}, u32[]{:S(2)}, u32[]{:S(2)}) %collective-permute-start.14) | collective-permute-done | bytes 524320 | tf_op jit(solution)/shard_map/ppermute | solution.py:480
  125.9 2.4 %project.4 = (bf16[2,32,2,32,128]{4,3,2,1,0:T(8,128)(2,1)S(1)}, bf16[2,32,2,32,128]{4,3,2,1,0:T(8,128)(2,1)S(1)}) custom-call(bf16[16,2,2,32,128]{4,3,2,1,0:T(8,128)(2,1)S(1)} %collective-permute-done.14.refs_0_, bf16[16,2,2,32,128]{4,3,2,1,0:T(8,128)(2,1)S(1)} %collective-permute-done.15.refs_1_, bf16[128,512]{1,0:T(8,128)(2,1)S(1)} %copy_bitcast_fusion.refs_1_.refs_2_, ...), custom_call_target="tpu_custom_call" | custom-call | tf_op jit(solution)/shard_map/project/pallas_call | solution.py:471
  128.4 1.0 copy-done.1
  129.4 4.1 %collective-permute-start.19 = (bf16[2,32,2,32,128]{4,3,2,1,0:T(8,128)(2,1)S(1)}, bf16[2,32,2,32,128]{4,3,2,1,0:T(8,128)(2,1)S(1)}, u32[]{:S(2)}, u32[]{:S(2)}) collective-permute-start(bf16[2,32,2,32,128]{4,3,2,1,0:T(8,128)(2,1)S(1)} %get-tuple-element.72), channel_id=1, source_target_pairs={{0,1},{1,0},{2,3},{3,2},{4,5},{5,4},{6,7},{7,6},{8,9},{9,8},{10,11... | collective-permute-start | bytes 3145736 | tf_op jit(solution)/shard_map/ppermute | solution.py:77
  133.6 1.5 collective-permute-start.16
  135.1 1.4 collective-permute-done.18.rest_2_.rest_3_
  137.9 7.9 %second_near.1.near = f32[2,128,128]{2,1,0:T(8,128)} custom-call(s32[4]{0:T(128)} %copy-done.7, s32[2]{0:T(128)} %copy-done.8, s32[14]{0:T(128)} %copy-done.13, s32[2,304]{1,0:T(2,128)} %copy-done.5, s32[2,304]{1,0:T(2,128)} %copy-done.6, bf16[288,128,128]{2,1,0:T(8,128)(2,1)} %bitcast.36, bf16[2,16,2,32,128]{4,3,2,1,0:T(8,128)(2,1)} %copy-done.3, ...), custom_call_target="tpu_custom_call" | custom-call | tf_op jit(solution)/shard_map/second_near/pallas_call | solution.py:491
  145.8 1.4 project.5
  148.6 3.1 %collective-permute-done.21.rest_5_ = bf16[2,16,2,32,128]{4,3,2,1,0:T(8,128)(2,1)S(1)} collective-permute-done((bf16[2,16,2,32,128]{4,3,2,1,0:T(8,128)(2,1)S(1)}, bf16[2,16,2,32,128]{4,3,2,1,0:T(8,128)(2,1)S(1)}, u32[]{:S(2)}, u32[]{:S(2)}) %collective-permute-start.21) | collective-permute-done | bytes 524320 | tf_op jit(solution)/shard_map/ppermute | solution.py:77
  152.9 7.7 %second.1 = bf16[256,128]{1,0:T(8,128)(2,1)} custom-call(s32[4]{0:T(128)} %copy-done.7, s32[2]{0:T(128)} %copy-done.8, s32[1]{0:T(128)} %get-tuple-element.56.htrips, s32[2,304]{1,0:T(2,128)} %copy-done.5, s32[2,304]{1,0:T(2,128)} %copy-done.6, s32[288]{0:T(512)} %get-tuple-element.57.hids, s32[288]{0:T(512)} %get-tuple-element.58.hplaces, ...), custom_call_target="tpu_custom_call" | custom-call | tf_op jit(solution)/shard_map/second/pallas_call | solution.py:511
  (119 shorter events, 14.9 us)
Async XLA Ops:
  0.0 14.2 %copy-start.10 = (s32[1,8,8]{2,1,0:T(8,128)S(1)}, s32[1,8,8]{2,1,0:T(8,128)}, u32[]{:S(2)}) copy-start(s32[1,8,8]{2,1,0:T(8,128)} %cols.1) | copy-start | bytes 772
  0.0 14.2 %copy-start.9 = (s32[1,8,8]{2,1,0:T(8,128)S(1)}, s32[1,8,8]{2,1,0:T(8,128)}, u32[]{:S(2)}) copy-start(s32[1,8,8]{2,1,0:T(8,128)} %slots.1) | copy-start | bytes 772
  0.0 14.2 %copy-start.12 = (s32[1,8,36]{2,1,0:T(8,128)S(1)}, s32[1,8,36]{2,1,0:T(8,128)}, u32[]{:S(2)}) copy-start(s32[1,8,36]{2,1,0:T(8,128)} %lcols.1) | copy-start | bytes 3460
  0.0 14.2 %copy-start.11 = (s32[1,8,36]{2,1,0:T(8,128)S(1)}, s32[1,8,36]{2,1,0:T(8,128)}, u32[]{:S(2)}) copy-start(s32[1,8,36]{2,1,0:T(8,128)} %rows.1) | copy-start | bytes 3460
  1.7 27.0 %all-to-all-start.1 = ((bf16[16,128,128]{2,1,0:T(8,128)(2,1)}), bf16[16,128,128]{2,1,0:T(8,128)(2,1)S(1)}, u32[]{:S(2)}, u32[]{:S(2)}) async-start(bf16[16,128,128]{2,1,0:T(8,128)(2,1)} %broadcast_in_dim.18), calls=%async_computation.1 | async-start | bytes 1048576 | tf_op jit(solution)/shard_map/all_to_all | solution.py:82
  14.2 14.5 %copy-start.7 = (s32[4]{0:T(128)}, s32[4]{0:T(128)S(1)}, u32[]{:S(2)}) copy-start(s32[4]{0:T(128)S(1)} %pad_add_fusion.meta) | copy-start | bytes 52
  28.8 11.9 %copy-start.16 = (bf16[16,128,128]{2,1,0:T(8,128)(2,1)}, bf16[16,128,128]{2,1,0:T(8,128)(2,1)S(1)}, u32[]{:S(2)}) copy-start(bf16[16,128,128]{2,1,0:T(8,128)(2,1)S(1)} %all-to-all-done.1.rest_0_) | copy-start | bytes 1572868
  28.8 48.1 %all-to-all-start = ((bf16[64,72,128]{2,1,0:T(8,128)(2,1)}), bf16[64,72,128]{2,1,0:T(8,128)(2,1)S(1)}, u32[]{:S(2)}, u32[]{:S(2)}) async-start(bf16[64,72,128]{2,1,0:T(8,128)(2,1)} %get-tuple-element.45), calls=%async_computation | async-start | bytes 2359296 | tf_op jit(solution)/shard_map/all_to_all | solution.py:401
  38.1 19.8 %collective-permute-start.1 = (bf16[16,128,128]{2,1,0:T(8,128)(2,1)S(1)}, bf16[16,128,128]{2,1,0:T(8,128)(2,1)S(1)}, u32[]{:S(2)}, u32[]{:S(2)}) collective-permute-start(bf16[16,128,128]{2,1,0:T(8,128)(2,1)S(1)} %all-to-all-done.1.rest_0_), channel_id=1, source_target_pairs={{0,192},{64,0},{128,64},{192,128},{1,193},{65,1},{129,65},{193,129... | collective-permute-start | bytes 1572872 | tf_op jit(solution)/shard_map/ppermute | solution.py:65
  40.6 23.6 %collective-permute-start = (bf16[16,128,128]{2,1,0:T(8,128)(2,1)S(1)}, bf16[16,128,128]{2,1,0:T(8,128)(2,1)S(1)}, u32[]{:S(2)}, u32[]{:S(2)}) collective-permute-start(bf16[16,128,128]{2,1,0:T(8,128)(2,1)S(1)} %all-to-all-done.1.rest_0_), channel_id=1, source_target_pairs={{0,64},{64,128},{128,192},{192,0},{1,65},{65,129},{129,193},{193,1... | collective-permute-start | bytes 1572872 | tf_op jit(solution)/shard_map/ppermute | solution.py:64
  40.6 27.8 %collective-permute-start.2 = (bf16[16,128,128]{2,1,0:T(8,128)(2,1)S(1)}, bf16[16,128,128]{2,1,0:T(8,128)(2,1)S(1)}, u32[]{:S(2)}, u32[]{:S(2)}) collective-permute-start(bf16[16,128,128]{2,1,0:T(8,128)(2,1)S(1)} %all-to-all-done.1.rest_0_), channel_id=1, source_target_pairs={{0,1},{1,0},{2,3},{3,2},{4,5},{5,4},{6,7},{7,6},{8,9},{9,8},{10,11... | collective-permute-start | bytes 1572872 | tf_op jit(solution)/shard_map/ppermute | solution.py:77
  57.9 10.4 %collective-permute-start.4 = (bf16[16,128,128]{2,1,0:T(8,128)(2,1)S(1)}, bf16[16,128,128]{2,1,0:T(8,128)(2,1)S(1)}, u32[]{:S(2)}, u32[]{:S(2)}) collective-permute-start(bf16[16,128,128]{2,1,0:T(8,128)(2,1)S(1)} %collective-permute-done.1.rest_2_), channel_id=1, source_target_pairs={{0,1},{1,0},{2,3},{3,2},{4,5},{5,4},{6,7},{7,6},{8,9},{9,8},{10,11... | collective-permute-start | bytes 1572872 | tf_op jit(solution)/shard_map/ppermute | solution.py:77
  64.2 4.2 %collective-permute-start.3 = (bf16[16,128,128]{2,1,0:T(8,128)(2,1)S(1)}, bf16[16,128,128]{2,1,0:T(8,128)(2,1)S(1)}, u32[]{:S(2)}, u32[]{:S(2)}) collective-permute-start(bf16[16,128,128]{2,1,0:T(8,128)(2,1)S(1)} %collective-permute-done.rest_1_), channel_id=1, source_target_pairs={{0,1},{1,0},{2,3},{3,2},{4,5},{5,4},{6,7},{7,6},{8,9},{9,8},{10,11... | collective-permute-start | bytes 1572872 | tf_op jit(solution)/shard_map/ppermute | solution.py:77
  66.7 8.7 %collective-permute-start.6 = (bf16[8,128,128]{2,1,0:T(8,128)(2,1)S(1)}, bf16[8,128,128]{2,1,0:T(8,128)(2,1)S(1)}, u32[]{:S(2)}, u32[]{:S(2)}) collective-permute-start(bf16[8,128,128]{2,1,0:T(8,128)(2,1)S(1)} %slice.33), channel_id=1, source_target_pairs={{0,192},{64,0},{128,64},{192,128},{1,193},{65,1},{129,65},{193,129... | collective-permute-start | bytes 786440 | tf_op jit(solution)/shard_map/ppermute | solution.py:72
  66.9 9.2 %collective-permute-start.5 = (bf16[8,128,128]{2,1,0:T(8,128)(2,1)S(1)}, bf16[8,128,128]{2,1,0:T(8,128)(2,1)S(1)}, u32[]{:S(2)}, u32[]{:S(2)}) collective-permute-start(bf16[8,128,128]{2,1,0:T(8,128)(2,1)S(1)} %slice.32), channel_id=1, source_target_pairs={{0,64},{64,128},{128,192},{192,0},{1,65},{65,129},{129,193},{193,1... | collective-permute-start | bytes 786440 | tf_op jit(solution)/shard_map/ppermute | solution.py:71
  76.1 1.9 %collective-permute-start.7 = (bf16[8,128,128]{2,1,0:T(8,128)(2,1)S(1)}, bf16[8,128,128]{2,1,0:T(8,128)(2,1)S(1)}, u32[]{:S(2)}, u32[]{:S(2)}) collective-permute-start(bf16[8,128,128]{2,1,0:T(8,128)(2,1)S(1)} %collective-permute-done.5.rest_3_), channel_id=1, source_target_pairs={{0,1},{1,0},{2,3},{3,2},{4,5},{5,4},{6,7},{7,6},{8,9},{9,8},{10,11... | collective-permute-start | bytes 786440 | tf_op jit(solution)/shard_map/ppermute | solution.py:77
  76.9 1.5 collective-permute-start.8
  86.0 11.2 %collective-permute-start.9 = (f32[136,128]{1,0:T(8,128)S(1)}, f32[136,128]{1,0:T(8,128)S(1)}, u32[]{:S(2)}, u32[]{:S(2)}) collective-permute-start(f32[136,128]{1,0:T(8,128)S(1)} %get-tuple-element.82), channel_id=1, source_target_pairs={{0,2},{2,0},{1,3},{3,1},{4,6},{6,4},{5,7},{7,5},{8,10},{10,8},{9,1... | collective-permute-start | bytes 208904 | tf_op jit(solution)/shard_map/ppermute | solution.py:77
  86.5 26.8 %all-to-all-start.2 = ((bf16[32,2,32,128]{3,2,1,0:T(8,128)(2,1)}), bf16[32,2,32,128]{3,2,1,0:T(8,128)(2,1)S(1)}, u32[]{:S(2)}, u32[]{:S(2)}) async-start(bf16[32,2,32,128]{3,2,1,0:T(8,128)(2,1)} %first.1), calls=%async_computation.2 | async-start | bytes 1048576 | tf_op jit(solution)/shard_map/all_to_all | solution.py:453
  96.1 3.4 %collective-permute-start.11 = (bf16[512,128]{1,0:T(8,128)(2,1)S(1)}, bf16[512,128]{1,0:T(8,128)(2,1)S(1)}, u32[]{:S(2)}, u32[]{:S(2)}) collective-permute-start(bf16[512,128]{1,0:T(8,128)(2,1)S(1)} %copy-done.32), channel_id=1, source_target_pairs={{0,1},{1,0},{2,3},{3,2},{4,5},{5,4},{6,7},{7,6},{8,9},{9,8},{10,11... | collective-permute-start | bytes 393224 | tf_op jit(solution)/shard_map/ppermute | solution.py:77
  97.2 2.3 %collective-permute-start.10 = (f32[2,136,128]{2,1,0:T(8,128)S(1)}, f32[2,136,128]{2,1,0:T(8,128)S(1)}, u32[]{:S(2)}, u32[]{:S(2)}) collective-permute-start(f32[2,136,128]{2,1,0:T(8,128)S(1)} %get-tuple-element.80), channel_id=1, source_target_pairs={{0,1},{1,0},{2,3},{3,2},{4,5},{5,4},{6,7},{7,6},{8,9},{9,8},{10,11... | collective-permute-start | bytes 417800 | tf_op jit(solution)/shard_map/ppermute | solution.py:77
  99.5 15.2 %copy-start.15 = (bf16[64,72,128]{2,1,0:T(8,128)(2,1)S(1)}, bf16[64,72,128]{2,1,0:T(8,128)(2,1)}, u32[]{:S(2)}) copy-start(bf16[64,72,128]{2,1,0:T(8,128)(2,1)} %copy-done.14) | copy-start | bytes 3538948
  113.3 10.5 %collective-permute-start.15 = (bf16[16,2,2,32,128]{4,3,2,1,0:T(8,128)(2,1)S(1)}, bf16[16,2,2,32,128]{4,3,2,1,0:T(8,128)(2,1)S(1)}, u32[]{:S(2)}, u32[]{:S(2)}) collective-permute-start(bf16[16,2,2,32,128]{4,3,2,1,0:T(8,128)(2,1)S(1)} %bitcast.31), channel_id=1, source_target_pairs={{0,192},{64,0},{128,64},{192,128},{1,193},{65,1},{129,65},{193,129... | collective-permute-start | bytes 1572872 | tf_op jit(solution)/shard_map/ppermute | solution.py:481
  114.5 11.4 %collective-permute-start.14 = (bf16[16,2,2,32,128]{4,3,2,1,0:T(8,128)(2,1)S(1)}, bf16[16,2,2,32,128]{4,3,2,1,0:T(8,128)(2,1)S(1)}, u32[]{:S(2)}, u32[]{:S(2)}) collective-permute-start(bf16[16,2,2,32,128]{4,3,2,1,0:T(8,128)(2,1)S(1)} %bitcast.32), channel_id=1, source_target_pairs={{0,64},{64,128},{128,192},{192,0},{1,65},{65,129},{129,193},{193,1... | collective-permute-start | bytes 1572872 | tf_op jit(solution)/shard_map/ppermute | solution.py:480
  114.7 33.3 %collective-permute-start.13 = (bf16[64,72,128]{2,1,0:T(8,128)(2,1)S(1)}, bf16[64,72,128]{2,1,0:T(8,128)(2,1)S(1)}, u32[]{:S(2)}, u32[]{:S(2)}) collective-permute-start(bf16[64,72,128]{2,1,0:T(8,128)(2,1)S(1)} %copy-done.15), channel_id=1, source_target_pairs={{0,2},{2,0},{1,3},{3,1},{4,6},{6,4},{5,7},{7,5},{8,10},{10,8},{9,1... | collective-permute-start | bytes 3538952 | tf_op jit(solution)/shard_map/ppermute | solution.py:77
  129.4 7.5 %collective-permute-start.19 = (bf16[2,32,2,32,128]{4,3,2,1,0:T(8,128)(2,1)S(1)}, bf16[2,32,2,32,128]{4,3,2,1,0:T(8,128)(2,1)S(1)}, u32[]{:S(2)}, u32[]{:S(2)}) collective-permute-start(bf16[2,32,2,32,128]{4,3,2,1,0:T(8,128)(2,1)S(1)} %get-tuple-element.72), channel_id=1, source_target_pairs={{0,1},{1,0},{2,3},{3,2},{4,5},{5,4},{6,7},{7,6},{8,9},{9,8},{10,11... | collective-permute-start | bytes 3145736 | tf_op jit(solution)/shard_map/ppermute | solution.py:77
  133.5 3.0 %collective-permute-start.18 = (bf16[2,16,2,32,128]{4,3,2,1,0:T(8,128)(2,1)S(1)}, bf16[2,16,2,32,128]{4,3,2,1,0:T(8,128)(2,1)S(1)}, u32[]{:S(2)}, u32[]{:S(2)}) collective-permute-start(bf16[2,16,2,32,128]{4,3,2,1,0:T(8,128)(2,1)S(1)} %get-tuple-element.71), channel_id=1, source_target_pairs={{0,1},{1,0},{2,3},{3,2},{4,5},{5,4},{6,7},{7,6},{8,9},{9,8},{10,11... | collective-permute-start | bytes 1572872 | tf_op jit(solution)/shard_map/ppermute | solution.py:77
  133.6 12.3 %collective-permute-start.17 = (bf16[8,2,2,32,128]{4,3,2,1,0:T(8,128)(2,1)S(1)}, bf16[8,2,2,32,128]{4,3,2,1,0:T(8,128)(2,1)S(1)}, u32[]{:S(2)}, u32[]{:S(2)}) collective-permute-start(bf16[8,2,2,32,128]{4,3,2,1,0:T(8,128)(2,1)S(1)} %slice.28), channel_id=1, source_target_pairs={{0,192},{64,0},{128,64},{192,128},{1,193},{65,1},{129,65},{193,129... | collective-permute-start | bytes 786440 | tf_op jit(solution)/shard_map/ppermute | solution.py:486
  133.6 12.2 %collective-permute-start.16 = (bf16[8,2,2,32,128]{4,3,2,1,0:T(8,128)(2,1)S(1)}, bf16[8,2,2,32,128]{4,3,2,1,0:T(8,128)(2,1)S(1)}, u32[]{:S(2)}, u32[]{:S(2)}) collective-permute-start(bf16[8,2,2,32,128]{4,3,2,1,0:T(8,128)(2,1)S(1)} %slice.27), channel_id=1, source_target_pairs={{0,64},{64,128},{128,192},{192,0},{1,65},{65,129},{129,193},{193,1... | collective-permute-start | bytes 786440 | tf_op jit(solution)/shard_map/ppermute | solution.py:485
  136.5 12.0 %collective-permute-start.12 = (bf16[64,72,128]{2,1,0:T(8,128)(2,1)S(1)}, bf16[64,72,128]{2,1,0:T(8,128)(2,1)S(1)}, u32[]{:S(2)}, u32[]{:S(2)}) collective-permute-start(bf16[64,72,128]{2,1,0:T(8,128)(2,1)S(1)} %copy-done.15), channel_id=1, source_target_pairs={{0,1},{1,0},{2,3},{3,2},{4,5},{5,4},{6,7},{7,6},{8,9},{9,8},{10,11... | collective-permute-start | bytes 3538952 | tf_op jit(solution)/shard_map/ppermute | solution.py:77
  148.0 3.6 %collective-permute-start.20 = (bf16[64,72,128]{2,1,0:T(8,128)(2,1)S(1)}, bf16[64,72,128]{2,1,0:T(8,128)(2,1)S(1)}, u32[]{:S(2)}, u32[]{:S(2)}) collective-permute-start(bf16[64,72,128]{2,1,0:T(8,128)(2,1)S(1)} %collective-permute-done.13.h2), channel_id=1, source_target_pairs={{0,1},{1,0},{2,3},{3,2},{4,5},{5,4},{6,7},{7,6},{8,9},{9,8},{10,11... | collective-permute-start | bytes 3538952 | tf_op jit(solution)/shard_map/ppermute | solution.py:77
  148.2 3.4 %collective-permute-start.21 = (bf16[2,16,2,32,128]{4,3,2,1,0:T(8,128)(2,1)S(1)}, bf16[2,16,2,32,128]{4,3,2,1,0:T(8,128)(2,1)S(1)}, u32[]{:S(2)}, u32[]{:S(2)}) collective-permute-start(bf16[2,16,2,32,128]{4,3,2,1,0:T(8,128)(2,1)S(1)} %get-tuple-element.76), channel_id=1, source_target_pairs={{0,1},{1,0},{2,3},{3,2},{4,5},{5,4},{6,7},{7,6},{8,9},{9,8},{10,11... | collective-permute-start | bytes 1572872 | tf_op jit(solution)/shard_map/ppermute | solution.py:77
  (28 other events, 70.2 us)

commit v3 on v2

--- a/solution.py
+++ b/solution.py
@@ -36,6 +36,7 @@
 SMEM = pl.BlockSpec(memory_space=pltpu.SMEM)
 VMEM = pl.BlockSpec(memory_space=pltpu.VMEM)
 ANY = pl.BlockSpec(memory_space=pl.ANY)
+HBM = pl.BlockSpec(memory_space=pltpu.MemorySpace.HBM)
 
 
 def params(mib):
@@ -371,7 +372,8 @@
     i32 = jnp.int32
     blk, core, feat = lax.axis_index(BLK), lax.axis_index("c"), lax.axis_index(FEAT)
     meta = jnp.stack([blk, feat, core, owner_map[0]]).astype(i32)
-    light = light_tiles.reshape(NL, T, T)
+    in_hbm = lambda x: pltpu.with_memory_space_constraint(x, pltpu.MemorySpace.HBM)
+    light = in_hbm(light_tiles.reshape(NL, T, T))
     int_list = jax.ShapeDtypeStruct((NL,), i32)
     int_lists = jax.ShapeDtypeStruct((2, LIST), i32)
     needs = jax.ShapeDtypeStruct((FAR_AT // STEP,), i32)
@@ -386,7 +388,7 @@
         out_shape=(
             jax.ShapeDtypeStruct((NG, 2 * QR + NOTES, T), BF16), int_lists, int_lists, needs, two_ints
         ),
-        in_specs=[SMEM] * 5 + [ANY],
+        in_specs=[SMEM] * 5 + [HBM],
         out_specs=(VMEM, SMEM, SMEM, SMEM, SMEM),
         scratch_shapes=[
             pltpu.VMEM((NH + 1, QR, T), BF16),
@@ -397,7 +399,7 @@
         compiler_params=params(16),
         cost_estimate=pl.CostEstimate(flops=0, transcendentals=0, bytes_accessed=30_000_000),
         name="pack",
-    )(meta, heavy_slots, heavy_cols, light_rows, light_cols, heavy_tiles.reshape(NH, T, T))
+    )(meta, heavy_slots, heavy_cols, light_rows, light_cols, in_hbm(heavy_tiles.reshape(NH, T, T)))
     arrived = lax.all_to_all(packed, GROUP, 0, 0, tiled=True)
     own = along_x(plane)
     own, far_parts = own[:3], own[3:]
@@ -411,14 +413,14 @@
     first_near = pl.pallas_call(
         first_near_kernel,
         out_shape=jax.ShapeDtypeStruct((2, QR, T), jnp.float32),
-        in_specs=[SMEM] * 4 + [ANY] * 7,
+        in_specs=[SMEM] * 4 + [HBM] + [ANY] * 6,
         out_specs=VMEM,
         scratch_shapes=[
             pltpu.VMEM((NT + 1, T, T), BF16),
             pltpu.VMEM((NEAR_STEPS * LT, QR, T), BF16),
             pltpu.SemaphoreType.DMA((6 + NEAR_STEPS,)),
         ],
-        compiler_params=params(54),
+        compiler_params=params(24),
         name="first_near",
     )(meta, trips, ids, places, light, *own, *other)
     first_near, far_parts = lax.optimization_barrier((first_near, far_parts))
@@ -426,7 +428,7 @@
     aggregated = pl.pallas_call(
         first_kernel,
         out_shape=jax.ShapeDtypeStruct((2 * NPLANE, 2, QR, T), BF16),
-        in_specs=[SMEM] * 5 + [ANY] * 2 + [VMEM] + [ANY] * len(held),
+        in_specs=[SMEM] * 5 + [HBM, ANY, VMEM] + [ANY] * len(held),
         out_specs=VMEM,
         scratch_shapes=[
             pltpu.VMEM((NT + 1, T, T), BF16),
@@ -434,7 +436,7 @@
             pltpu.VMEM((SLOTS, QR, T), BF16),
             pltpu.SemaphoreType.DMA((len(held) + 4,)),
         ],
-        compiler_params=params(54),
+        compiler_params=params(24),
         name="first",
     )(meta, trips, ids, places, hplaces, light, arrived, first_near, *held)
 
@@ -491,7 +493,7 @@
     second_near = pl.pallas_call(
         second_near_kernel,
         out_shape=jax.ShapeDtypeStruct((2, T, T), jnp.float32),
-        in_specs=[SMEM] * 5 + [ANY] * 5,
+        in_specs=[SMEM] * 5 + [HBM] + [ANY] * 4,
         out_specs=VMEM,
         scratch_shapes=[
             pltpu.VMEM((NT + 1, 2, 2, QR, T), BF16),
@@ -499,7 +501,7 @@
             pltpu.SemaphoreType.DMA((12,)),
             pltpu.SemaphoreType.DMA((NEAR_STEPS,)),
         ],
-        compiler_params=params(54),
+        compiler_params=params(24),
         name="second_near",
     )(meta, trips, need, ids, places, light, *mine, *swapped)
     far, second_near = lax.optimization_barrier((far, second_near))
@@ -511,7 +513,7 @@
     return pl.pallas_call(
         second_kernel,
         out_shape=jax.ShapeDtypeStruct((2 * T, T), BF16),
-        in_specs=[SMEM] * 7 + [ANY] * 5 + [VMEM] * 2 + [ANY] * 6,
+        in_specs=[SMEM] * 7 + [HBM] + [ANY] * 4 + [VMEM] * 2 + [ANY] * 6,
         out_specs=VMEM,
         scratch_shapes=[
             pltpu.VMEM((NT + 1, 2, 2, QR, T), BF16),
@@ -519,7 +521,7 @@
             pltpu.VMEM((SLOTS, T, T), BF16),
             pltpu.SemaphoreType.DMA((26,)),
         ],
-        compiler_params=params(54),
+        compiler_params=params(24),
         name="second",
     )(
         meta, trips, htrips, ids, places, hids, hlist, light, arrived, hc, hy, hyc, second_near,

time: 161 us -> 154 us (0.957)
  local copies, waits for them, and re-layouts: 14 us -> 5.44 us
  waiting for transfers between devices: 48.9 us -> 56 us
  Pallas kernels: 42.3 us -> 35.4 us
    unnamed x70 -> x34, local copies, waits for them, and re-layouts: 11.7 us -> 3.73 us
    all_to_all x1, waiting for transfers between devices: 3.65 us -> 7.34 us  [everyone(): return lax.all_to_all(spread, axis, 0, 0, tiled=True)]
    pallas_call x1, Pallas kernels: 7.94 us -> 5.48 us  [per_device(): pl.pallas_call(second_near_kernel, out_shape=jax.ShapeDtypeStruct((2, T,...]
    pallas_call x1, Pallas kernels: 6.46 us -> 4.39 us  [per_device(): pl.pallas_call(first_kernel, out_shape=jax.ShapeDtypeStruct((2 * NPLANE,...]
    ppermute x1, waiting for transfers between devices: 0.01 us -> 1.97 us  [along_x(): lax.ppermute(ahead[far:], 'x', around('x', -1))]
  transfers between devices with their start and end apart: 25 -> 25, of which waited for: 11 -> 12; matrix products, arithmetic and copies ran while one was open for 1% -> 1% of each run, Pallas kernels for 17% -> 16%
where the time goes in v3:
time: 154 us; the launch traced here: 153 us
  waiting for transfers between devices  56 us (36%)
  starting transfers between devices  54.8 us (36%)
  Pallas kernels  35.4 us (23%)
  local copies, waits for them, and re-layouts  5.44 us (4%)
    ppermute x14, starting transfers between devices, swap(): return lax.ppermute(x, axis, around(axis, 1))  17 us
    ppermute x1, waiting for transfers between devices, along_x(): ahead = lax.ppermute(near, 'x', around('x', -1))  15.3 us
    all_to_all x1, waiting for transfers between devices, per_device(): lax.all_to_all(aggregated, (*PLANE, 'yl'), 0, 0, tiled=True)  13 us
    all_to_all x1, starting transfers between devices, everyone(): return lax.all_to_all(spread, axis, 0, 0, tiled=True)  11.7 us
    all_to_all x1, starting transfers between devices, per_device(): lax.all_to_all(aggregated, (*PLANE, 'yl'), 0, 0, tiled=True)  9.57 us
    all_to_all x1, starting transfers between devices, per_device(): arrived = lax.all_to_all(packed, GROUP, 0, 0, tiled=True)  9.33 us
    ppermute x1, waiting for transfers between devices, per_device(): ahead = lax.ppermute(rows, 'x', around('x', -1))  7.66 us
    all_to_all x1, waiting for transfers between devices, everyone(): return lax.all_to_all(spread, axis, 0, 0, tiled=True)  7.34 us
  transfers between devices with their start and end apart: 25, of which 12 were waited for; matrix products, arithmetic and copies ran while one was open for 1% of the time, Pallas kernels for 16%

profile of v3, /device:TPU:1, one launch (start us, length us, event | category | flops | bytes accessed | tf_op | source)
XLA Modules:
  0.0 153.2 jit_solution(16442096230404803874)
XLA Ops:
  1.7 11.7 %all-to-all-start.1 = ((bf16[16,128,128]{2,1,0:T(8,128)(2,1)}), bf16[16,128,128]{2,1,0:T(8,128)(2,1)S(1)}, u32[]{:S(2)}, u32[]{:S(2)}) async-start(bf16[16,128,128]{2,1,0:T(8,128)(2,1)} %broadcast_in_dim.18), calls=%async_computation.1 | async-start | bytes 1048576 | tf_op jit(solution)/shard_map/all_to_all | solution.py:83
  14.3 7.1 %pack.1 = (bf16[64,72,128]{2,1,0:T(8,128)(2,1)}, s32[2,304]{1,0:T(2,128)S(1)}, s32[2,304]{1,0:T(2,128)S(1)}, s32[14]{0:T(128)S(1)}, s32[2]{0:T(128)S(1)}) custom-call(s32[4]{0:T(128)S(1)} %pad_add_fusion.meta, s32[1,8,8]{2,1,0:T(8,128)S(1)} %copy-done.6, s32[1,8,8]{2,1,0:T(8,128)S(1)} %copy-done.7, s32[1,8,36]{2,1,0:T(8,128)S(1)} %copy-done.8, ...), custom_call_target="tpu_custom_call" | custom-call | bytes 30000000 | tf_op jit(solution)/shard_map/pack/pallas_call | solution.py:386
  21.4 7.3 %all-to-all-done.1.rest_0_ = bf16[16,128,128]{2,1,0:T(8,128)(2,1)S(1)} async-done(((bf16[16,128,128]{2,1,0:T(8,128)(2,1)}), bf16[16,128,128]{2,1,0:T(8,128)(2,1)S(1)}, u32[]{:S(2)}, u32[]{:S(2)}) %all-to-all-start.1) | async-done | bytes 524320 | tf_op jit(solution)/shard_map/all_to_all | solution.py:83
  28.7 9.3 %all-to-all-start = ((bf16[64,72,128]{2,1,0:T(8,128)(2,1)}), bf16[64,72,128]{2,1,0:T(8,128)(2,1)S(1)}, u32[]{:S(2)}, u32[]{:S(2)}) async-start(bf16[64,72,128]{2,1,0:T(8,128)(2,1)} %get-tuple-element.45), calls=%async_computation | async-start | bytes 2359296 | tf_op jit(solution)/shard_map/all_to_all | solution.py:403
  38.1 2.5 %collective-permute-start.1 = (bf16[16,128,128]{2,1,0:T(8,128)(2,1)S(1)}, bf16[16,128,128]{2,1,0:T(8,128)(2,1)S(1)}, u32[]{:S(2)}, u32[]{:S(2)}) collective-permute-start(bf16[16,128,128]{2,1,0:T(8,128)(2,1)S(1)} %all-to-all-done.1.rest_0_), channel_id=1, source_target_pairs={{0,192},{64,0},{128,64},{192,128},{1,193},{65,1},{129,65},{193,129... | collective-permute-start | bytes 1572872 | tf_op jit(solution)/shard_map/ppermute | solution.py:66
  40.6 2.1 %collective-permute-start.2 = (bf16[16,128,128]{2,1,0:T(8,128)(2,1)S(1)}, bf16[16,128,128]{2,1,0:T(8,128)(2,1)S(1)}, u32[]{:S(2)}, u32[]{:S(2)}) collective-permute-start(bf16[16,128,128]{2,1,0:T(8,128)(2,1)S(1)} %all-to-all-done.1.rest_0_), channel_id=1, source_target_pairs={{0,1},{1,0},{2,3},{3,2},{4,5},{5,4},{6,7},{7,6},{8,9},{9,8},{10,11... | collective-permute-start | bytes 1572872 | tf_op jit(solution)/shard_map/ppermute | solution.py:78
  42.6 15.3 %collective-permute-done.1.rest_2_ = bf16[16,128,128]{2,1,0:T(8,128)(2,1)S(1)} collective-permute-done((bf16[16,128,128]{2,1,0:T(8,128)(2,1)S(1)}, bf16[16,128,128]{2,1,0:T(8,128)(2,1)S(1)}, u32[]{:S(2)}, u32[]{:S(2)}) %collective-permute-start.1) | collective-permute-done | bytes 524320 | tf_op jit(solution)/shard_map/ppermute | solution.py:66
  57.9 4.0 %collective-permute-start.4 = (bf16[16,128,128]{2,1,0:T(8,128)(2,1)S(1)}, bf16[16,128,128]{2,1,0:T(8,128)(2,1)S(1)}, u32[]{:S(2)}, u32[]{:S(2)}) collective-permute-start(bf16[16,128,128]{2,1,0:T(8,128)(2,1)S(1)} %collective-permute-done.1.rest_2_), channel_id=1, source_target_pairs={{0,1},{1,0},{2,3},{3,2},{4,5},{5,4},{6,7},{7,6},{8,9},{9,8},{10,11... | collective-permute-start | bytes 1572872 | tf_op jit(solution)/shard_map/ppermute | solution.py:78
  61.9 2.3 %collective-permute-done.rest_1_ = bf16[16,128,128]{2,1,0:T(8,128)(2,1)S(1)} collective-permute-done((bf16[16,128,128]{2,1,0:T(8,128)(2,1)S(1)}, bf16[16,128,128]{2,1,0:T(8,128)(2,1)S(1)}, u32[]{:S(2)}, u32[]{:S(2)}) %collective-permute-start) | collective-permute-done | bytes 524320 | tf_op jit(solution)/shard_map/ppermute | solution.py:65
  64.2 2.5 %collective-permute-start.3 = (bf16[16,128,128]{2,1,0:T(8,128)(2,1)S(1)}, bf16[16,128,128]{2,1,0:T(8,128)(2,1)S(1)}, u32[]{:S(2)}, u32[]{:S(2)}) collective-permute-start(bf16[16,128,128]{2,1,0:T(8,128)(2,1)S(1)} %collective-permute-done.rest_1_), channel_id=1, source_target_pairs={{0,1},{1,0},{2,3},{3,2},{4,5},{5,4},{6,7},{7,6},{8,9},{9,8},{10,11... | collective-permute-start | bytes 1572872 | tf_op jit(solution)/shard_map/ppermute | solution.py:78
  66.8 1.5 collective-permute-start.5
  68.4 4.5 %first_near.1.near = f32[2,32,128]{2,1,0:T(8,128)S(1)} custom-call(s32[4]{0:T(128)S(1)} %pad_add_fusion.meta, s32[2]{0:T(128)S(1)} %get-tuple-element.42.trips, s32[2,304]{1,0:T(2,128)S(1)} %get-tuple-element.43.ids, s32[2,304]{1,0:T(2,128)S(1)} %get-tuple-element.44.places, bf16[288,128,128]{2,1,0:T(8,128)(2,1)} %bitcast.34, ...), custom_call_target="tpu_custom_call" | custom-call | tf_op jit(solution)/shard_map/first_near/pallas_call | solution.py:413
  72.9 2.0 %collective-permute-done.6.rest_4_ = bf16[8,128,128]{2,1,0:T(8,128)(2,1)} collective-permute-done((bf16[8,128,128]{2,1,0:T(8,128)(2,1)S(1)}, bf16[8,128,128]{2,1,0:T(8,128)(2,1)}, u32[]{:S(2)}, u32[]{:S(2)}) %collective-permute-start.6) | collective-permute-done | bytes 262176 | tf_op jit(solution)/shard_map/ppermute | solution.py:73
  74.8 1.3 collective-permute-done.5.rest_3_
  77.3 1.2 collective-permute-done.7.rest_8_
  78.8 1.0 copy-done.2
  80.9 4.4 %first.1 = bf16[32,2,32,128]{3,2,1,0:T(8,128)(2,1)S(1)} custom-call(s32[4]{0:T(128)S(1)} %pad_add_fusion.meta, s32[2]{0:T(128)S(1)} %get-tuple-element.42.trips, s32[2,304]{1,0:T(2,128)S(1)} %get-tuple-element.43.ids, s32[2,304]{1,0:T(2,128)S(1)} %get-tuple-element.44.places, s32[128]{0:T(128)S(1)} %reshape.116.hplaces, bf16[288,128,128]{2,1,0:T(8,128)(2,1)} %bitcast.35, ...), custom_call_target="tpu_custom_call" | custom-call | tf_op jit(solution)/shard_map/first/pallas_call | solution.py:428
  86.7 9.6 %all-to-all-start.2 = ((bf16[32,2,32,128]{3,2,1,0:T(8,128)(2,1)}), bf16[32,2,32,128]{3,2,1,0:T(8,128)(2,1)S(1)}, u32[]{:S(2)}, u32[]{:S(2)}) async-start(bf16[32,2,32,128]{3,2,1,0:T(8,128)(2,1)} %copy-done.5), calls=%async_computation.2 | async-start | bytes 1048576 | tf_op jit(solution)/shard_map/all_to_all | solution.py:455
  97.4 2.2 %compact.1 = (s32[288]{0:T(512)}, s32[288]{0:T(512)}, s32[1]{0:T(128)}) custom-call(s32[128]{0:T(128)} %copy-done.13), custom_call_target="tpu_custom_call" | custom-call | tf_op jit(solution)/shard_map/compact/pallas_call | solution.py:457
  100.4 13.0 %all-to-all-done.2 = bf16[32,2,32,128]{3,2,1,0:T(8,128)(2,1)S(1)} async-done(((bf16[32,2,32,128]{3,2,1,0:T(8,128)(2,1)}), bf16[32,2,32,128]{3,2,1,0:T(8,128)(2,1)S(1)}, u32[]{:S(2)}, u32[]{:S(2)}) %all-to-all-start.2) | async-done | bytes 524320 | tf_op jit(solution)/shard_map/all_to_all | solution.py:455
  113.4 1.5 collective-permute-start.14
  114.8 1.4 project.3
  116.2 7.7 %collective-permute-done.15.refs_1_ = bf16[16,2,2,32,128]{4,3,2,1,0:T(8,128)(2,1)S(1)} collective-permute-done((bf16[16,2,2,32,128]{4,3,2,1,0:T(8,128)(2,1)S(1)}, bf16[16,2,2,32,128]{4,3,2,1,0:T(8,128)(2,1)S(1)}, u32[]{:S(2)}, u32[]{:S(2)}) %collective-permute-start.15) | collective-permute-done | bytes 524320 | tf_op jit(solution)/shard_map/ppermute | solution.py:483
  124.9 2.4 %project.4 = (bf16[2,32,2,32,128]{4,3,2,1,0:T(8,128)(2,1)S(1)}, bf16[2,32,2,32,128]{4,3,2,1,0:T(8,128)(2,1)S(1)}) custom-call(bf16[16,2,2,32,128]{4,3,2,1,0:T(8,128)(2,1)S(1)} %collective-permute-done.14.refs_0_, bf16[16,2,2,32,128]{4,3,2,1,0:T(8,128)(2,1)S(1)} %collective-permute-done.15.refs_1_, bf16[128,512]{1,0:T(8,128)(2,1)S(1)} %copy_bitcast_fusion.refs_1_.refs_2_, ...), custom_call_target="tpu_custom_call" | custom-call | tf_op jit(solution)/shard_map/project/pallas_call | solution.py:473
  127.4 4.1 %collective-permute-start.19 = (bf16[2,32,2,32,128]{4,3,2,1,0:T(8,128)(2,1)S(1)}, bf16[2,32,2,32,128]{4,3,2,1,0:T(8,128)(2,1)S(1)}, u32[]{:S(2)}, u32[]{:S(2)}) collective-permute-start(bf16[2,32,2,32,128]{4,3,2,1,0:T(8,128)(2,1)S(1)} %get-tuple-element.72), channel_id=1, source_target_pairs={{0,1},{1,0},{2,3},{3,2},{4,5},{5,4},{6,7},{7,6},{8,9},{9,8},{10,11... | collective-permute-start | bytes 3145736 | tf_op jit(solution)/shard_map/ppermute | solution.py:78
  131.7 1.5 collective-permute-start.16
  133.2 1.3 collective-permute-done.18.rest_2_.rest_3_
  134.9 5.5 %second_near.1.near = f32[2,128,128]{2,1,0:T(8,128)S(1)} custom-call(s32[4]{0:T(128)S(1)} %pad_add_fusion.meta, s32[2]{0:T(128)S(1)} %get-tuple-element.42.trips, s32[14]{0:T(128)S(1)} %get-tuple-element.68.need, s32[2,304]{1,0:T(2,128)S(1)} %get-tuple-element.43.ids, s32[2,304]{1,0:T(2,128)S(1)} %get-tuple-element.44.places, ...), custom_call_target="tpu_custom_call" | custom-call | tf_op jit(solution)/shard_map/second_near/pallas_call | solution.py:493
  140.4 1.4 project.5
  141.8 1.4 collective-permute-start.20
  143.3 3.2 %collective-permute-done.21.rest_5_ = bf16[2,16,2,32,128]{4,3,2,1,0:T(8,128)(2,1)S(1)} collective-permute-done((bf16[2,16,2,32,128]{4,3,2,1,0:T(8,128)(2,1)S(1)}, bf16[2,16,2,32,128]{4,3,2,1,0:T(8,128)(2,1)S(1)}, u32[]{:S(2)}, u32[]{:S(2)}) %collective-permute-start.21) | collective-permute-done | bytes 524320 | tf_op jit(solution)/shard_map/ppermute | solution.py:78
  146.5 6.6 %second.1 = bf16[256,128]{1,0:T(8,128)(2,1)} custom-call(s32[4]{0:T(128)S(1)} %pad_add_fusion.meta, s32[2]{0:T(128)S(1)} %get-tuple-element.42.trips, s32[1]{0:T(128)} %get-tuple-element.56.htrips, s32[2,304]{1,0:T(2,128)S(1)} %get-tuple-element.43.ids, s32[2,304]{1,0:T(2,128)S(1)} %get-tuple-element.44.places, s32[288]{0:T(512)S(1)} %copy-done.10, ...), custom_call_target="tpu_custom_call" | custom-call | tf_op jit(solution)/shard_map/second/pallas_call | solution.py:513
  (83 shorter events, 9.4 us)
Async XLA Ops:
  0.0 14.2 %copy-start.7 = (s32[1,8,8]{2,1,0:T(8,128)S(1)}, s32[1,8,8]{2,1,0:T(8,128)}, u32[]{:S(2)}) copy-start(s32[1,8,8]{2,1,0:T(8,128)} %cols.1) | copy-start | bytes 772
  0.0 14.2 %copy-start.6 = (s32[1,8,8]{2,1,0:T(8,128)S(1)}, s32[1,8,8]{2,1,0:T(8,128)}, u32[]{:S(2)}) copy-start(s32[1,8,8]{2,1,0:T(8,128)} %slots.1) | copy-start | bytes 772
  0.0 14.2 %copy-start.9 = (s32[1,8,36]{2,1,0:T(8,128)S(1)}, s32[1,8,36]{2,1,0:T(8,128)}, u32[]{:S(2)}) copy-start(s32[1,8,36]{2,1,0:T(8,128)} %lcols.1) | copy-start | bytes 3460
  0.0 14.2 %copy-start.8 = (s32[1,8,36]{2,1,0:T(8,128)S(1)}, s32[1,8,36]{2,1,0:T(8,128)}, u32[]{:S(2)}) copy-start(s32[1,8,36]{2,1,0:T(8,128)} %rows.1) | copy-start | bytes 3460
  1.7 27.0 %all-to-all-start.1 = ((bf16[16,128,128]{2,1,0:T(8,128)(2,1)}), bf16[16,128,128]{2,1,0:T(8,128)(2,1)S(1)}, u32[]{:S(2)}, u32[]{:S(2)}) async-start(bf16[16,128,128]{2,1,0:T(8,128)(2,1)} %broadcast_in_dim.18), calls=%async_computation.1 | async-start | bytes 1048576 | tf_op jit(solution)/shard_map/all_to_all | solution.py:83
  28.7 48.2 %all-to-all-start = ((bf16[64,72,128]{2,1,0:T(8,128)(2,1)}), bf16[64,72,128]{2,1,0:T(8,128)(2,1)S(1)}, u32[]{:S(2)}, u32[]{:S(2)}) async-start(bf16[64,72,128]{2,1,0:T(8,128)(2,1)} %get-tuple-element.45), calls=%async_computation | async-start | bytes 2359296 | tf_op jit(solution)/shard_map/all_to_all | solution.py:403
  38.1 19.8 %collective-permute-start.1 = (bf16[16,128,128]{2,1,0:T(8,128)(2,1)S(1)}, bf16[16,128,128]{2,1,0:T(8,128)(2,1)S(1)}, u32[]{:S(2)}, u32[]{:S(2)}) collective-permute-start(bf16[16,128,128]{2,1,0:T(8,128)(2,1)S(1)} %all-to-all-done.1.rest_0_), channel_id=1, source_target_pairs={{0,192},{64,0},{128,64},{192,128},{1,193},{65,1},{129,65},{193,129... | collective-permute-start | bytes 1572872 | tf_op jit(solution)/shard_map/ppermute | solution.py:66
  40.6 23.6 %collective-permute-start = (bf16[16,128,128]{2,1,0:T(8,128)(2,1)S(1)}, bf16[16,128,128]{2,1,0:T(8,128)(2,1)S(1)}, u32[]{:S(2)}, u32[]{:S(2)}) collective-permute-start(bf16[16,128,128]{2,1,0:T(8,128)(2,1)S(1)} %all-to-all-done.1.rest_0_), channel_id=1, source_target_pairs={{0,64},{64,128},{128,192},{192,0},{1,65},{65,129},{129,193},{193,1... | collective-permute-start | bytes 1572872 | tf_op jit(solution)/shard_map/ppermute | solution.py:65
  40.6 27.8 %collective-permute-start.2 = (bf16[16,128,128]{2,1,0:T(8,128)(2,1)S(1)}, bf16[16,128,128]{2,1,0:T(8,128)(2,1)S(1)}, u32[]{:S(2)}, u32[]{:S(2)}) collective-permute-start(bf16[16,128,128]{2,1,0:T(8,128)(2,1)S(1)} %all-to-all-done.1.rest_0_), channel_id=1, source_target_pairs={{0,1},{1,0},{2,3},{3,2},{4,5},{5,4},{6,7},{7,6},{8,9},{9,8},{10,11... | collective-permute-start | bytes 1572872 | tf_op jit(solution)/shard_map/ppermute | solution.py:78
  57.9 10.4 %collective-permute-start.4 = (bf16[16,128,128]{2,1,0:T(8,128)(2,1)S(1)}, bf16[16,128,128]{2,1,0:T(8,128)(2,1)S(1)}, u32[]{:S(2)}, u32[]{:S(2)}) collective-permute-start(bf16[16,128,128]{2,1,0:T(8,128)(2,1)S(1)} %collective-permute-done.1.rest_2_), channel_id=1, source_target_pairs={{0,1},{1,0},{2,3},{3,2},{4,5},{5,4},{6,7},{7,6},{8,9},{9,8},{10,11... | collective-permute-start | bytes 1572872 | tf_op jit(solution)/shard_map/ppermute | solution.py:78
  64.2 4.2 %collective-permute-start.3 = (bf16[16,128,128]{2,1,0:T(8,128)(2,1)S(1)}, bf16[16,128,128]{2,1,0:T(8,128)(2,1)S(1)}, u32[]{:S(2)}, u32[]{:S(2)}) collective-permute-start(bf16[16,128,128]{2,1,0:T(8,128)(2,1)S(1)} %collective-permute-done.rest_1_), channel_id=1, source_target_pairs={{0,1},{1,0},{2,3},{3,2},{4,5},{5,4},{6,7},{7,6},{8,9},{9,8},{10,11... | collective-permute-start | bytes 1572872 | tf_op jit(solution)/shard_map/ppermute | solution.py:78
  66.7 8.1 %collective-permute-start.6 = (bf16[8,128,128]{2,1,0:T(8,128)(2,1)S(1)}, bf16[8,128,128]{2,1,0:T(8,128)(2,1)}, u32[]{:S(2)}, u32[]{:S(2)}) collective-permute-start(bf16[8,128,128]{2,1,0:T(8,128)(2,1)S(1)} %slice.33), channel_id=1, source_target_pairs={{0,192},{64,0},{128,64},{192,128},{1,193},{65,1},{129,65},{193,129... | collective-permute-start | bytes 786440 | tf_op jit(solution)/shard_map/ppermute | solution.py:73
  66.8 9.3 %collective-permute-start.5 = (bf16[8,128,128]{2,1,0:T(8,128)(2,1)S(1)}, bf16[8,128,128]{2,1,0:T(8,128)(2,1)}, u32[]{:S(2)}, u32[]{:S(2)}) collective-permute-start(bf16[8,128,128]{2,1,0:T(8,128)(2,1)S(1)} %slice.32), channel_id=1, source_target_pairs={{0,64},{64,128},{128,192},{192,0},{1,65},{65,129},{129,193},{193,1... | collective-permute-start | bytes 786440 | tf_op jit(solution)/shard_map/ppermute | solution.py:72
  76.2 2.3 %collective-permute-start.7 = (bf16[8,128,128]{2,1,0:T(8,128)(2,1)}, bf16[8,128,128]{2,1,0:T(8,128)(2,1)}, u32[]{:S(2)}, u32[]{:S(2)}) collective-permute-start(bf16[8,128,128]{2,1,0:T(8,128)(2,1)} %collective-permute-done.5.rest_3_), channel_id=1, source_target_pairs={{0,1},{1,0},{2,3},{3,2},{4,5},{5,4},{6,7},{7,6},{8,9},{9,8},{10,11... | collective-permute-start | bytes 786440 | tf_op jit(solution)/shard_map/ppermute | solution.py:78
  77.0 1.9 %collective-permute-start.8 = (bf16[8,128,128]{2,1,0:T(8,128)(2,1)}, bf16[8,128,128]{2,1,0:T(8,128)(2,1)}, u32[]{:S(2)}, u32[]{:S(2)}) collective-permute-start(bf16[8,128,128]{2,1,0:T(8,128)(2,1)} %collective-permute-done.6.rest_4_), channel_id=1, source_target_pairs={{0,1},{1,0},{2,3},{3,2},{4,5},{5,4},{6,7},{7,6},{8,9},{9,8},{10,11... | collective-permute-start | bytes 786440 | tf_op jit(solution)/shard_map/ppermute | solution.py:78
  86.2 11.1 %collective-permute-start.9 = (f32[136,128]{1,0:T(8,128)S(1)}, f32[136,128]{1,0:T(8,128)S(1)}, u32[]{:S(2)}, u32[]{:S(2)}) collective-permute-start(f32[136,128]{1,0:T(8,128)S(1)} %get-tuple-element.82), channel_id=1, source_target_pairs={{0,2},{2,0},{1,3},{3,1},{4,6},{6,4},{5,7},{7,5},{8,10},{10,8},{9,1... | collective-permute-start | bytes 208904 | tf_op jit(solution)/shard_map/ppermute | solution.py:78
  86.7 26.7 %all-to-all-start.2 = ((bf16[32,2,32,128]{3,2,1,0:T(8,128)(2,1)}), bf16[32,2,32,128]{3,2,1,0:T(8,128)(2,1)S(1)}, u32[]{:S(2)}, u32[]{:S(2)}) async-start(bf16[32,2,32,128]{3,2,1,0:T(8,128)(2,1)} %copy-done.5), calls=%async_computation.2 | async-start | bytes 1048576 | tf_op jit(solution)/shard_map/all_to_all | solution.py:455
  96.2 3.3 %collective-permute-start.11 = (bf16[512,128]{1,0:T(8,128)(2,1)S(1)}, bf16[512,128]{1,0:T(8,128)(2,1)S(1)}, u32[]{:S(2)}, u32[]{:S(2)}) collective-permute-start(bf16[512,128]{1,0:T(8,128)(2,1)S(1)} %copy-done.14), channel_id=1, source_target_pairs={{0,1},{1,0},{2,3},{3,2},{4,5},{5,4},{6,7},{7,6},{8,9},{9,8},{10,11... | collective-permute-start | bytes 393224 | tf_op jit(solution)/shard_map/ppermute | solution.py:78
  97.3 2.3 %collective-permute-start.10 = (f32[2,136,128]{2,1,0:T(8,128)S(1)}, f32[2,136,128]{2,1,0:T(8,128)S(1)}, u32[]{:S(2)}, u32[]{:S(2)}) collective-permute-start(f32[2,136,128]{2,1,0:T(8,128)S(1)} %get-tuple-element.80), channel_id=1, source_target_pairs={{0,1},{1,0},{2,3},{3,2},{4,5},{5,4},{6,7},{7,6},{8,9},{9,8},{10,11... | collective-permute-start | bytes 417800 | tf_op jit(solution)/shard_map/ppermute | solution.py:78
  113.4 10.5 %collective-permute-start.15 = (bf16[16,2,2,32,128]{4,3,2,1,0:T(8,128)(2,1)S(1)}, bf16[16,2,2,32,128]{4,3,2,1,0:T(8,128)(2,1)S(1)}, u32[]{:S(2)}, u32[]{:S(2)}) collective-permute-start(bf16[16,2,2,32,128]{4,3,2,1,0:T(8,128)(2,1)S(1)} %bitcast.30), channel_id=1, source_target_pairs={{0,192},{64,0},{128,64},{192,128},{1,193},{65,1},{129,65},{193,129... | collective-permute-start | bytes 1572872 | tf_op jit(solution)/shard_map/ppermute | solution.py:483
  113.4 11.5 %collective-permute-start.14 = (bf16[16,2,2,32,128]{4,3,2,1,0:T(8,128)(2,1)S(1)}, bf16[16,2,2,32,128]{4,3,2,1,0:T(8,128)(2,1)S(1)}, u32[]{:S(2)}, u32[]{:S(2)}) collective-permute-start(bf16[16,2,2,32,128]{4,3,2,1,0:T(8,128)(2,1)S(1)} %bitcast.31), channel_id=1, source_target_pairs={{0,64},{64,128},{128,192},{192,0},{1,65},{65,129},{129,193},{193,1... | collective-permute-start | bytes 1572872 | tf_op jit(solution)/shard_map/ppermute | solution.py:482
  114.8 26.9 %collective-permute-start.13 = (bf16[64,72,128]{2,1,0:T(8,128)(2,1)S(1)}, bf16[64,72,128]{2,1,0:T(8,128)(2,1)S(1)}, u32[]{:S(2)}, u32[]{:S(2)}) collective-permute-start(bf16[64,72,128]{2,1,0:T(8,128)(2,1)S(1)} %all-to-all-done.heavy.h0), channel_id=1, source_target_pairs={{0,2},{2,0},{1,3},{3,1},{4,6},{6,4},{5,7},{7,5},{8,10},{10,8},{9,1... | collective-permute-start | bytes 3538952 | tf_op jit(solution)/shard_map/ppermute | solution.py:78
  127.4 7.5 %collective-permute-start.19 = (bf16[2,32,2,32,128]{4,3,2,1,0:T(8,128)(2,1)S(1)}, bf16[2,32,2,32,128]{4,3,2,1,0:T(8,128)(2,1)S(1)}, u32[]{:S(2)}, u32[]{:S(2)}) collective-permute-start(bf16[2,32,2,32,128]{4,3,2,1,0:T(8,128)(2,1)S(1)} %get-tuple-element.72), channel_id=1, source_target_pairs={{0,1},{1,0},{2,3},{3,2},{4,5},{5,4},{6,7},{7,6},{8,9},{9,8},{10,11... | collective-permute-start | bytes 3145736 | tf_op jit(solution)/shard_map/ppermute | solution.py:78
  131.5 3.0 %collective-permute-start.18 = (bf16[2,16,2,32,128]{4,3,2,1,0:T(8,128)(2,1)S(1)}, bf16[2,16,2,32,128]{4,3,2,1,0:T(8,128)(2,1)S(1)}, u32[]{:S(2)}, u32[]{:S(2)}) collective-permute-start(bf16[2,16,2,32,128]{4,3,2,1,0:T(8,128)(2,1)S(1)} %get-tuple-element.71), channel_id=1, source_target_pairs={{0,1},{1,0},{2,3},{3,2},{4,5},{5,4},{6,7},{7,6},{8,9},{9,8},{10,11... | collective-permute-start | bytes 1572872 | tf_op jit(solution)/shard_map/ppermute | solution.py:78
  131.6 8.8 %collective-permute-start.17 = (bf16[8,2,2,32,128]{4,3,2,1,0:T(8,128)(2,1)S(1)}, bf16[8,2,2,32,128]{4,3,2,1,0:T(8,128)(2,1)S(1)}, u32[]{:S(2)}, u32[]{:S(2)}) collective-permute-start(bf16[8,2,2,32,128]{4,3,2,1,0:T(8,128)(2,1)S(1)} %slice.28), channel_id=1, source_target_pairs={{0,192},{64,0},{128,64},{192,128},{1,193},{65,1},{129,65},{193,129... | collective-permute-start | bytes 786440 | tf_op jit(solution)/shard_map/ppermute | solution.py:488
  131.7 8.7 %collective-permute-start.16 = (bf16[8,2,2,32,128]{4,3,2,1,0:T(8,128)(2,1)S(1)}, bf16[8,2,2,32,128]{4,3,2,1,0:T(8,128)(2,1)S(1)}, u32[]{:S(2)}, u32[]{:S(2)}) collective-permute-start(bf16[8,2,2,32,128]{4,3,2,1,0:T(8,128)(2,1)S(1)} %slice.27), channel_id=1, source_target_pairs={{0,64},{64,128},{128,192},{192,0},{1,65},{65,129},{129,193},{193,1... | collective-permute-start | bytes 786440 | tf_op jit(solution)/shard_map/ppermute | solution.py:487
  134.5 8.8 %collective-permute-start.12 = (bf16[64,72,128]{2,1,0:T(8,128)(2,1)S(1)}, bf16[64,72,128]{2,1,0:T(8,128)(2,1)S(1)}, u32[]{:S(2)}, u32[]{:S(2)}) collective-permute-start(bf16[64,72,128]{2,1,0:T(8,128)(2,1)S(1)} %all-to-all-done.heavy.h0), channel_id=1, source_target_pairs={{0,1},{1,0},{2,3},{3,2},{4,5},{5,4},{6,7},{7,6},{8,9},{9,8},{10,11... | collective-permute-start | bytes 3538952 | tf_op jit(solution)/shard_map/ppermute | solution.py:78
  134.9 11.6 %copy-start.10 = (s32[288]{0:T(512)S(1)}, s32[288]{0:T(512)}, u32[]{:S(2)}) copy-start(s32[288]{0:T(512)} %get-tuple-element.57.hids) | copy-start | bytes 3460
  134.9 11.6 %copy-start.11 = (s32[288]{0:T(512)S(1)}, s32[288]{0:T(512)}, u32[]{:S(2)}) copy-start(s32[288]{0:T(512)} %get-tuple-element.58.hplaces) | copy-start | bytes 3460
  134.9 11.6 %copy-start.12 = (f32[128]{0:T(128)S(1)}, f32[128]{0:T(128)}, u32[]{:S(2)}) copy-start(f32[128]{0:T(128)} %param.16) | copy-start | bytes 1540
  141.8 4.7 %collective-permute-start.20 = (bf16[64,72,128]{2,1,0:T(8,128)(2,1)S(1)}, bf16[64,72,128]{2,1,0:T(8,128)(2,1)S(1)}, u32[]{:S(2)}, u32[]{:S(2)}) collective-permute-start(bf16[64,72,128]{2,1,0:T(8,128)(2,1)S(1)} %collective-permute-done.13.h2), channel_id=1, source_target_pairs={{0,1},{1,0},{2,3},{3,2},{4,5},{5,4},{6,7},{7,6},{8,9},{9,8},{10,11... | collective-permute-start | bytes 3538952 | tf_op jit(solution)/shard_map/ppermute | solution.py:78
  143.2 3.2 %collective-permute-start.21 = (bf16[2,16,2,32,128]{4,3,2,1,0:T(8,128)(2,1)S(1)}, bf16[2,16,2,32,128]{4,3,2,1,0:T(8,128)(2,1)S(1)}, u32[]{:S(2)}, u32[]{:S(2)}) collective-permute-start(bf16[2,16,2,32,128]{4,3,2,1,0:T(8,128)(2,1)S(1)} %get-tuple-element.76), channel_id=1, source_target_pairs={{0,1},{1,0},{2,3},{3,2},{4,5},{5,4},{6,7},{7,6},{8,9},{9,8},{10,11... | collective-permute-start | bytes 1572872 | tf_op jit(solution)/shard_map/ppermute | solution.py:78
  (10 other events, 44.9 us)

commit v4 on v3

--- a/solution.py
+++ b/solution.py
@@ -410,6 +410,7 @@
         nodes < NT, (nodes & 1) * NG + turned(blk, nodes >> 4) * NR + ((nodes & 15) >> 1), NT
     )
 
+    trips, hplaces = lax.optimization_barrier((trips, hplaces))
     first_near = pl.pallas_call(
         first_near_kernel,
         out_shape=jax.ShapeDtypeStruct((2, QR, T), jnp.float32),
@@ -420,7 +421,7 @@
             pltpu.VMEM((NEAR_STEPS * LT, QR, T), BF16),
             pltpu.SemaphoreType.DMA((6 + NEAR_STEPS,)),
         ],
-        compiler_params=params(24),
+        compiler_params=params(10),
         name="first_near",
     )(meta, trips, ids, places, light, *own, *other)
     first_near, far_parts = lax.optimization_barrier((first_near, far_parts))
@@ -436,7 +437,7 @@
             pltpu.VMEM((SLOTS, QR, T), BF16),
             pltpu.SemaphoreType.DMA((len(held) + 4,)),
         ],
-        compiler_params=params(24),
+        compiler_params=params(10),
         name="first",
     )(meta, trips, ids, places, hplaces, light, arrived, first_near, *held)
 
@@ -475,7 +476,7 @@
             out_shape=(half_values, half_values),
             in_specs=[VMEM] * (len(parts) + 3),
             out_specs=(VMEM, VMEM),
-            compiler_params=params(24),
+            compiler_params=params(12),
             name="project",
         )(*parts, w_in, b_in, w_mid)
 
@@ -501,7 +502,7 @@
             pltpu.SemaphoreType.DMA((12,)),
             pltpu.SemaphoreType.DMA((NEAR_STEPS,)),
         ],
-        compiler_params=params(24),
+        compiler_params=params(16),
         name="second_near",
     )(meta, trips, need, ids, places, light, *mine, *swapped)
     far, second_near = lax.optimization_barrier((far, second_near))
@@ -521,7 +522,7 @@
             pltpu.VMEM((SLOTS, T, T), BF16),
             pltpu.SemaphoreType.DMA((26,)),
         ],
-        compiler_params=params(24),
+        compiler_params=params(16),
         name="second",
     )(
         meta, trips, htrips, ids, places, hids, hlist, light, arrived, hc, hy, hyc, second_near,

time: 154 us -> 153 us (level)
    unnamed x34 -> x26, local copies, waits for them, and re-layouts: 3.73 us -> 1.64 us
  transfers between devices with their start and end apart: 25 -> 25, of which waited for: 12 -> 12; matrix products, arithmetic and copies ran while one was open for 1% -> 2% of each run, Pallas kernels for 16% -> 16%
where the time goes in v4:
time: 153 us
  waiting for transfers between devices  56 us (37%)
  starting transfers between devices  54.1 us (35%)
  Pallas kernels  36.2 us (24%)
  local copies, waits for them, and re-layouts  4.75 us (3%)
    ppermute x14, starting transfers between devices, swap(): return lax.ppermute(x, axis, around(axis, 1))  16.5 us
    ppermute x1, waiting for transfers between devices, along_x(): ahead = lax.ppermute(near, 'x', around('x', -1))  15.3 us
    all_to_all x1, waiting for transfers between devices, per_device(): lax.all_to_all(aggregated, (*PLANE, 'yl'), 0, 0, tiled=True)  13 us
    all_to_all x1, starting transfers between devices, everyone(): return lax.all_to_all(spread, axis, 0, 0, tiled=True)  11.7 us
    all_to_all x1, starting transfers between devices, per_device(): lax.all_to_all(aggregated, (*PLANE, 'yl'), 0, 0, tiled=True)  9.59 us
    all_to_all x1, starting transfers between devices, per_device(): arrived = lax.all_to_all(packed, GROUP, 0, 0, tiled=True)  9.33 us
    ppermute x1, waiting for transfers between devices, per_device(): ahead = lax.ppermute(rows, 'x', around('x', -1))  7.65 us
    all_to_all x1, waiting for transfers between devices, everyone(): return lax.all_to_all(spread, axis, 0, 0, tiled=True)  7.35 us
  transfers between devices with their start and end apart: 25, of which 12 were waited for; matrix products, arithmetic and copies ran while one was open for 2% of the time, Pallas kernels for 16%

profile of v4, /device:TPU:1, one launch (start us, length us, event | category | flops | bytes accessed | tf_op | source)
XLA Modules:
  0.0 152.7 jit_solution(1086041964016739104)
XLA Ops:
  1.8 11.7 %all-to-all-start.1 = ((bf16[16,128,128]{2,1,0:T(8,128)(2,1)}), bf16[16,128,128]{2,1,0:T(8,128)(2,1)S(1)}, u32[]{:S(2)}, u32[]{:S(2)}) async-start(bf16[16,128,128]{2,1,0:T(8,128)(2,1)} %broadcast_in_dim.18), calls=%async_computation.1 | async-start | bytes 1048576 | tf_op jit(solution)/shard_map/all_to_all | solution.py:83
  14.3 7.1 %pack.1 = (bf16[64,72,128]{2,1,0:T(8,128)(2,1)}, s32[2,304]{1,0:T(2,128)S(1)}, s32[2,304]{1,0:T(2,128)S(1)}, s32[14]{0:T(128)S(1)}, s32[2]{0:T(128)S(1)}) custom-call(s32[4]{0:T(128)S(1)} %pad_add_fusion.meta, s32[1,8,8]{2,1,0:T(8,128)S(1)} %copy-done.2, s32[1,8,8]{2,1,0:T(8,128)S(1)} %copy-done.3, s32[1,8,36]{2,1,0:T(8,128)S(1)} %copy-done.4, ...), custom_call_target="tpu_custom_call" | custom-call | bytes 30000000 | tf_op jit(solution)/shard_map/pack/pallas_call | solution.py:386
  21.4 7.3 %all-to-all-done.1.rest_0_ = bf16[16,128,128]{2,1,0:T(8,128)(2,1)S(1)} async-done(((bf16[16,128,128]{2,1,0:T(8,128)(2,1)}), bf16[16,128,128]{2,1,0:T(8,128)(2,1)S(1)}, u32[]{:S(2)}, u32[]{:S(2)}) %all-to-all-start.1) | async-done | bytes 524320 | tf_op jit(solution)/shard_map/all_to_all | solution.py:83
  28.8 9.3 %all-to-all-start = ((bf16[64,72,128]{2,1,0:T(8,128)(2,1)}), bf16[64,72,128]{2,1,0:T(8,128)(2,1)S(1)}, u32[]{:S(2)}, u32[]{:S(2)}) async-start(bf16[64,72,128]{2,1,0:T(8,128)(2,1)} %get-tuple-element.45), calls=%async_computation | async-start | bytes 2359296 | tf_op jit(solution)/shard_map/all_to_all | solution.py:403
  38.1 2.5 %collective-permute-start.1 = (bf16[16,128,128]{2,1,0:T(8,128)(2,1)S(1)}, bf16[16,128,128]{2,1,0:T(8,128)(2,1)S(1)}, u32[]{:S(2)}, u32[]{:S(2)}) collective-permute-start(bf16[16,128,128]{2,1,0:T(8,128)(2,1)S(1)} %all-to-all-done.1.rest_0_), channel_id=1, source_target_pairs={{0,192},{64,0},{128,64},{192,128},{1,193},{65,1},{129,65},{193,129... | collective-permute-start | bytes 1572872 | tf_op jit(solution)/shard_map/ppermute | solution.py:66
  40.6 2.1 %collective-permute-start.2 = (bf16[16,128,128]{2,1,0:T(8,128)(2,1)S(1)}, bf16[16,128,128]{2,1,0:T(8,128)(2,1)S(1)}, u32[]{:S(2)}, u32[]{:S(2)}) collective-permute-start(bf16[16,128,128]{2,1,0:T(8,128)(2,1)S(1)} %all-to-all-done.1.rest_0_), channel_id=1, source_target_pairs={{0,1},{1,0},{2,3},{3,2},{4,5},{5,4},{6,7},{7,6},{8,9},{9,8},{10,11... | collective-permute-start | bytes 1572872 | tf_op jit(solution)/shard_map/ppermute | solution.py:78
  42.7 15.3 %collective-permute-done.1.rest_2_ = bf16[16,128,128]{2,1,0:T(8,128)(2,1)S(1)} collective-permute-done((bf16[16,128,128]{2,1,0:T(8,128)(2,1)S(1)}, bf16[16,128,128]{2,1,0:T(8,128)(2,1)S(1)}, u32[]{:S(2)}, u32[]{:S(2)}) %collective-permute-start.1) | collective-permute-done | bytes 524320 | tf_op jit(solution)/shard_map/ppermute | solution.py:66
  57.9 4.0 %collective-permute-start.4 = (bf16[16,128,128]{2,1,0:T(8,128)(2,1)S(1)}, bf16[16,128,128]{2,1,0:T(8,128)(2,1)}, u32[]{:S(2)}, u32[]{:S(2)}) collective-permute-start(bf16[16,128,128]{2,1,0:T(8,128)(2,1)S(1)} %collective-permute-done.1.rest_2_), channel_id=1, source_target_pairs={{0,1},{1,0},{2,3},{3,2},{4,5},{5,4},{6,7},{7,6},{8,9},{9,8},{10,11... | collective-permute-start | bytes 1572872 | tf_op jit(solution)/shard_map/ppermute | solution.py:78
  61.9 2.3 %collective-permute-done.rest_1_ = bf16[16,128,128]{2,1,0:T(8,128)(2,1)S(1)} collective-permute-done((bf16[16,128,128]{2,1,0:T(8,128)(2,1)S(1)}, bf16[16,128,128]{2,1,0:T(8,128)(2,1)S(1)}, u32[]{:S(2)}, u32[]{:S(2)}) %collective-permute-start) | collective-permute-done | bytes 524320 | tf_op jit(solution)/shard_map/ppermute | solution.py:65
  64.2 2.5 %collective-permute-start.3 = (bf16[16,128,128]{2,1,0:T(8,128)(2,1)S(1)}, bf16[16,128,128]{2,1,0:T(8,128)(2,1)}, u32[]{:S(2)}, u32[]{:S(2)}) collective-permute-start(bf16[16,128,128]{2,1,0:T(8,128)(2,1)S(1)} %collective-permute-done.rest_1_), channel_id=1, source_target_pairs={{0,1},{1,0},{2,3},{3,2},{4,5},{5,4},{6,7},{7,6},{8,9},{9,8},{10,11... | collective-permute-start | bytes 1572872 | tf_op jit(solution)/shard_map/ppermute | solution.py:78
  68.1 1.5 collective-permute-start.5
  70.0 4.7 %first_near.1.near = f32[2,32,128]{2,1,0:T(8,128)S(1)} custom-call(s32[4]{0:T(128)S(1)} %pad_add_fusion.meta, s32[2]{0:T(128)S(1)} %get-tuple-element.46.trips, s32[2,304]{1,0:T(2,128)S(1)} %get-tuple-element.47.ids, s32[2,304]{1,0:T(2,128)S(1)} %get-tuple-element.48.places, bf16[288,128,128]{2,1,0:T(8,128)(2,1)} %bitcast.34, ...), custom_call_target="tpu_custom_call" | custom-call | tf_op jit(solution)/shard_map/first_near/pallas_call | solution.py:414
  75.7 1.9 %collective-permute-done.5.rest_3_ = bf16[8,128,128]{2,1,0:T(8,128)(2,1)} collective-permute-done((bf16[8,128,128]{2,1,0:T(8,128)(2,1)}, bf16[8,128,128]{2,1,0:T(8,128)(2,1)}, u32[]{:S(2)}, u32[]{:S(2)}) %collective-permute-start.5) | collective-permute-done | bytes 262176 | tf_op jit(solution)/shard_map/ppermute | solution.py:72
  78.4 1.3 collective-permute-done.7.rest_8_
  80.1 4.5 %first.1 = bf16[32,2,32,128]{3,2,1,0:T(8,128)(2,1)S(1)} custom-call(s32[4]{0:T(128)S(1)} %pad_add_fusion.meta, s32[2]{0:T(128)S(1)} %get-tuple-element.46.trips, s32[2,304]{1,0:T(2,128)S(1)} %get-tuple-element.47.ids, s32[2,304]{1,0:T(2,128)S(1)} %get-tuple-element.48.places, s32[128]{0:T(128)S(1)} %reshape.116.hplaces, bf16[288,128,128]{2,1,0:T(8,128)(2,1)} %bitcast.35, ...), custom_call_target="tpu_custom_call" | custom-call | tf_op jit(solution)/shard_map/first/pallas_call | solution.py:429
  86.0 9.6 %all-to-all-start.2 = ((bf16[32,2,32,128]{3,2,1,0:T(8,128)(2,1)}), bf16[32,2,32,128]{3,2,1,0:T(8,128)(2,1)S(1)}, u32[]{:S(2)}, u32[]{:S(2)}) async-start(bf16[32,2,32,128]{3,2,1,0:T(8,128)(2,1)} %copy-done.1), calls=%async_computation.2 | async-start | bytes 1048576 | tf_op jit(solution)/shard_map/all_to_all | solution.py:456
  95.6 1.0 collective-permute-start.11
  96.8 2.2 %compact.1 = (s32[288]{0:T(512)}, s32[288]{0:T(512)}, s32[1]{0:T(128)}) custom-call(s32[128]{0:T(128)} %copy-done.9), custom_call_target="tpu_custom_call" | custom-call | tf_op jit(solution)/shard_map/compact/pallas_call | solution.py:458
  99.8 13.0 %all-to-all-done.2 = bf16[32,2,32,128]{3,2,1,0:T(8,128)(2,1)S(1)} async-done(((bf16[32,2,32,128]{3,2,1,0:T(8,128)(2,1)}), bf16[32,2,32,128]{3,2,1,0:T(8,128)(2,1)S(1)}, u32[]{:S(2)}, u32[]{:S(2)}) %all-to-all-start.2) | async-done | bytes 524320 | tf_op jit(solution)/shard_map/all_to_all | solution.py:456
  112.7 1.5 collective-permute-start.14
  114.2 1.4 project.3
  115.6 7.7 %collective-permute-done.15.refs_1_ = bf16[16,2,2,32,128]{4,3,2,1,0:T(8,128)(2,1)S(1)} collective-permute-done((bf16[16,2,2,32,128]{4,3,2,1,0:T(8,128)(2,1)S(1)}, bf16[16,2,2,32,128]{4,3,2,1,0:T(8,128)(2,1)S(1)}, u32[]{:S(2)}, u32[]{:S(2)}) %collective-permute-start.15) | collective-permute-done | bytes 524320 | tf_op jit(solution)/shard_map/ppermute | solution.py:484
  123.2 1.2 collective-permute-done.14.refs_0_
  124.4 2.4 %project.4 = (bf16[2,32,2,32,128]{4,3,2,1,0:T(8,128)(2,1)S(1)}, bf16[2,32,2,32,128]{4,3,2,1,0:T(8,128)(2,1)S(1)}) custom-call(bf16[16,2,2,32,128]{4,3,2,1,0:T(8,128)(2,1)S(1)} %collective-permute-done.14.refs_0_, bf16[16,2,2,32,128]{4,3,2,1,0:T(8,128)(2,1)S(1)} %collective-permute-done.15.refs_1_, bf16[128,512]{1,0:T(8,128)(2,1)S(1)} %copy_bitcast_fusion.refs_1_.refs_2_, ...), custom_call_target="tpu_custom_call" | custom-call | tf_op jit(solution)/shard_map/project/pallas_call | solution.py:474
  126.9 3.9 %collective-permute-start.19 = (bf16[2,32,2,32,128]{4,3,2,1,0:T(8,128)(2,1)S(1)}, bf16[2,32,2,32,128]{4,3,2,1,0:T(8,128)(2,1)S(1)}, u32[]{:S(2)}, u32[]{:S(2)}) collective-permute-start(bf16[2,32,2,32,128]{4,3,2,1,0:T(8,128)(2,1)S(1)} %get-tuple-element.76), channel_id=1, source_target_pairs={{0,1},{1,0},{2,3},{3,2},{4,5},{5,4},{6,7},{7,6},{8,9},{9,8},{10,11... | collective-permute-start | bytes 3145736 | tf_op jit(solution)/shard_map/ppermute | solution.py:78
  131.1 1.5 collective-permute-start.16
  132.5 1.3 collective-permute-done.18.rest_2_.rest_3_
  134.3 5.8 %second_near.1.near = f32[2,128,128]{2,1,0:T(8,128)S(1)} custom-call(s32[4]{0:T(128)S(1)} %pad_add_fusion.meta, s32[2]{0:T(128)S(1)} %get-tuple-element.46.trips, s32[14]{0:T(128)S(1)} %get-tuple-element.72.need, s32[2,304]{1,0:T(2,128)S(1)} %get-tuple-element.47.ids, s32[2,304]{1,0:T(2,128)S(1)} %get-tuple-element.48.places, ...), custom_call_target="tpu_custom_call" | custom-call | tf_op jit(solution)/shard_map/second_near/pallas_call | solution.py:494
  140.1 1.4 project.5
  141.5 1.1 collective-permute-start.20
  142.7 3.2 %collective-permute-done.21.rest_5_ = bf16[2,16,2,32,128]{4,3,2,1,0:T(8,128)(2,1)S(1)} collective-permute-done((bf16[2,16,2,32,128]{4,3,2,1,0:T(8,128)(2,1)S(1)}, bf16[2,16,2,32,128]{4,3,2,1,0:T(8,128)(2,1)S(1)}, u32[]{:S(2)}, u32[]{:S(2)}) %collective-permute-start.21) | collective-permute-done | bytes 524320 | tf_op jit(solution)/shard_map/ppermute | solution.py:78
  145.8 6.7 %second.1 = bf16[256,128]{1,0:T(8,128)(2,1)} custom-call(s32[4]{0:T(128)S(1)} %pad_add_fusion.meta, s32[2]{0:T(128)S(1)} %get-tuple-element.46.trips, s32[1]{0:T(128)} %get-tuple-element.60.htrips, s32[2,304]{1,0:T(2,128)S(1)} %get-tuple-element.47.ids, s32[2,304]{1,0:T(2,128)S(1)} %get-tuple-element.48.places, s32[288]{0:T(512)S(1)} %copy-done.6, ...), custom_call_target="tpu_custom_call" | custom-call | tf_op jit(solution)/shard_map/second/pallas_call | solution.py:514
  (75 shorter events, 8.6 us)
Async XLA Ops:
  0.0 14.2 %copy-start.3 = (s32[1,8,8]{2,1,0:T(8,128)S(1)}, s32[1,8,8]{2,1,0:T(8,128)}, u32[]{:S(2)}) copy-start(s32[1,8,8]{2,1,0:T(8,128)} %cols.1) | copy-start | bytes 772
  0.0 14.3 %copy-start.2 = (s32[1,8,8]{2,1,0:T(8,128)S(1)}, s32[1,8,8]{2,1,0:T(8,128)}, u32[]{:S(2)}) copy-start(s32[1,8,8]{2,1,0:T(8,128)} %slots.1) | copy-start | bytes 772
  0.0 14.2 %copy-start.5 = (s32[1,8,36]{2,1,0:T(8,128)S(1)}, s32[1,8,36]{2,1,0:T(8,128)}, u32[]{:S(2)}) copy-start(s32[1,8,36]{2,1,0:T(8,128)} %lcols.1) | copy-start | bytes 3460
  0.0 14.2 %copy-start.4 = (s32[1,8,36]{2,1,0:T(8,128)S(1)}, s32[1,8,36]{2,1,0:T(8,128)}, u32[]{:S(2)}) copy-start(s32[1,8,36]{2,1,0:T(8,128)} %rows.1) | copy-start | bytes 3460
  1.8 27.0 %all-to-all-start.1 = ((bf16[16,128,128]{2,1,0:T(8,128)(2,1)}), bf16[16,128,128]{2,1,0:T(8,128)(2,1)S(1)}, u32[]{:S(2)}, u32[]{:S(2)}) async-start(bf16[16,128,128]{2,1,0:T(8,128)(2,1)} %broadcast_in_dim.18), calls=%async_computation.1 | async-start | bytes 1048576 | tf_op jit(solution)/shard_map/all_to_all | solution.py:83
  28.8 40.8 %all-to-all-start = ((bf16[64,72,128]{2,1,0:T(8,128)(2,1)}), bf16[64,72,128]{2,1,0:T(8,128)(2,1)S(1)}, u32[]{:S(2)}, u32[]{:S(2)}) async-start(bf16[64,72,128]{2,1,0:T(8,128)(2,1)} %get-tuple-element.45), calls=%async_computation | async-start | bytes 2359296 | tf_op jit(solution)/shard_map/all_to_all | solution.py:403
  38.1 19.8 %collective-permute-start.1 = (bf16[16,128,128]{2,1,0:T(8,128)(2,1)S(1)}, bf16[16,128,128]{2,1,0:T(8,128)(2,1)S(1)}, u32[]{:S(2)}, u32[]{:S(2)}) collective-permute-start(bf16[16,128,128]{2,1,0:T(8,128)(2,1)S(1)} %all-to-all-done.1.rest_0_), channel_id=1, source_target_pairs={{0,192},{64,0},{128,64},{192,128},{1,193},{65,1},{129,65},{193,129... | collective-permute-start | bytes 1572872 | tf_op jit(solution)/shard_map/ppermute | solution.py:66
  40.6 23.6 %collective-permute-start = (bf16[16,128,128]{2,1,0:T(8,128)(2,1)S(1)}, bf16[16,128,128]{2,1,0:T(8,128)(2,1)S(1)}, u32[]{:S(2)}, u32[]{:S(2)}) collective-permute-start(bf16[16,128,128]{2,1,0:T(8,128)(2,1)S(1)} %all-to-all-done.1.rest_0_), channel_id=1, source_target_pairs={{0,64},{64,128},{128,192},{192,0},{1,65},{65,129},{129,193},{193,1... | collective-permute-start | bytes 1572872 | tf_op jit(solution)/shard_map/ppermute | solution.py:65
  40.6 29.3 %collective-permute-start.2 = (bf16[16,128,128]{2,1,0:T(8,128)(2,1)S(1)}, bf16[16,128,128]{2,1,0:T(8,128)(2,1)S(1)}, u32[]{:S(2)}, u32[]{:S(2)}) collective-permute-start(bf16[16,128,128]{2,1,0:T(8,128)(2,1)S(1)} %all-to-all-done.1.rest_0_), channel_id=1, source_target_pairs={{0,1},{1,0},{2,3},{3,2},{4,5},{5,4},{6,7},{7,6},{8,9},{9,8},{10,11... | collective-permute-start | bytes 1572872 | tf_op jit(solution)/shard_map/ppermute | solution.py:78
  57.9 12.0 %collective-permute-start.4 = (bf16[16,128,128]{2,1,0:T(8,128)(2,1)S(1)}, bf16[16,128,128]{2,1,0:T(8,128)(2,1)}, u32[]{:S(2)}, u32[]{:S(2)}) collective-permute-start(bf16[16,128,128]{2,1,0:T(8,128)(2,1)S(1)} %collective-permute-done.1.rest_2_), channel_id=1, source_target_pairs={{0,1},{1,0},{2,3},{3,2},{4,5},{5,4},{6,7},{7,6},{8,9},{9,8},{10,11... | collective-permute-start | bytes 1572872 | tf_op jit(solution)/shard_map/ppermute | solution.py:78
  64.2 5.7 %collective-permute-start.3 = (bf16[16,128,128]{2,1,0:T(8,128)(2,1)S(1)}, bf16[16,128,128]{2,1,0:T(8,128)(2,1)}, u32[]{:S(2)}, u32[]{:S(2)}) collective-permute-start(bf16[16,128,128]{2,1,0:T(8,128)(2,1)S(1)} %collective-permute-done.rest_1_), channel_id=1, source_target_pairs={{0,1},{1,0},{2,3},{3,2},{4,5},{5,4},{6,7},{7,6},{8,9},{9,8},{10,11... | collective-permute-start | bytes 1572872 | tf_op jit(solution)/shard_map/ppermute | solution.py:78
  67.4 8.3 %collective-permute-start.6 = (bf16[8,128,128]{2,1,0:T(8,128)(2,1)}, bf16[8,128,128]{2,1,0:T(8,128)(2,1)}, u32[]{:S(2)}, u32[]{:S(2)}) collective-permute-start(bf16[8,128,128]{2,1,0:T(8,128)(2,1)} %slice.33), channel_id=1, source_target_pairs={{0,192},{64,0},{128,64},{192,128},{1,193},{65,1},{129,65},{193,129... | collective-permute-start | bytes 786440 | tf_op jit(solution)/shard_map/ppermute | solution.py:73
  68.1 9.5 %collective-permute-start.5 = (bf16[8,128,128]{2,1,0:T(8,128)(2,1)}, bf16[8,128,128]{2,1,0:T(8,128)(2,1)}, u32[]{:S(2)}, u32[]{:S(2)}) collective-permute-start(bf16[8,128,128]{2,1,0:T(8,128)(2,1)} %slice.32), channel_id=1, source_target_pairs={{0,64},{64,128},{128,192},{192,0},{1,65},{65,129},{129,193},{193,1... | collective-permute-start | bytes 786440 | tf_op jit(solution)/shard_map/ppermute | solution.py:72
  77.6 2.2 %collective-permute-start.7 = (bf16[8,128,128]{2,1,0:T(8,128)(2,1)}, bf16[8,128,128]{2,1,0:T(8,128)(2,1)S(1)}, u32[]{:S(2)}, u32[]{:S(2)}) collective-permute-start(bf16[8,128,128]{2,1,0:T(8,128)(2,1)} %collective-permute-done.5.rest_3_), channel_id=1, source_target_pairs={{0,1},{1,0},{2,3},{3,2},{4,5},{5,4},{6,7},{7,6},{8,9},{9,8},{10,11... | collective-permute-start | bytes 786440 | tf_op jit(solution)/shard_map/ppermute | solution.py:78
  78.4 1.7 %collective-permute-start.8 = (bf16[8,128,128]{2,1,0:T(8,128)(2,1)}, bf16[8,128,128]{2,1,0:T(8,128)(2,1)S(1)}, u32[]{:S(2)}, u32[]{:S(2)}) collective-permute-start(bf16[8,128,128]{2,1,0:T(8,128)(2,1)} %collective-permute-done.6.rest_4_), channel_id=1, source_target_pairs={{0,1},{1,0},{2,3},{3,2},{4,5},{5,4},{6,7},{7,6},{8,9},{9,8},{10,11... | collective-permute-start | bytes 786440 | tf_op jit(solution)/shard_map/ppermute | solution.py:78
  85.5 11.1 %collective-permute-start.9 = (f32[136,128]{1,0:T(8,128)S(1)}, f32[136,128]{1,0:T(8,128)S(1)}, u32[]{:S(2)}, u32[]{:S(2)}) collective-permute-start(f32[136,128]{1,0:T(8,128)S(1)} %get-tuple-element.86), channel_id=1, source_target_pairs={{0,2},{2,0},{1,3},{3,1},{4,6},{6,4},{5,7},{7,5},{8,10},{10,8},{9,1... | collective-permute-start | bytes 208904 | tf_op jit(solution)/shard_map/ppermute | solution.py:78
  86.0 26.7 %all-to-all-start.2 = ((bf16[32,2,32,128]{3,2,1,0:T(8,128)(2,1)}), bf16[32,2,32,128]{3,2,1,0:T(8,128)(2,1)S(1)}, u32[]{:S(2)}, u32[]{:S(2)}) async-start(bf16[32,2,32,128]{3,2,1,0:T(8,128)(2,1)} %copy-done.1), calls=%async_computation.2 | async-start | bytes 1048576 | tf_op jit(solution)/shard_map/all_to_all | solution.py:456
  95.6 3.3 %collective-permute-start.11 = (bf16[512,128]{1,0:T(8,128)(2,1)S(1)}, bf16[512,128]{1,0:T(8,128)(2,1)S(1)}, u32[]{:S(2)}, u32[]{:S(2)}) collective-permute-start(bf16[512,128]{1,0:T(8,128)(2,1)S(1)} %copy-done.10), channel_id=1, source_target_pairs={{0,1},{1,0},{2,3},{3,2},{4,5},{5,4},{6,7},{7,6},{8,9},{9,8},{10,11... | collective-permute-start | bytes 393224 | tf_op jit(solution)/shard_map/ppermute | solution.py:78
  96.7 2.3 %collective-permute-start.10 = (f32[2,136,128]{2,1,0:T(8,128)S(1)}, f32[2,136,128]{2,1,0:T(8,128)S(1)}, u32[]{:S(2)}, u32[]{:S(2)}) collective-permute-start(f32[2,136,128]{2,1,0:T(8,128)S(1)} %get-tuple-element.84), channel_id=1, source_target_pairs={{0,1},{1,0},{2,3},{3,2},{4,5},{5,4},{6,7},{7,6},{8,9},{9,8},{10,11... | collective-permute-start | bytes 417800 | tf_op jit(solution)/shard_map/ppermute | solution.py:78
  112.7 10.5 %collective-permute-start.15 = (bf16[16,2,2,32,128]{4,3,2,1,0:T(8,128)(2,1)S(1)}, bf16[16,2,2,32,128]{4,3,2,1,0:T(8,128)(2,1)S(1)}, u32[]{:S(2)}, u32[]{:S(2)}) collective-permute-start(bf16[16,2,2,32,128]{4,3,2,1,0:T(8,128)(2,1)S(1)} %bitcast.30), channel_id=1, source_target_pairs={{0,192},{64,0},{128,64},{192,128},{1,193},{65,1},{129,65},{193,129... | collective-permute-start | bytes 1572872 | tf_op jit(solution)/shard_map/ppermute | solution.py:484
  112.7 11.7 %collective-permute-start.14 = (bf16[16,2,2,32,128]{4,3,2,1,0:T(8,128)(2,1)S(1)}, bf16[16,2,2,32,128]{4,3,2,1,0:T(8,128)(2,1)S(1)}, u32[]{:S(2)}, u32[]{:S(2)}) collective-permute-start(bf16[16,2,2,32,128]{4,3,2,1,0:T(8,128)(2,1)S(1)} %bitcast.31), channel_id=1, source_target_pairs={{0,64},{64,128},{128,192},{192,0},{1,65},{65,129},{129,193},{193,1... | collective-permute-start | bytes 1572872 | tf_op jit(solution)/shard_map/ppermute | solution.py:483
  114.2 27.3 %collective-permute-start.13 = (bf16[64,72,128]{2,1,0:T(8,128)(2,1)S(1)}, bf16[64,72,128]{2,1,0:T(8,128)(2,1)S(1)}, u32[]{:S(2)}, u32[]{:S(2)}) collective-permute-start(bf16[64,72,128]{2,1,0:T(8,128)(2,1)S(1)} %all-to-all-done.heavy.h0), channel_id=1, source_target_pairs={{0,2},{2,0},{1,3},{3,1},{4,6},{6,4},{5,7},{7,5},{8,10},{10,8},{9,1... | collective-permute-start | bytes 3538952 | tf_op jit(solution)/shard_map/ppermute | solution.py:78
  126.9 7.4 %collective-permute-start.19 = (bf16[2,32,2,32,128]{4,3,2,1,0:T(8,128)(2,1)S(1)}, bf16[2,32,2,32,128]{4,3,2,1,0:T(8,128)(2,1)S(1)}, u32[]{:S(2)}, u32[]{:S(2)}) collective-permute-start(bf16[2,32,2,32,128]{4,3,2,1,0:T(8,128)(2,1)S(1)} %get-tuple-element.76), channel_id=1, source_target_pairs={{0,1},{1,0},{2,3},{3,2},{4,5},{5,4},{6,7},{7,6},{8,9},{9,8},{10,11... | collective-permute-start | bytes 3145736 | tf_op jit(solution)/shard_map/ppermute | solution.py:78
  130.8 3.0 %collective-permute-start.18 = (bf16[2,16,2,32,128]{4,3,2,1,0:T(8,128)(2,1)S(1)}, bf16[2,16,2,32,128]{4,3,2,1,0:T(8,128)(2,1)S(1)}, u32[]{:S(2)}, u32[]{:S(2)}) collective-permute-start(bf16[2,16,2,32,128]{4,3,2,1,0:T(8,128)(2,1)S(1)} %get-tuple-element.75), channel_id=1, source_target_pairs={{0,1},{1,0},{2,3},{3,2},{4,5},{5,4},{6,7},{7,6},{8,9},{9,8},{10,11... | collective-permute-start | bytes 1572872 | tf_op jit(solution)/shard_map/ppermute | solution.py:78
  131.0 9.1 %collective-permute-start.17 = (bf16[8,2,2,32,128]{4,3,2,1,0:T(8,128)(2,1)S(1)}, bf16[8,2,2,32,128]{4,3,2,1,0:T(8,128)(2,1)S(1)}, u32[]{:S(2)}, u32[]{:S(2)}) collective-permute-start(bf16[8,2,2,32,128]{4,3,2,1,0:T(8,128)(2,1)S(1)} %slice.28), channel_id=1, source_target_pairs={{0,192},{64,0},{128,64},{192,128},{1,193},{65,1},{129,65},{193,129... | collective-permute-start | bytes 786440 | tf_op jit(solution)/shard_map/ppermute | solution.py:489
  131.1 9.0 %collective-permute-start.16 = (bf16[8,2,2,32,128]{4,3,2,1,0:T(8,128)(2,1)S(1)}, bf16[8,2,2,32,128]{4,3,2,1,0:T(8,128)(2,1)S(1)}, u32[]{:S(2)}, u32[]{:S(2)}) collective-permute-start(bf16[8,2,2,32,128]{4,3,2,1,0:T(8,128)(2,1)S(1)} %slice.27), channel_id=1, source_target_pairs={{0,64},{64,128},{128,192},{192,0},{1,65},{65,129},{129,193},{193,1... | collective-permute-start | bytes 786440 | tf_op jit(solution)/shard_map/ppermute | solution.py:488
  133.9 8.8 %collective-permute-start.12 = (bf16[64,72,128]{2,1,0:T(8,128)(2,1)S(1)}, bf16[64,72,128]{2,1,0:T(8,128)(2,1)S(1)}, u32[]{:S(2)}, u32[]{:S(2)}) collective-permute-start(bf16[64,72,128]{2,1,0:T(8,128)(2,1)S(1)} %all-to-all-done.heavy.h0), channel_id=1, source_target_pairs={{0,1},{1,0},{2,3},{3,2},{4,5},{5,4},{6,7},{7,6},{8,9},{9,8},{10,11... | collective-permute-start | bytes 3538952 | tf_op jit(solution)/shard_map/ppermute | solution.py:78
  134.2 11.6 %copy-start.6 = (s32[288]{0:T(512)S(1)}, s32[288]{0:T(512)}, u32[]{:S(2)}) copy-start(s32[288]{0:T(512)} %get-tuple-element.61.hids) | copy-start | bytes 3460
  134.3 11.6 %copy-start.7 = (s32[288]{0:T(512)S(1)}, s32[288]{0:T(512)}, u32[]{:S(2)}) copy-start(s32[288]{0:T(512)} %get-tuple-element.62.hplaces) | copy-start | bytes 3460
  134.3 11.6 %copy-start.8 = (f32[128]{0:T(128)S(1)}, f32[128]{0:T(128)}, u32[]{:S(2)}) copy-start(f32[128]{0:T(128)} %param.16) | copy-start | bytes 1540
  141.5 4.3 %collective-permute-start.20 = (bf16[64,72,128]{2,1,0:T(8,128)(2,1)S(1)}, bf16[64,72,128]{2,1,0:T(8,128)(2,1)S(1)}, u32[]{:S(2)}, u32[]{:S(2)}) collective-permute-start(bf16[64,72,128]{2,1,0:T(8,128)(2,1)S(1)} %collective-permute-done.13.h2), channel_id=1, source_target_pairs={{0,1},{1,0},{2,3},{3,2},{4,5},{5,4},{6,7},{7,6},{8,9},{9,8},{10,11... | collective-permute-start | bytes 3538952 | tf_op jit(solution)/shard_map/ppermute | solution.py:78
  142.6 3.2 %collective-permute-start.21 = (bf16[2,16,2,32,128]{4,3,2,1,0:T(8,128)(2,1)S(1)}, bf16[2,16,2,32,128]{4,3,2,1,0:T(8,128)(2,1)S(1)}, u32[]{:S(2)}, u32[]{:S(2)}) collective-permute-start(bf16[2,16,2,32,128]{4,3,2,1,0:T(8,128)(2,1)S(1)} %get-tuple-element.80), channel_id=1, source_target_pairs={{0,1},{1,0},{2,3},{3,2},{4,5},{5,4},{6,7},{7,6},{8,9},{9,8},{10,11... | collective-permute-start | bytes 1572872 | tf_op jit(solution)/shard_map/ppermute | solution.py:78
  (6 other events, 36.2 us)

commit v5 on v4

--- a/solution.py
+++ b/solution.py
@@ -260,23 +260,28 @@
     hsum = lax.fori_loop(0, SLOTS // HSTEP, heavy_body, jnp.zeros((QR, T), jnp.float32))
     for t in range(2):
         total = (sums[t] + jnp.where(owner == t, hsum, 0.0)).astype(BF16)
-        for n in range(2 * NPLANE):
+        for n in range(2 * NR):
             out[n, t] = total
 
 
-def project_kernel(n, *refs):
+def project_kernel(across, n, meta, *refs):
     parts, (w_in, b_in, w_mid, mine, theirs) = refs[:n], refs[n:]
+    y = meta[0] & 1
     at = 0
-    for part in parts:
+    for part, first in zip(parts, across):
         size = part.shape[0]
-        for rt in range(2):
-            x = part[:, :, rt].reshape(-1, T)
+        for k in range(size):
+            group = pl.ds(at + jnp.bitwise_xor(y, k + first) * NR, NR)
+            x = part[k].reshape(-1, T)
             h = jnp.dot(x, w_in[...], preferred_element_type=jnp.float32) + b_in[...]
             h = jnp.maximum(h, 0.0).astype(BF16)
             s = jnp.dot(h, w_mid[...], preferred_element_type=jnp.float32).astype(BF16)
-            mine[rt, at : at + size] = s[:, :T].reshape(size, *mine.shape[2:])
-            theirs[rt, at : at + size] = s[:, T:].reshape(size, *mine.shape[2:])
-        at += size
+            s = s.reshape(NR, 2, 2, QR, 2 * T)
+            for rt in range(2):
+                mine[rt, group] = s[:, :, rt, :, :T]
+                theirs[rt, group] = s[:, :, rt, :, T:]
+        if size == 2:
+            at += NPLANE
 
 
 def value_copies(meta, held, parts, values, sems):
@@ -428,7 +433,7 @@
     held = own + far_parts + other + [swap(part, "c") for part in far_parts]
     aggregated = pl.pallas_call(
         first_kernel,
-        out_shape=jax.ShapeDtypeStruct((2 * NPLANE, 2, QR, T), BF16),
+        out_shape=jax.ShapeDtypeStruct((2 * NR, 2, QR, T), BF16),
         in_specs=[SMEM] * 5 + [HBM, ANY, VMEM] + [ANY] * len(held),
         out_specs=VMEM,
         scratch_shapes=[
@@ -453,7 +458,8 @@
     b_in = pieces[:, T].reshape(1, 4 * T)
     w_mid = jnp.concatenate([weight_mid, swap(weight_mid, "c")], axis=1)
 
-    rows = lax.all_to_all(aggregated, (*PLANE, "yl"), 0, 0, tiled=True).reshape(NPLANE, 2, 2, QR, T)
+    column = lax.all_to_all(aggregated, ("z", "yl"), 0, 0, tiled=True).reshape(NR, 2, 2, QR, T)
+    rows = jnp.stack([column, swap(column, "yh")])
 
     hids, hlist, htrips = pl.pallas_call(
         compact_kernel,
@@ -468,27 +474,27 @@
     )
     hc = swap(arrived, "c")
     hy = swap(arrived, "yl")
-    def project(*parts):
-        groups = sum(part.shape[0] for part in parts)
+    def project(parts, across):
+        groups = sum(part.shape[0] for part in parts) * NR
         half_values = jax.ShapeDtypeStruct((2, groups, 2, QR, T), BF16)
         return pl.pallas_call(
-            functools.partial(project_kernel, len(parts)),
+            functools.partial(project_kernel, across, len(parts)),
             out_shape=(half_values, half_values),
-            in_specs=[VMEM] * (len(parts) + 3),
+            in_specs=[SMEM] + [VMEM] * (len(parts) + 3),
             out_specs=(VMEM, VMEM),
             compiler_params=params(12),
             name="project",
-        )(*parts, w_in, b_in, w_mid)
+        )(meta, *parts, w_in, b_in, w_mid)
 
     behind = lax.ppermute(rows, "x", around("x", 1))
     ahead = lax.ppermute(rows, "x", around("x", -1))
-    near = project(rows)
+    near = project([rows], (0,))
     behind, ahead, near = lax.optimization_barrier((behind, ahead, near))
     far = [
-        lax.ppermute(behind[:NR], "x", around("x", 1)),
-        lax.ppermute(ahead[NR:], "x", around("x", -1)),
+        lax.ppermute(behind[:1], "x", around("x", 1)),
+        lax.ppermute(ahead[1:], "x", around("x", -1)),
     ]
-    sides = project(behind, ahead)
+    sides = project([behind, ahead], (0, 0))
     mine = [near[0], sides[0]]
     swapped = [swap(near[1], "c"), swap(sides[1], "c")]
     second_near = pl.pallas_call(
@@ -506,7 +512,7 @@
         name="second_near",
     )(meta, trips, need, ids, places, light, *mine, *swapped)
     far, second_near = lax.optimization_barrier((far, second_near))
-    far = project(*far)
+    far = project(far, (0, 1))
     mine.append(far[0])
     swapped.append(swap(far[1], "c"))
     hy_late, _ = lax.optimization_barrier((hy, far))

time: 153 us -> 152 us (level)
  waiting for transfers between devices: 56 us -> 52.7 us
  Pallas kernels: 36.2 us -> 37.8 us
    all_to_all x1, waiting for transfers between devices: 13 us -> 6.4 us  [per_device(): lax.all_to_all(aggregated, ('z', 'yl'), 0, 0, tiled=True)]
    ppermute x14 -> x15, waiting for transfers between devices: 6.25 us -> 10.2 us  [swap(): return lax.ppermute(x, axis, around(axis, 1))]
    ppermute x14 -> x15, starting transfers between devices: 16.5 us -> 19.9 us  [swap(): return lax.ppermute(x, axis, around(axis, 1))]
    all_to_all x1, starting transfers between devices: 9.59 us -> 6.69 us  [per_device(): lax.all_to_all(aggregated, ('z', 'yl'), 0, 0, tiled=True)]
    pallas_call x4, Pallas kernels: 9.7 us -> 11.3 us  [the longest x3 6.78 us: project(): pl.pallas_call(functools.partial(project_kernel, across, len(parts)), out...]
  transfers between devices with their start and end apart: 25 -> 26, of which waited for: 12 -> 13; matrix products, arithmetic and copies ran while one was open for 2% -> 2% of each run, Pallas kernels for 16% -> 18%
where the time goes in v5:
time: 152 us; the launch traced here: 151 us
  starting transfers between devices  54.7 us (36%)
  waiting for transfers between devices  52.7 us (35%)
  Pallas kernels  37.8 us (25%)
  local copies, waits for them, and re-layouts  4.14 us (3%)
    ppermute x15, starting transfers between devices, swap(): return lax.ppermute(x, axis, around(axis, 1))  19.9 us
    ppermute x1, waiting for transfers between devices, along_x(): ahead = lax.ppermute(near, 'x', around('x', -1))  15.3 us
    all_to_all x1, starting transfers between devices, everyone(): return lax.all_to_all(spread, axis, 0, 0, tiled=True)  11.7 us
    ppermute x15, waiting for transfers between devices, swap(): return lax.ppermute(x, axis, around(axis, 1))  10.2 us
    all_to_all x1, starting transfers between devices, per_device(): arrived = lax.all_to_all(packed, GROUP, 0, 0, tiled=True)  9.33 us
    all_to_all x1, waiting for transfers between devices, everyone(): return lax.all_to_all(spread, axis, 0, 0, tiled=True)  7.35 us
    pallas_call x1, Pallas kernels, per_device(): pl.pallas_call(pack_kernel, out_shape=(jax.ShapeDtypeStruct((NG, 2 * QR +...  7.13 us
    ppermute x1, waiting for transfers between devices, per_device(): ahead = lax.ppermute(rows, 'x', around('x', -1))  6.85 us
  transfers between devices with their start and end apart: 26, of which 13 were waited for; matrix products, arithmetic and copies ran while one was open for 2% of the time, Pallas kernels for 18%

profile of v5, /device:TPU:1, one launch (start us, length us, event | category | flops | bytes accessed | tf_op | source)
XLA Modules:
  0.0 151.0 jit_solution(5117105817687057281)
XLA Ops:
  1.8 11.7 %all-to-all-start.1 = ((bf16[16,128,128]{2,1,0:T(8,128)(2,1)}), bf16[16,128,128]{2,1,0:T(8,128)(2,1)S(1)}, u32[]{:S(2)}, u32[]{:S(2)}) async-start(bf16[16,128,128]{2,1,0:T(8,128)(2,1)} %broadcast_in_dim.18), calls=%async_computation.1 | async-start | bytes 1048576 | tf_op jit(solution)/shard_map/all_to_all | solution.py:83
  14.3 7.1 %pack.1 = (bf16[64,72,128]{2,1,0:T(8,128)(2,1)}, s32[2,304]{1,0:T(2,128)S(1)}, s32[2,304]{1,0:T(2,128)S(1)}, s32[14]{0:T(128)S(1)}, s32[2]{0:T(128)S(1)}) custom-call(s32[4]{0:T(128)S(1)} %pad_add_fusion.meta, s32[1,8,8]{2,1,0:T(8,128)S(1)} %copy-done.2, s32[1,8,8]{2,1,0:T(8,128)S(1)} %copy-done.3, s32[1,8,36]{2,1,0:T(8,128)S(1)} %copy-done.4, ...), custom_call_target="tpu_custom_call" | custom-call | bytes 30000000 | tf_op jit(solution)/shard_map/pack/pallas_call | solution.py:391
  21.4 7.4 %all-to-all-done.1.rest_0_ = bf16[16,128,128]{2,1,0:T(8,128)(2,1)S(1)} async-done(((bf16[16,128,128]{2,1,0:T(8,128)(2,1)}), bf16[16,128,128]{2,1,0:T(8,128)(2,1)S(1)}, u32[]{:S(2)}, u32[]{:S(2)}) %all-to-all-start.1) | async-done | bytes 524320 | tf_op jit(solution)/shard_map/all_to_all | solution.py:83
  28.8 9.3 %all-to-all-start = ((bf16[64,72,128]{2,1,0:T(8,128)(2,1)}), bf16[64,72,128]{2,1,0:T(8,128)(2,1)S(1)}, u32[]{:S(2)}, u32[]{:S(2)}) async-start(bf16[64,72,128]{2,1,0:T(8,128)(2,1)} %get-tuple-element.45), calls=%async_computation | async-start | bytes 2359296 | tf_op jit(solution)/shard_map/all_to_all | solution.py:408
  38.1 2.5 %collective-permute-start.1 = (bf16[16,128,128]{2,1,0:T(8,128)(2,1)S(1)}, bf16[16,128,128]{2,1,0:T(8,128)(2,1)S(1)}, u32[]{:S(2)}, u32[]{:S(2)}) collective-permute-start(bf16[16,128,128]{2,1,0:T(8,128)(2,1)S(1)} %all-to-all-done.1.rest_0_), channel_id=1, source_target_pairs={{0,192},{64,0},{128,64},{192,128},{1,193},{65,1},{129,65},{193,129... | collective-permute-start | bytes 1572872 | tf_op jit(solution)/shard_map/ppermute | solution.py:66
  40.6 2.1 %collective-permute-start.2 = (bf16[16,128,128]{2,1,0:T(8,128)(2,1)S(1)}, bf16[16,128,128]{2,1,0:T(8,128)(2,1)S(1)}, u32[]{:S(2)}, u32[]{:S(2)}) collective-permute-start(bf16[16,128,128]{2,1,0:T(8,128)(2,1)S(1)} %all-to-all-done.1.rest_0_), channel_id=1, source_target_pairs={{0,1},{1,0},{2,3},{3,2},{4,5},{5,4},{6,7},{7,6},{8,9},{9,8},{10,11... | collective-permute-start | bytes 1572872 | tf_op jit(solution)/shard_map/ppermute | solution.py:78
  42.7 15.3 %collective-permute-done.1.rest_2_ = bf16[16,128,128]{2,1,0:T(8,128)(2,1)S(1)} collective-permute-done((bf16[16,128,128]{2,1,0:T(8,128)(2,1)S(1)}, bf16[16,128,128]{2,1,0:T(8,128)(2,1)S(1)}, u32[]{:S(2)}, u32[]{:S(2)}) %collective-permute-start.1) | collective-permute-done | bytes 524320 | tf_op jit(solution)/shard_map/ppermute | solution.py:66
  57.9 4.0 %collective-permute-start.4 = (bf16[16,128,128]{2,1,0:T(8,128)(2,1)S(1)}, bf16[16,128,128]{2,1,0:T(8,128)(2,1)}, u32[]{:S(2)}, u32[]{:S(2)}) collective-permute-start(bf16[16,128,128]{2,1,0:T(8,128)(2,1)S(1)} %collective-permute-done.1.rest_2_), channel_id=1, source_target_pairs={{0,1},{1,0},{2,3},{3,2},{4,5},{5,4},{6,7},{7,6},{8,9},{9,8},{10,11... | collective-permute-start | bytes 1572872 | tf_op jit(solution)/shard_map/ppermute | solution.py:78
  61.9 2.3 %collective-permute-done.rest_1_ = bf16[16,128,128]{2,1,0:T(8,128)(2,1)S(1)} collective-permute-done((bf16[16,128,128]{2,1,0:T(8,128)(2,1)S(1)}, bf16[16,128,128]{2,1,0:T(8,128)(2,1)S(1)}, u32[]{:S(2)}, u32[]{:S(2)}) %collective-permute-start) | collective-permute-done | bytes 524320 | tf_op jit(solution)/shard_map/ppermute | solution.py:65
  64.2 2.5 %collective-permute-start.3 = (bf16[16,128,128]{2,1,0:T(8,128)(2,1)S(1)}, bf16[16,128,128]{2,1,0:T(8,128)(2,1)}, u32[]{:S(2)}, u32[]{:S(2)}) collective-permute-start(bf16[16,128,128]{2,1,0:T(8,128)(2,1)S(1)} %collective-permute-done.rest_1_), channel_id=1, source_target_pairs={{0,1},{1,0},{2,3},{3,2},{4,5},{5,4},{6,7},{7,6},{8,9},{9,8},{10,11... | collective-permute-start | bytes 1572872 | tf_op jit(solution)/shard_map/ppermute | solution.py:78
  68.1 1.5 collective-permute-start.5
  70.0 4.7 %first_near.1.near = f32[2,32,128]{2,1,0:T(8,128)S(1)} custom-call(s32[4]{0:T(128)S(1)} %pad_add_fusion.meta, s32[2]{0:T(128)S(1)} %get-tuple-element.46.trips, s32[2,304]{1,0:T(2,128)S(1)} %get-tuple-element.47.ids, s32[2,304]{1,0:T(2,128)S(1)} %get-tuple-element.48.places, bf16[288,128,128]{2,1,0:T(8,128)(2,1)} %bitcast.33, ...), custom_call_target="tpu_custom_call" | custom-call | tf_op jit(solution)/shard_map/first_near/pallas_call | solution.py:419
  75.7 1.9 %collective-permute-done.5.rest_3_ = bf16[8,128,128]{2,1,0:T(8,128)(2,1)} collective-permute-done((bf16[8,128,128]{2,1,0:T(8,128)(2,1)}, bf16[8,128,128]{2,1,0:T(8,128)(2,1)}, u32[]{:S(2)}, u32[]{:S(2)}) %collective-permute-start.5) | collective-permute-done | bytes 262176 | tf_op jit(solution)/shard_map/ppermute | solution.py:72
  78.4 1.3 collective-permute-done.7.rest_8_
  80.1 4.5 %first.1 = bf16[16,2,32,128]{3,2,1,0:T(8,128)(2,1)S(1)} custom-call(s32[4]{0:T(128)S(1)} %pad_add_fusion.meta, s32[2]{0:T(128)S(1)} %get-tuple-element.46.trips, s32[2,304]{1,0:T(2,128)S(1)} %get-tuple-element.47.ids, s32[2,304]{1,0:T(2,128)S(1)} %get-tuple-element.48.places, s32[128]{0:T(128)S(1)} %reshape.116.hplaces, bf16[288,128,128]{2,1,0:T(8,128)(2,1)} %bitcast.34, ...), custom_call_target="tpu_custom_call" | custom-call | tf_op jit(solution)/shard_map/first/pallas_call | solution.py:434
  85.4 6.7 %all-to-all-start.2 = ((bf16[16,2,32,128]{3,2,1,0:T(8,128)(2,1)}), bf16[16,2,32,128]{3,2,1,0:T(8,128)(2,1)S(1)}, u32[]{:S(2)}, u32[]{:S(2)}) async-start(bf16[16,2,32,128]{3,2,1,0:T(8,128)(2,1)} %copy-done.1), calls=%async_computation.2 | async-start | bytes 524288 | tf_op jit(solution)/shard_map/all_to_all | solution.py:461
  93.3 2.2 %compact.1 = (s32[288]{0:T(512)}, s32[288]{0:T(512)}, s32[1]{0:T(128)}) custom-call(s32[128]{0:T(128)} %copy-done.9), custom_call_target="tpu_custom_call" | custom-call | tf_op jit(solution)/shard_map/compact/pallas_call | solution.py:464
  96.2 6.4 %all-to-all-done.2 = bf16[16,2,32,128]{3,2,1,0:T(8,128)(2,1)S(1)} async-done(((bf16[16,2,32,128]{3,2,1,0:T(8,128)(2,1)}), bf16[16,2,32,128]{3,2,1,0:T(8,128)(2,1)S(1)}, u32[]{:S(2)}, u32[]{:S(2)}) %all-to-all-start.2) | async-done | bytes 262176 | tf_op jit(solution)/shard_map/all_to_all | solution.py:461
  102.6 3.2 %collective-permute-start.9 = (bf16[8,2,2,32,128]{4,3,2,1,0:T(8,128)(2,1)S(1)}, bf16[8,2,2,32,128]{4,3,2,1,0:T(8,128)(2,1)S(1)}, u32[]{:S(2)}, u32[]{:S(2)}) collective-permute-start(bf16[8,2,2,32,128]{4,3,2,1,0:T(8,128)(2,1)S(1)} %bitcast.39), channel_id=1, source_target_pairs={{0,32},{32,0},{1,33},{33,1},{2,34},{34,2},{3,35},{35,3},{4,36},{36... | collective-permute-start | bytes 786440 | tf_op jit(solution)/shard_map/ppermute | solution.py:78
  105.8 4.0 %collective-permute-done.9 = bf16[8,2,2,32,128]{4,3,2,1,0:T(8,128)(2,1)S(1)} collective-permute-done((bf16[8,2,2,32,128]{4,3,2,1,0:T(8,128)(2,1)S(1)}, bf16[8,2,2,32,128]{4,3,2,1,0:T(8,128)(2,1)S(1)}, u32[]{:S(2)}, u32[]{:S(2)}) %collective-permute-start.9) | collective-permute-done | bytes 262176 | tf_op jit(solution)/shard_map/ppermute | solution.py:78
  110.0 1.5 collective-permute-start.15
  111.4 1.9 %project.3 = (bf16[2,16,2,32,128]{4,3,2,1,0:T(8,128)(2,1)S(1)}, bf16[2,16,2,32,128]{4,3,2,1,0:T(8,128)(2,1)S(1)}) custom-call(s32[4]{0:T(128)S(1)} %pad_add_fusion.meta, bf16[2,8,2,2,32,128]{5,4,3,2,1,0:T(8,128)(2,1)S(1)} %pad_maximum_fusion.refs_0_, bf16[128,512]{1,0:T(8,128)(2,1)S(1)} %copy_bitcast_fusion.refs_1_.refs_2_, ...), custom_call_target="tpu_custom_call" | custom-call | tf_op jit(solution)/shard_map/project/pallas_call | solution.py:480
  113.3 6.8 %collective-permute-done.16.refs_1_ = bf16[2,8,2,2,32,128]{5,4,3,2,1,0:T(8,128)(2,1)S(1)} collective-permute-done((bf16[2,8,2,2,32,128]{5,4,3,2,1,0:T(8,128)(2,1)S(1)}, bf16[2,8,2,2,32,128]{5,4,3,2,1,0:T(8,128)(2,1)S(1)}, u32[]{:S(2)}, u32[]{:S(2)}) %collective-permute-start.16) | collective-permute-done | bytes 524320 | tf_op jit(solution)/shard_map/ppermute | solution.py:490
  120.2 1.3 collective-permute-done.15.refs_0_
  121.5 3.0 %project.4 = (bf16[2,32,2,32,128]{4,3,2,1,0:T(8,128)(2,1)S(1)}, bf16[2,32,2,32,128]{4,3,2,1,0:T(8,128)(2,1)S(1)}) custom-call(s32[4]{0:T(128)S(1)} %pad_add_fusion.meta, bf16[2,8,2,2,32,128]{5,4,3,2,1,0:T(8,128)(2,1)S(1)} %collective-permute-done.15.refs_0_, bf16[2,8,2,2,32,128]{5,4,3,2,1,0:T(8,128)(2,1)S(1)} %collective-permute-done.16.refs_1_, ...), custom_call_target="tpu_custom_call" | custom-call | tf_op jit(solution)/shard_map/project/pallas_call | solution.py:480
  124.5 4.2 %collective-permute-start.20 = (bf16[2,32,2,32,128]{4,3,2,1,0:T(8,128)(2,1)S(1)}, bf16[2,32,2,32,128]{4,3,2,1,0:T(8,128)(2,1)S(1)}, u32[]{:S(2)}, u32[]{:S(2)}) collective-permute-start(bf16[2,32,2,32,128]{4,3,2,1,0:T(8,128)(2,1)S(1)} %get-tuple-element.76), channel_id=1, source_target_pairs={{0,1},{1,0},{2,3},{3,2},{4,5},{5,4},{6,7},{7,6},{8,9},{9,8},{10,11... | collective-permute-start | bytes 3145736 | tf_op jit(solution)/shard_map/ppermute | solution.py:78
  128.9 1.5 collective-permute-start.17
  130.4 1.3 collective-permute-done.19.rest_2_.rest_3_
  132.1 5.8 %second_near.1.near = f32[2,128,128]{2,1,0:T(8,128)S(1)} custom-call(s32[4]{0:T(128)S(1)} %pad_add_fusion.meta, s32[2]{0:T(128)S(1)} %get-tuple-element.46.trips, s32[14]{0:T(128)S(1)} %get-tuple-element.72.need, s32[2,304]{1,0:T(2,128)S(1)} %get-tuple-element.47.ids, s32[2,304]{1,0:T(2,128)S(1)} %get-tuple-element.48.places, ...), custom_call_target="tpu_custom_call" | custom-call | tf_op jit(solution)/shard_map/second_near/pallas_call | solution.py:500
  137.9 1.9 %project.5 = (bf16[2,16,2,32,128]{4,3,2,1,0:T(8,128)(2,1)S(1)}, bf16[2,16,2,32,128]{4,3,2,1,0:T(8,128)(2,1)S(1)}) custom-call(s32[4]{0:T(128)S(1)} %pad_add_fusion.meta, bf16[1,8,2,2,32,128]{5,4,3,2,1,0:T(8,128)(2,1)S(1)} %collective-permute-done.17.refs_0_, bf16[1,8,2,2,32,128]{5,4,3,2,1,0:T(8,128)(2,1)S(1)} %collective-permute-done.18.refs_1_, ...), custom_call_target="tpu_custom_call" | custom-call | tf_op jit(solution)/shard_map/project/pallas_call | solution.py:480
  141.0 3.1 %collective-permute-done.22.rest_5_ = bf16[2,16,2,32,128]{4,3,2,1,0:T(8,128)(2,1)S(1)} collective-permute-done((bf16[2,16,2,32,128]{4,3,2,1,0:T(8,128)(2,1)S(1)}, bf16[2,16,2,32,128]{4,3,2,1,0:T(8,128)(2,1)S(1)}, u32[]{:S(2)}, u32[]{:S(2)}) %collective-permute-start.22) | collective-permute-done | bytes 524320 | tf_op jit(solution)/shard_map/ppermute | solution.py:78
  144.1 6.7 %second.1 = bf16[256,128]{1,0:T(8,128)(2,1)} custom-call(s32[4]{0:T(128)S(1)} %pad_add_fusion.meta, s32[2]{0:T(128)S(1)} %get-tuple-element.46.trips, s32[1]{0:T(128)} %get-tuple-element.60.htrips, s32[2,304]{1,0:T(2,128)S(1)} %get-tuple-element.47.ids, s32[2,304]{1,0:T(2,128)S(1)} %get-tuple-element.48.places, s32[288]{0:T(512)S(1)} %copy-done.6, ...), custom_call_target="tpu_custom_call" | custom-call | tf_op jit(solution)/shard_map/second/pallas_call | solution.py:520
  (78 shorter events, 10.3 us)
Async XLA Ops:
  0.0 14.2 %copy-start.3 = (s32[1,8,8]{2,1,0:T(8,128)S(1)}, s32[1,8,8]{2,1,0:T(8,128)}, u32[]{:S(2)}) copy-start(s32[1,8,8]{2,1,0:T(8,128)} %cols.1) | copy-start | bytes 772
  0.0 14.2 %copy-start.2 = (s32[1,8,8]{2,1,0:T(8,128)S(1)}, s32[1,8,8]{2,1,0:T(8,128)}, u32[]{:S(2)}) copy-start(s32[1,8,8]{2,1,0:T(8,128)} %slots.1) | copy-start | bytes 772
  0.0 14.2 %copy-start.5 = (s32[1,8,36]{2,1,0:T(8,128)S(1)}, s32[1,8,36]{2,1,0:T(8,128)}, u32[]{:S(2)}) copy-start(s32[1,8,36]{2,1,0:T(8,128)} %lcols.1) | copy-start | bytes 3460
  0.0 14.2 %copy-start.4 = (s32[1,8,36]{2,1,0:T(8,128)S(1)}, s32[1,8,36]{2,1,0:T(8,128)}, u32[]{:S(2)}) copy-start(s32[1,8,36]{2,1,0:T(8,128)} %rows.1) | copy-start | bytes 3460
  1.8 27.0 %all-to-all-start.1 = ((bf16[16,128,128]{2,1,0:T(8,128)(2,1)}), bf16[16,128,128]{2,1,0:T(8,128)(2,1)S(1)}, u32[]{:S(2)}, u32[]{:S(2)}) async-start(bf16[16,128,128]{2,1,0:T(8,128)(2,1)} %broadcast_in_dim.18), calls=%async_computation.1 | async-start | bytes 1048576 | tf_op jit(solution)/shard_map/all_to_all | solution.py:83
  28.8 40.9 %all-to-all-start = ((bf16[64,72,128]{2,1,0:T(8,128)(2,1)}), bf16[64,72,128]{2,1,0:T(8,128)(2,1)S(1)}, u32[]{:S(2)}, u32[]{:S(2)}) async-start(bf16[64,72,128]{2,1,0:T(8,128)(2,1)} %get-tuple-element.45), calls=%async_computation | async-start | bytes 2359296 | tf_op jit(solution)/shard_map/all_to_all | solution.py:408
  38.1 19.8 %collective-permute-start.1 = (bf16[16,128,128]{2,1,0:T(8,128)(2,1)S(1)}, bf16[16,128,128]{2,1,0:T(8,128)(2,1)S(1)}, u32[]{:S(2)}, u32[]{:S(2)}) collective-permute-start(bf16[16,128,128]{2,1,0:T(8,128)(2,1)S(1)} %all-to-all-done.1.rest_0_), channel_id=1, source_target_pairs={{0,192},{64,0},{128,64},{192,128},{1,193},{65,1},{129,65},{193,129... | collective-permute-start | bytes 1572872 | tf_op jit(solution)/shard_map/ppermute | solution.py:66
  40.6 23.6 %collective-permute-start = (bf16[16,128,128]{2,1,0:T(8,128)(2,1)S(1)}, bf16[16,128,128]{2,1,0:T(8,128)(2,1)S(1)}, u32[]{:S(2)}, u32[]{:S(2)}) collective-permute-start(bf16[16,128,128]{2,1,0:T(8,128)(2,1)S(1)} %all-to-all-done.1.rest_0_), channel_id=1, source_target_pairs={{0,64},{64,128},{128,192},{192,0},{1,65},{65,129},{129,193},{193,1... | collective-permute-start | bytes 1572872 | tf_op jit(solution)/shard_map/ppermute | solution.py:65
  40.6 29.3 %collective-permute-start.2 = (bf16[16,128,128]{2,1,0:T(8,128)(2,1)S(1)}, bf16[16,128,128]{2,1,0:T(8,128)(2,1)S(1)}, u32[]{:S(2)}, u32[]{:S(2)}) collective-permute-start(bf16[16,128,128]{2,1,0:T(8,128)(2,1)S(1)} %all-to-all-done.1.rest_0_), channel_id=1, source_target_pairs={{0,1},{1,0},{2,3},{3,2},{4,5},{5,4},{6,7},{7,6},{8,9},{9,8},{10,11... | collective-permute-start | bytes 1572872 | tf_op jit(solution)/shard_map/ppermute | solution.py:78
  57.9 12.0 %collective-permute-start.4 = (bf16[16,128,128]{2,1,0:T(8,128)(2,1)S(1)}, bf16[16,128,128]{2,1,0:T(8,128)(2,1)}, u32[]{:S(2)}, u32[]{:S(2)}) collective-permute-start(bf16[16,128,128]{2,1,0:T(8,128)(2,1)S(1)} %collective-permute-done.1.rest_2_), channel_id=1, source_target_pairs={{0,1},{1,0},{2,3},{3,2},{4,5},{5,4},{6,7},{7,6},{8,9},{9,8},{10,11... | collective-permute-start | bytes 1572872 | tf_op jit(solution)/shard_map/ppermute | solution.py:78
  64.2 5.8 %collective-permute-start.3 = (bf16[16,128,128]{2,1,0:T(8,128)(2,1)S(1)}, bf16[16,128,128]{2,1,0:T(8,128)(2,1)}, u32[]{:S(2)}, u32[]{:S(2)}) collective-permute-start(bf16[16,128,128]{2,1,0:T(8,128)(2,1)S(1)} %collective-permute-done.rest_1_), channel_id=1, source_target_pairs={{0,1},{1,0},{2,3},{3,2},{4,5},{5,4},{6,7},{7,6},{8,9},{9,8},{10,11... | collective-permute-start | bytes 1572872 | tf_op jit(solution)/shard_map/ppermute | solution.py:78
  67.4 8.3 %collective-permute-start.6 = (bf16[8,128,128]{2,1,0:T(8,128)(2,1)}, bf16[8,128,128]{2,1,0:T(8,128)(2,1)}, u32[]{:S(2)}, u32[]{:S(2)}) collective-permute-start(bf16[8,128,128]{2,1,0:T(8,128)(2,1)} %slice.33), channel_id=1, source_target_pairs={{0,192},{64,0},{128,64},{192,128},{1,193},{65,1},{129,65},{193,129... | collective-permute-start | bytes 786440 | tf_op jit(solution)/shard_map/ppermute | solution.py:73
  68.1 9.5 %collective-permute-start.5 = (bf16[8,128,128]{2,1,0:T(8,128)(2,1)}, bf16[8,128,128]{2,1,0:T(8,128)(2,1)}, u32[]{:S(2)}, u32[]{:S(2)}) collective-permute-start(bf16[8,128,128]{2,1,0:T(8,128)(2,1)} %slice.32), channel_id=1, source_target_pairs={{0,64},{64,128},{128,192},{192,0},{1,65},{65,129},{129,193},{193,1... | collective-permute-start | bytes 786440 | tf_op jit(solution)/shard_map/ppermute | solution.py:72
  77.6 2.2 %collective-permute-start.7 = (bf16[8,128,128]{2,1,0:T(8,128)(2,1)}, bf16[8,128,128]{2,1,0:T(8,128)(2,1)S(1)}, u32[]{:S(2)}, u32[]{:S(2)}) collective-permute-start(bf16[8,128,128]{2,1,0:T(8,128)(2,1)} %collective-permute-done.5.rest_3_), channel_id=1, source_target_pairs={{0,1},{1,0},{2,3},{3,2},{4,5},{5,4},{6,7},{7,6},{8,9},{9,8},{10,11... | collective-permute-start | bytes 786440 | tf_op jit(solution)/shard_map/ppermute | solution.py:78
  78.4 1.7 %collective-permute-start.8 = (bf16[8,128,128]{2,1,0:T(8,128)(2,1)}, bf16[8,128,128]{2,1,0:T(8,128)(2,1)S(1)}, u32[]{:S(2)}, u32[]{:S(2)}) collective-permute-start(bf16[8,128,128]{2,1,0:T(8,128)(2,1)} %collective-permute-done.6.rest_4_), channel_id=1, source_target_pairs={{0,1},{1,0},{2,3},{3,2},{4,5},{5,4},{6,7},{7,6},{8,9},{9,8},{10,11... | collective-permute-start | bytes 786440 | tf_op jit(solution)/shard_map/ppermute | solution.py:78
  78.4 13.7 %copy-start.10 = (bf16[512,128]{1,0:T(8,128)(2,1)S(1)}, bf16[512,128]{1,0:T(8,128)(2,1)}, u32[]{:S(2)}) copy-start(bf16[512,128]{1,0:T(8,128)(2,1)} %param.15) | copy-start | bytes 393220
  84.7 8.4 %collective-permute-start.10 = (f32[136,128]{1,0:T(8,128)S(1)}, f32[136,128]{1,0:T(8,128)S(1)}, u32[]{:S(2)}, u32[]{:S(2)}) collective-permute-start(f32[136,128]{1,0:T(8,128)S(1)} %get-tuple-element.86), channel_id=1, source_target_pairs={{0,2},{2,0},{1,3},{3,1},{4,6},{6,4},{5,7},{7,5},{8,10},{10,8},{9,1... | collective-permute-start | bytes 208904 | tf_op jit(solution)/shard_map/ppermute | solution.py:78
  85.4 17.2 %all-to-all-start.2 = ((bf16[16,2,32,128]{3,2,1,0:T(8,128)(2,1)}), bf16[16,2,32,128]{3,2,1,0:T(8,128)(2,1)S(1)}, u32[]{:S(2)}, u32[]{:S(2)}) async-start(bf16[16,2,32,128]{3,2,1,0:T(8,128)(2,1)} %copy-done.1), calls=%async_computation.2 | async-start | bytes 524288 | tf_op jit(solution)/shard_map/all_to_all | solution.py:461
  92.1 3.3 %collective-permute-start.12 = (bf16[512,128]{1,0:T(8,128)(2,1)S(1)}, bf16[512,128]{1,0:T(8,128)(2,1)S(1)}, u32[]{:S(2)}, u32[]{:S(2)}) collective-permute-start(bf16[512,128]{1,0:T(8,128)(2,1)S(1)} %copy-done.10), channel_id=1, source_target_pairs={{0,1},{1,0},{2,3},{3,2},{4,5},{5,4},{6,7},{7,6},{8,9},{9,8},{10,11... | collective-permute-start | bytes 393224 | tf_op jit(solution)/shard_map/ppermute | solution.py:78
  93.1 2.3 %collective-permute-start.11 = (f32[2,136,128]{2,1,0:T(8,128)S(1)}, f32[2,136,128]{2,1,0:T(8,128)S(1)}, u32[]{:S(2)}, u32[]{:S(2)}) collective-permute-start(f32[2,136,128]{2,1,0:T(8,128)S(1)} %get-tuple-element.84), channel_id=1, source_target_pairs={{0,1},{1,0},{2,3},{3,2},{4,5},{5,4},{6,7},{7,6},{8,9},{9,8},{10,11... | collective-permute-start | bytes 417800 | tf_op jit(solution)/shard_map/ppermute | solution.py:78
  102.6 7.2 %collective-permute-start.9 = (bf16[8,2,2,32,128]{4,3,2,1,0:T(8,128)(2,1)S(1)}, bf16[8,2,2,32,128]{4,3,2,1,0:T(8,128)(2,1)S(1)}, u32[]{:S(2)}, u32[]{:S(2)}) collective-permute-start(bf16[8,2,2,32,128]{4,3,2,1,0:T(8,128)(2,1)S(1)} %bitcast.39), channel_id=1, source_target_pairs={{0,32},{32,0},{1,33},{33,1},{2,34},{34,2},{3,35},{35,3},{4,36},{36... | collective-permute-start | bytes 786440 | tf_op jit(solution)/shard_map/ppermute | solution.py:78
  109.9 10.3 %collective-permute-start.16 = (bf16[2,8,2,2,32,128]{5,4,3,2,1,0:T(8,128)(2,1)S(1)}, bf16[2,8,2,2,32,128]{5,4,3,2,1,0:T(8,128)(2,1)S(1)}, u32[]{:S(2)}, u32[]{:S(2)}) collective-permute-start(bf16[2,8,2,2,32,128]{5,4,3,2,1,0:T(8,128)(2,1)S(1)} %pad_maximum_fusion.refs_0_), channel_id=1, source_target_pairs={{0,192},{64,0},{128,64},{192,128},{1,193},{65,1},{129,65},{193,129... | collective-permute-start | bytes 1572872 | tf_op jit(solution)/shard_map/ppermute | solution.py:490
  110.0 11.5 %collective-permute-start.15 = (bf16[2,8,2,2,32,128]{5,4,3,2,1,0:T(8,128)(2,1)S(1)}, bf16[2,8,2,2,32,128]{5,4,3,2,1,0:T(8,128)(2,1)S(1)}, u32[]{:S(2)}, u32[]{:S(2)}) collective-permute-start(bf16[2,8,2,2,32,128]{5,4,3,2,1,0:T(8,128)(2,1)S(1)} %pad_maximum_fusion.refs_0_), channel_id=1, source_target_pairs={{0,64},{64,128},{128,192},{192,0},{1,65},{65,129},{129,193},{193,1... | collective-permute-start | bytes 1572872 | tf_op jit(solution)/shard_map/ppermute | solution.py:489
  111.4 28.4 %collective-permute-start.14 = (bf16[64,72,128]{2,1,0:T(8,128)(2,1)S(1)}, bf16[64,72,128]{2,1,0:T(8,128)(2,1)S(1)}, u32[]{:S(2)}, u32[]{:S(2)}) collective-permute-start(bf16[64,72,128]{2,1,0:T(8,128)(2,1)S(1)} %all-to-all-done.heavy.h0), channel_id=1, source_target_pairs={{0,2},{2,0},{1,3},{3,1},{4,6},{6,4},{5,7},{7,5},{8,10},{10,8},{9,1... | collective-permute-start | bytes 3538952 | tf_op jit(solution)/shard_map/ppermute | solution.py:78
  124.5 7.6 %collective-permute-start.20 = (bf16[2,32,2,32,128]{4,3,2,1,0:T(8,128)(2,1)S(1)}, bf16[2,32,2,32,128]{4,3,2,1,0:T(8,128)(2,1)S(1)}, u32[]{:S(2)}, u32[]{:S(2)}) collective-permute-start(bf16[2,32,2,32,128]{4,3,2,1,0:T(8,128)(2,1)S(1)} %get-tuple-element.76), channel_id=1, source_target_pairs={{0,1},{1,0},{2,3},{3,2},{4,5},{5,4},{6,7},{7,6},{8,9},{9,8},{10,11... | collective-permute-start | bytes 3145736 | tf_op jit(solution)/shard_map/ppermute | solution.py:78
  128.7 3.0 %collective-permute-start.19 = (bf16[2,16,2,32,128]{4,3,2,1,0:T(8,128)(2,1)S(1)}, bf16[2,16,2,32,128]{4,3,2,1,0:T(8,128)(2,1)S(1)}, u32[]{:S(2)}, u32[]{:S(2)}) collective-permute-start(bf16[2,16,2,32,128]{4,3,2,1,0:T(8,128)(2,1)S(1)} %get-tuple-element.75), channel_id=1, source_target_pairs={{0,1},{1,0},{2,3},{3,2},{4,5},{5,4},{6,7},{7,6},{8,9},{9,8},{10,11... | collective-permute-start | bytes 1572872 | tf_op jit(solution)/shard_map/ppermute | solution.py:78
  128.8 9.1 %collective-permute-start.18 = (bf16[1,8,2,2,32,128]{5,4,3,2,1,0:T(8,128)(2,1)S(1)}, bf16[1,8,2,2,32,128]{5,4,3,2,1,0:T(8,128)(2,1)S(1)}, u32[]{:S(2)}, u32[]{:S(2)}) collective-permute-start(bf16[1,8,2,2,32,128]{5,4,3,2,1,0:T(8,128)(2,1)S(1)} %slice.28), channel_id=1, source_target_pairs={{0,192},{64,0},{128,64},{192,128},{1,193},{65,1},{129,65},{193,129... | collective-permute-start | bytes 786440 | tf_op jit(solution)/shard_map/ppermute | solution.py:495
  128.9 9.0 %collective-permute-start.17 = (bf16[1,8,2,2,32,128]{5,4,3,2,1,0:T(8,128)(2,1)S(1)}, bf16[1,8,2,2,32,128]{5,4,3,2,1,0:T(8,128)(2,1)S(1)}, u32[]{:S(2)}, u32[]{:S(2)}) collective-permute-start(bf16[1,8,2,2,32,128]{5,4,3,2,1,0:T(8,128)(2,1)S(1)} %slice.27), channel_id=1, source_target_pairs={{0,64},{64,128},{128,192},{192,0},{1,65},{65,129},{129,193},{193,1... | collective-permute-start | bytes 786440 | tf_op jit(solution)/shard_map/ppermute | solution.py:494
  131.7 9.3 %collective-permute-start.13 = (bf16[64,72,128]{2,1,0:T(8,128)(2,1)S(1)}, bf16[64,72,128]{2,1,0:T(8,128)(2,1)S(1)}, u32[]{:S(2)}, u32[]{:S(2)}) collective-permute-start(bf16[64,72,128]{2,1,0:T(8,128)(2,1)S(1)} %all-to-all-done.heavy.h0), channel_id=1, source_target_pairs={{0,1},{1,0},{2,3},{3,2},{4,5},{5,4},{6,7},{7,6},{8,9},{9,8},{10,11... | collective-permute-start | bytes 3538952 | tf_op jit(solution)/shard_map/ppermute | solution.py:78
  132.1 12.1 %copy-start.8 = (f32[128]{0:T(128)S(1)}, f32[128]{0:T(128)}, u32[]{:S(2)}) copy-start(f32[128]{0:T(128)} %param.16) | copy-start | bytes 1540
  139.9 4.3 %collective-permute-start.21 = (bf16[64,72,128]{2,1,0:T(8,128)(2,1)S(1)}, bf16[64,72,128]{2,1,0:T(8,128)(2,1)S(1)}, u32[]{:S(2)}, u32[]{:S(2)}) collective-permute-start(bf16[64,72,128]{2,1,0:T(8,128)(2,1)S(1)} %collective-permute-done.14.h2), channel_id=1, source_target_pairs={{0,1},{1,0},{2,3},{3,2},{4,5},{5,4},{6,7},{7,6},{8,9},{9,8},{10,11... | collective-permute-start | bytes 3538952 | tf_op jit(solution)/shard_map/ppermute | solution.py:78
  140.9 3.2 %collective-permute-start.22 = (bf16[2,16,2,32,128]{4,3,2,1,0:T(8,128)(2,1)S(1)}, bf16[2,16,2,32,128]{4,3,2,1,0:T(8,128)(2,1)S(1)}, u32[]{:S(2)}, u32[]{:S(2)}) collective-permute-start(bf16[2,16,2,32,128]{4,3,2,1,0:T(8,128)(2,1)S(1)} %get-tuple-element.80), channel_id=1, source_target_pairs={{0,1},{1,0},{2,3},{3,2},{4,5},{5,4},{6,7},{7,6},{8,9},{9,8},{10,11... | collective-permute-start | bytes 1572872 | tf_op jit(solution)/shard_map/ppermute | solution.py:78
  (7 other events, 48.4 us)

commit v6 on v5

--- a/solution.py
+++ b/solution.py
@@ -27,7 +27,8 @@
 NOTES = 8
 NX = 4
 NPLANE = 2 * NR
-HSTEP = 32
+HSTEP = 64
+HLIST_STEP = 32
 NEAR_STEPS = NB - 2
 FAR_AT = -(-NEAR_STEPS * LT // STEP) * STEP
 LIST = FAR_AT + -(-2 * LT // STEP) * STEP
@@ -172,7 +173,7 @@
     n = lax.fori_loop(0, SLOTS, put, 0, unroll=8)
     ids[n] = 0
     places[n] = NT
-    htrips[0] = (n + STEP - 1) // STEP
+    htrips[0] = (n + HLIST_STEP - 1) // HLIST_STEP
 
 
 def dots(tile, value, count, ids, places, acc):
@@ -359,9 +360,9 @@
         copy.wait()
 
     def heavy_body(g, acc):
-        base = g * STEP
+        base = g * HLIST_STEP
         return dots(
-            lambda i: htiles[i], value, STEP, lambda u: hids[base + u], lambda u: hplaces[base + u], acc
+            lambda i: htiles[i], value, HLIST_STEP, lambda u: hids[base + u], lambda u: hplaces[base + u], acc
         )
 
     hsum = lax.fori_loop(0, htrips[0], heavy_body, jnp.zeros((T, T), jnp.float32))

time: 152 us -> 151 us (level)
  no operation moved by 1% of the time
where the time goes in v6:
time: 151 us; the launch traced here: 150 us
  starting transfers between devices  54.3 us (36%)
  waiting for transfers between devices  52.1 us (35%)
  Pallas kernels  38.2 us (25%)
  local copies, waits for them, and re-layouts  4.14 us (3%)
    ppermute x15, starting transfers between devices, swap(): return lax.ppermute(x, axis, around(axis, 1))  19.5 us
    ppermute x1, waiting for transfers between devices, along_x(): ahead = lax.ppermute(near, 'x', around('x', -1))  15.3 us
    all_to_all x1, starting transfers between devices, everyone(): return lax.all_to_all(spread, axis, 0, 0, tiled=True)  11.7 us
    ppermute x15, waiting for transfers between devices, swap(): return lax.ppermute(x, axis, around(axis, 1))  10.2 us
    all_to_all x1, starting transfers between devices, per_device(): arrived = lax.all_to_all(packed, GROUP, 0, 0, tiled=True)  9.33 us
    pallas_call x1, Pallas kernels, per_device(): pl.pallas_call(pack_kernel, out_shape=(jax.ShapeDtypeStruct((NG, 2 * QR +...  7.37 us
    all_to_all x1, waiting for transfers between devices, everyone(): return lax.all_to_all(spread, axis, 0, 0, tiled=True)  7.11 us
    ppermute x1, waiting for transfers between devices, per_device(): ahead = lax.ppermute(rows, 'x', around('x', -1))  6.85 us
  transfers between devices with their start and end apart: 26, of which 13 were waited for; matrix products, arithmetic and copies ran while one was open for 2% of the time, Pallas kernels for 18%

profile of v6, /device:TPU:1, one launch (start us, length us, event | category | flops | bytes accessed | tf_op | source)
XLA Modules:
  0.0 150.4 jit_solution(12781406786638988052)
XLA Ops:
  1.8 11.7 %all-to-all-start.1 = ((bf16[16,128,128]{2,1,0:T(8,128)(2,1)}), bf16[16,128,128]{2,1,0:T(8,128)(2,1)S(1)}, u32[]{:S(2)}, u32[]{:S(2)}) async-start(bf16[16,128,128]{2,1,0:T(8,128)(2,1)} %broadcast_in_dim.18), calls=%async_computation.1 | async-start | bytes 1048576 | tf_op jit(solution)/shard_map/all_to_all | solution.py:84
  14.3 7.4 %pack.1 = (bf16[64,72,128]{2,1,0:T(8,128)(2,1)}, s32[2,304]{1,0:T(2,128)S(1)}, s32[2,304]{1,0:T(2,128)S(1)}, s32[14]{0:T(128)S(1)}, s32[2]{0:T(128)S(1)}) custom-call(s32[4]{0:T(128)S(1)} %pad_add_fusion.meta, s32[1,8,8]{2,1,0:T(8,128)S(1)} %copy-done.2, s32[1,8,8]{2,1,0:T(8,128)S(1)} %copy-done.3, s32[1,8,36]{2,1,0:T(8,128)S(1)} %copy-done.4, ...), custom_call_target="tpu_custom_call" | custom-call | bytes 30000000 | tf_op jit(solution)/shard_map/pack/pallas_call | solution.py:392
  21.6 7.1 %all-to-all-done.1.rest_0_ = bf16[16,128,128]{2,1,0:T(8,128)(2,1)S(1)} async-done(((bf16[16,128,128]{2,1,0:T(8,128)(2,1)}), bf16[16,128,128]{2,1,0:T(8,128)(2,1)S(1)}, u32[]{:S(2)}, u32[]{:S(2)}) %all-to-all-start.1) | async-done | bytes 524320 | tf_op jit(solution)/shard_map/all_to_all | solution.py:84
  28.8 9.3 %all-to-all-start = ((bf16[64,72,128]{2,1,0:T(8,128)(2,1)}), bf16[64,72,128]{2,1,0:T(8,128)(2,1)S(1)}, u32[]{:S(2)}, u32[]{:S(2)}) async-start(bf16[64,72,128]{2,1,0:T(8,128)(2,1)} %get-tuple-element.45), calls=%async_computation | async-start | bytes 2359296 | tf_op jit(solution)/shard_map/all_to_all | solution.py:409
  38.1 2.5 %collective-permute-start.1 = (bf16[16,128,128]{2,1,0:T(8,128)(2,1)S(1)}, bf16[16,128,128]{2,1,0:T(8,128)(2,1)S(1)}, u32[]{:S(2)}, u32[]{:S(2)}) collective-permute-start(bf16[16,128,128]{2,1,0:T(8,128)(2,1)S(1)} %all-to-all-done.1.rest_0_), channel_id=1, source_target_pairs={{0,192},{64,0},{128,64},{192,128},{1,193},{65,1},{129,65},{193,129... | collective-permute-start | bytes 1572872 | tf_op jit(solution)/shard_map/ppermute | solution.py:67
  40.6 2.1 %collective-permute-start.2 = (bf16[16,128,128]{2,1,0:T(8,128)(2,1)S(1)}, bf16[16,128,128]{2,1,0:T(8,128)(2,1)S(1)}, u32[]{:S(2)}, u32[]{:S(2)}) collective-permute-start(bf16[16,128,128]{2,1,0:T(8,128)(2,1)S(1)} %all-to-all-done.1.rest_0_), channel_id=1, source_target_pairs={{0,1},{1,0},{2,3},{3,2},{4,5},{5,4},{6,7},{7,6},{8,9},{9,8},{10,11... | collective-permute-start | bytes 1572872 | tf_op jit(solution)/shard_map/ppermute | solution.py:79
  42.7 15.3 %collective-permute-done.1.rest_2_ = bf16[16,128,128]{2,1,0:T(8,128)(2,1)S(1)} collective-permute-done((bf16[16,128,128]{2,1,0:T(8,128)(2,1)S(1)}, bf16[16,128,128]{2,1,0:T(8,128)(2,1)S(1)}, u32[]{:S(2)}, u32[]{:S(2)}) %collective-permute-start.1) | collective-permute-done | bytes 524320 | tf_op jit(solution)/shard_map/ppermute | solution.py:67
  57.9 4.0 %collective-permute-start.4 = (bf16[16,128,128]{2,1,0:T(8,128)(2,1)S(1)}, bf16[16,128,128]{2,1,0:T(8,128)(2,1)}, u32[]{:S(2)}, u32[]{:S(2)}) collective-permute-start(bf16[16,128,128]{2,1,0:T(8,128)(2,1)S(1)} %collective-permute-done.1.rest_2_), channel_id=1, source_target_pairs={{0,1},{1,0},{2,3},{3,2},{4,5},{5,4},{6,7},{7,6},{8,9},{9,8},{10,11... | collective-permute-start | bytes 1572872 | tf_op jit(solution)/shard_map/ppermute | solution.py:79
  61.9 2.3 %collective-permute-done.rest_1_ = bf16[16,128,128]{2,1,0:T(8,128)(2,1)S(1)} collective-permute-done((bf16[16,128,128]{2,1,0:T(8,128)(2,1)S(1)}, bf16[16,128,128]{2,1,0:T(8,128)(2,1)S(1)}, u32[]{:S(2)}, u32[]{:S(2)}) %collective-permute-start) | collective-permute-done | bytes 524320 | tf_op jit(solution)/shard_map/ppermute | solution.py:66
  64.2 2.5 %collective-permute-start.3 = (bf16[16,128,128]{2,1,0:T(8,128)(2,1)S(1)}, bf16[16,128,128]{2,1,0:T(8,128)(2,1)}, u32[]{:S(2)}, u32[]{:S(2)}) collective-permute-start(bf16[16,128,128]{2,1,0:T(8,128)(2,1)S(1)} %collective-permute-done.rest_1_), channel_id=1, source_target_pairs={{0,1},{1,0},{2,3},{3,2},{4,5},{5,4},{6,7},{7,6},{8,9},{9,8},{10,11... | collective-permute-start | bytes 1572872 | tf_op jit(solution)/shard_map/ppermute | solution.py:79
  68.1 1.5 collective-permute-start.5
  70.0 5.0 %first_near.1.near = f32[2,32,128]{2,1,0:T(8,128)S(1)} custom-call(s32[4]{0:T(128)S(1)} %pad_add_fusion.meta, s32[2]{0:T(128)S(1)} %get-tuple-element.46.trips, s32[2,304]{1,0:T(2,128)S(1)} %get-tuple-element.47.ids, s32[2,304]{1,0:T(2,128)S(1)} %get-tuple-element.48.places, bf16[288,128,128]{2,1,0:T(8,128)(2,1)} %bitcast.33, ...), custom_call_target="tpu_custom_call" | custom-call | tf_op jit(solution)/shard_map/first_near/pallas_call | solution.py:420
  75.7 1.9 %collective-permute-done.5.rest_3_ = bf16[8,128,128]{2,1,0:T(8,128)(2,1)} collective-permute-done((bf16[8,128,128]{2,1,0:T(8,128)(2,1)}, bf16[8,128,128]{2,1,0:T(8,128)(2,1)}, u32[]{:S(2)}, u32[]{:S(2)}) %collective-permute-start.5) | collective-permute-done | bytes 262176 | tf_op jit(solution)/shard_map/ppermute | solution.py:73
  78.4 1.3 collective-permute-done.7.rest_8_
  80.1 4.3 %first.1 = bf16[16,2,32,128]{3,2,1,0:T(8,128)(2,1)S(1)} custom-call(s32[4]{0:T(128)S(1)} %pad_add_fusion.meta, s32[2]{0:T(128)S(1)} %get-tuple-element.46.trips, s32[2,304]{1,0:T(2,128)S(1)} %get-tuple-element.47.ids, s32[2,304]{1,0:T(2,128)S(1)} %get-tuple-element.48.places, s32[128]{0:T(128)S(1)} %reshape.116.hplaces, bf16[288,128,128]{2,1,0:T(8,128)(2,1)} %bitcast.34, ...), custom_call_target="tpu_custom_call" | custom-call | tf_op jit(solution)/shard_map/first/pallas_call | solution.py:435
  85.1 6.7 %all-to-all-start.2 = ((bf16[16,2,32,128]{3,2,1,0:T(8,128)(2,1)}), bf16[16,2,32,128]{3,2,1,0:T(8,128)(2,1)S(1)}, u32[]{:S(2)}, u32[]{:S(2)}) async-start(bf16[16,2,32,128]{3,2,1,0:T(8,128)(2,1)} %copy-done.1), calls=%async_computation.2 | async-start | bytes 524288 | tf_op jit(solution)/shard_map/all_to_all | solution.py:462
  93.0 2.2 %compact.1 = (s32[288]{0:T(512)}, s32[288]{0:T(512)}, s32[1]{0:T(128)}) custom-call(s32[128]{0:T(128)} %copy-done.9), custom_call_target="tpu_custom_call" | custom-call | tf_op jit(solution)/shard_map/compact/pallas_call | solution.py:465
  95.9 6.4 %all-to-all-done.2 = bf16[16,2,32,128]{3,2,1,0:T(8,128)(2,1)S(1)} async-done(((bf16[16,2,32,128]{3,2,1,0:T(8,128)(2,1)}), bf16[16,2,32,128]{3,2,1,0:T(8,128)(2,1)S(1)}, u32[]{:S(2)}, u32[]{:S(2)}) %all-to-all-start.2) | async-done | bytes 262176 | tf_op jit(solution)/shard_map/all_to_all | solution.py:462
  102.3 3.2 %collective-permute-start.9 = (bf16[8,2,2,32,128]{4,3,2,1,0:T(8,128)(2,1)S(1)}, bf16[8,2,2,32,128]{4,3,2,1,0:T(8,128)(2,1)S(1)}, u32[]{:S(2)}, u32[]{:S(2)}) collective-permute-start(bf16[8,2,2,32,128]{4,3,2,1,0:T(8,128)(2,1)S(1)} %bitcast.39), channel_id=1, source_target_pairs={{0,32},{32,0},{1,33},{33,1},{2,34},{34,2},{3,35},{35,3},{4,36},{36... | collective-permute-start | bytes 786440 | tf_op jit(solution)/shard_map/ppermute | solution.py:79
  105.5 4.0 %collective-permute-done.9 = bf16[8,2,2,32,128]{4,3,2,1,0:T(8,128)(2,1)S(1)} collective-permute-done((bf16[8,2,2,32,128]{4,3,2,1,0:T(8,128)(2,1)S(1)}, bf16[8,2,2,32,128]{4,3,2,1,0:T(8,128)(2,1)S(1)}, u32[]{:S(2)}, u32[]{:S(2)}) %collective-permute-start.9) | collective-permute-done | bytes 262176 | tf_op jit(solution)/shard_map/ppermute | solution.py:79
  109.7 1.5 collective-permute-start.15
  111.2 1.9 %project.3 = (bf16[2,16,2,32,128]{4,3,2,1,0:T(8,128)(2,1)S(1)}, bf16[2,16,2,32,128]{4,3,2,1,0:T(8,128)(2,1)S(1)}) custom-call(s32[4]{0:T(128)S(1)} %pad_add_fusion.meta, bf16[2,8,2,2,32,128]{5,4,3,2,1,0:T(8,128)(2,1)S(1)} %pad_maximum_fusion.refs_0_, bf16[128,512]{1,0:T(8,128)(2,1)S(1)} %copy_bitcast_fusion.refs_1_.refs_2_, ...), custom_call_target="tpu_custom_call" | custom-call | tf_op jit(solution)/shard_map/project/pallas_call | solution.py:481
  113.1 6.8 %collective-permute-done.16.refs_1_ = bf16[2,8,2,2,32,128]{5,4,3,2,1,0:T(8,128)(2,1)S(1)} collective-permute-done((bf16[2,8,2,2,32,128]{5,4,3,2,1,0:T(8,128)(2,1)S(1)}, bf16[2,8,2,2,32,128]{5,4,3,2,1,0:T(8,128)(2,1)S(1)}, u32[]{:S(2)}, u32[]{:S(2)}) %collective-permute-start.16) | collective-permute-done | bytes 524320 | tf_op jit(solution)/shard_map/ppermute | solution.py:491
  119.9 1.3 collective-permute-done.15.refs_0_
  121.2 3.0 %project.4 = (bf16[2,32,2,32,128]{4,3,2,1,0:T(8,128)(2,1)S(1)}, bf16[2,32,2,32,128]{4,3,2,1,0:T(8,128)(2,1)S(1)}) custom-call(s32[4]{0:T(128)S(1)} %pad_add_fusion.meta, bf16[2,8,2,2,32,128]{5,4,3,2,1,0:T(8,128)(2,1)S(1)} %collective-permute-done.15.refs_0_, bf16[2,8,2,2,32,128]{5,4,3,2,1,0:T(8,128)(2,1)S(1)} %collective-permute-done.16.refs_1_, ...), custom_call_target="tpu_custom_call" | custom-call | tf_op jit(solution)/shard_map/project/pallas_call | solution.py:481
  124.2 4.2 %collective-permute-start.20 = (bf16[2,32,2,32,128]{4,3,2,1,0:T(8,128)(2,1)S(1)}, bf16[2,32,2,32,128]{4,3,2,1,0:T(8,128)(2,1)S(1)}, u32[]{:S(2)}, u32[]{:S(2)}) collective-permute-start(bf16[2,32,2,32,128]{4,3,2,1,0:T(8,128)(2,1)S(1)} %get-tuple-element.76), channel_id=1, source_target_pairs={{0,1},{1,0},{2,3},{3,2},{4,5},{5,4},{6,7},{7,6},{8,9},{9,8},{10,11... | collective-permute-start | bytes 3145736 | tf_op jit(solution)/shard_map/ppermute | solution.py:79
  128.7 1.5 collective-permute-start.17
  130.1 1.3 collective-permute-done.19.rest_2_.rest_3_
  131.8 6.3 %second_near.1.near = f32[2,128,128]{2,1,0:T(8,128)S(1)} custom-call(s32[4]{0:T(128)S(1)} %pad_add_fusion.meta, s32[2]{0:T(128)S(1)} %get-tuple-element.46.trips, s32[14]{0:T(128)S(1)} %get-tuple-element.72.need, s32[2,304]{1,0:T(2,128)S(1)} %get-tuple-element.47.ids, s32[2,304]{1,0:T(2,128)S(1)} %get-tuple-element.48.places, ...), custom_call_target="tpu_custom_call" | custom-call | tf_op jit(solution)/shard_map/second_near/pallas_call | solution.py:501
  138.1 1.9 %project.5 = (bf16[2,16,2,32,128]{4,3,2,1,0:T(8,128)(2,1)S(1)}, bf16[2,16,2,32,128]{4,3,2,1,0:T(8,128)(2,1)S(1)}) custom-call(s32[4]{0:T(128)S(1)} %pad_add_fusion.meta, bf16[1,8,2,2,32,128]{5,4,3,2,1,0:T(8,128)(2,1)S(1)} %collective-permute-done.17.refs_0_, bf16[1,8,2,2,32,128]{5,4,3,2,1,0:T(8,128)(2,1)S(1)} %collective-permute-done.18.refs_1_, ...), custom_call_target="tpu_custom_call" | custom-call | tf_op jit(solution)/shard_map/project/pallas_call | solution.py:481
  140.8 3.1 %collective-permute-done.22.rest_5_ = bf16[2,16,2,32,128]{4,3,2,1,0:T(8,128)(2,1)S(1)} collective-permute-done((bf16[2,16,2,32,128]{4,3,2,1,0:T(8,128)(2,1)S(1)}, bf16[2,16,2,32,128]{4,3,2,1,0:T(8,128)(2,1)S(1)}, u32[]{:S(2)}, u32[]{:S(2)}) %collective-permute-start.22) | collective-permute-done | bytes 524320 | tf_op jit(solution)/shard_map/ppermute | solution.py:79
  143.9 6.4 %second.1 = bf16[256,128]{1,0:T(8,128)(2,1)} custom-call(s32[4]{0:T(128)S(1)} %pad_add_fusion.meta, s32[2]{0:T(128)S(1)} %get-tuple-element.46.trips, s32[1]{0:T(128)} %get-tuple-element.60.htrips, s32[2,304]{1,0:T(2,128)S(1)} %get-tuple-element.47.ids, s32[2,304]{1,0:T(2,128)S(1)} %get-tuple-element.48.places, s32[288]{0:T(512)S(1)} %copy-done.6, ...), custom_call_target="tpu_custom_call" | custom-call | tf_op jit(solution)/shard_map/second/pallas_call | solution.py:521
  (78 shorter events, 9.5 us)
Async XLA Ops:
  0.0 14.2 %copy-start.3 = (s32[1,8,8]{2,1,0:T(8,128)S(1)}, s32[1,8,8]{2,1,0:T(8,128)}, u32[]{:S(2)}) copy-start(s32[1,8,8]{2,1,0:T(8,128)} %cols.1) | copy-start | bytes 772
  0.0 14.2 %copy-start.2 = (s32[1,8,8]{2,1,0:T(8,128)S(1)}, s32[1,8,8]{2,1,0:T(8,128)}, u32[]{:S(2)}) copy-start(s32[1,8,8]{2,1,0:T(8,128)} %slots.1) | copy-start | bytes 772
  0.0 14.2 %copy-start.5 = (s32[1,8,36]{2,1,0:T(8,128)S(1)}, s32[1,8,36]{2,1,0:T(8,128)}, u32[]{:S(2)}) copy-start(s32[1,8,36]{2,1,0:T(8,128)} %lcols.1) | copy-start | bytes 3460
  0.0 14.2 %copy-start.4 = (s32[1,8,36]{2,1,0:T(8,128)S(1)}, s32[1,8,36]{2,1,0:T(8,128)}, u32[]{:S(2)}) copy-start(s32[1,8,36]{2,1,0:T(8,128)} %rows.1) | copy-start | bytes 3460
  1.8 27.0 %all-to-all-start.1 = ((bf16[16,128,128]{2,1,0:T(8,128)(2,1)}), bf16[16,128,128]{2,1,0:T(8,128)(2,1)S(1)}, u32[]{:S(2)}, u32[]{:S(2)}) async-start(bf16[16,128,128]{2,1,0:T(8,128)(2,1)} %broadcast_in_dim.18), calls=%async_computation.1 | async-start | bytes 1048576 | tf_op jit(solution)/shard_map/all_to_all | solution.py:84
  28.8 40.9 %all-to-all-start = ((bf16[64,72,128]{2,1,0:T(8,128)(2,1)}), bf16[64,72,128]{2,1,0:T(8,128)(2,1)S(1)}, u32[]{:S(2)}, u32[]{:S(2)}) async-start(bf16[64,72,128]{2,1,0:T(8,128)(2,1)} %get-tuple-element.45), calls=%async_computation | async-start | bytes 2359296 | tf_op jit(solution)/shard_map/all_to_all | solution.py:409
  38.1 19.8 %collective-permute-start.1 = (bf16[16,128,128]{2,1,0:T(8,128)(2,1)S(1)}, bf16[16,128,128]{2,1,0:T(8,128)(2,1)S(1)}, u32[]{:S(2)}, u32[]{:S(2)}) collective-permute-start(bf16[16,128,128]{2,1,0:T(8,128)(2,1)S(1)} %all-to-all-done.1.rest_0_), channel_id=1, source_target_pairs={{0,192},{64,0},{128,64},{192,128},{1,193},{65,1},{129,65},{193,129... | collective-permute-start | bytes 1572872 | tf_op jit(solution)/shard_map/ppermute | solution.py:67
  40.6 23.6 %collective-permute-start = (bf16[16,128,128]{2,1,0:T(8,128)(2,1)S(1)}, bf16[16,128,128]{2,1,0:T(8,128)(2,1)S(1)}, u32[]{:S(2)}, u32[]{:S(2)}) collective-permute-start(bf16[16,128,128]{2,1,0:T(8,128)(2,1)S(1)} %all-to-all-done.1.rest_0_), channel_id=1, source_target_pairs={{0,64},{64,128},{128,192},{192,0},{1,65},{65,129},{129,193},{193,1... | collective-permute-start | bytes 1572872 | tf_op jit(solution)/shard_map/ppermute | solution.py:66
  40.6 29.3 %collective-permute-start.2 = (bf16[16,128,128]{2,1,0:T(8,128)(2,1)S(1)}, bf16[16,128,128]{2,1,0:T(8,128)(2,1)S(1)}, u32[]{:S(2)}, u32[]{:S(2)}) collective-permute-start(bf16[16,128,128]{2,1,0:T(8,128)(2,1)S(1)} %all-to-all-done.1.rest_0_), channel_id=1, source_target_pairs={{0,1},{1,0},{2,3},{3,2},{4,5},{5,4},{6,7},{7,6},{8,9},{9,8},{10,11... | collective-permute-start | bytes 1572872 | tf_op jit(solution)/shard_map/ppermute | solution.py:79
  57.9 12.0 %collective-permute-start.4 = (bf16[16,128,128]{2,1,0:T(8,128)(2,1)S(1)}, bf16[16,128,128]{2,1,0:T(8,128)(2,1)}, u32[]{:S(2)}, u32[]{:S(2)}) collective-permute-start(bf16[16,128,128]{2,1,0:T(8,128)(2,1)S(1)} %collective-permute-done.1.rest_2_), channel_id=1, source_target_pairs={{0,1},{1,0},{2,3},{3,2},{4,5},{5,4},{6,7},{7,6},{8,9},{9,8},{10,11... | collective-permute-start | bytes 1572872 | tf_op jit(solution)/shard_map/ppermute | solution.py:79
  64.2 5.8 %collective-permute-start.3 = (bf16[16,128,128]{2,1,0:T(8,128)(2,1)S(1)}, bf16[16,128,128]{2,1,0:T(8,128)(2,1)}, u32[]{:S(2)}, u32[]{:S(2)}) collective-permute-start(bf16[16,128,128]{2,1,0:T(8,128)(2,1)S(1)} %collective-permute-done.rest_1_), channel_id=1, source_target_pairs={{0,1},{1,0},{2,3},{3,2},{4,5},{5,4},{6,7},{7,6},{8,9},{9,8},{10,11... | collective-permute-start | bytes 1572872 | tf_op jit(solution)/shard_map/ppermute | solution.py:79
  67.4 8.3 %collective-permute-start.6 = (bf16[8,128,128]{2,1,0:T(8,128)(2,1)}, bf16[8,128,128]{2,1,0:T(8,128)(2,1)}, u32[]{:S(2)}, u32[]{:S(2)}) collective-permute-start(bf16[8,128,128]{2,1,0:T(8,128)(2,1)} %slice.33), channel_id=1, source_target_pairs={{0,192},{64,0},{128,64},{192,128},{1,193},{65,1},{129,65},{193,129... | collective-permute-start | bytes 786440 | tf_op jit(solution)/shard_map/ppermute | solution.py:74
  68.1 9.5 %collective-permute-start.5 = (bf16[8,128,128]{2,1,0:T(8,128)(2,1)}, bf16[8,128,128]{2,1,0:T(8,128)(2,1)}, u32[]{:S(2)}, u32[]{:S(2)}) collective-permute-start(bf16[8,128,128]{2,1,0:T(8,128)(2,1)} %slice.32), channel_id=1, source_target_pairs={{0,64},{64,128},{128,192},{192,0},{1,65},{65,129},{129,193},{193,1... | collective-permute-start | bytes 786440 | tf_op jit(solution)/shard_map/ppermute | solution.py:73
  77.6 2.2 %collective-permute-start.7 = (bf16[8,128,128]{2,1,0:T(8,128)(2,1)}, bf16[8,128,128]{2,1,0:T(8,128)(2,1)S(1)}, u32[]{:S(2)}, u32[]{:S(2)}) collective-permute-start(bf16[8,128,128]{2,1,0:T(8,128)(2,1)} %collective-permute-done.5.rest_3_), channel_id=1, source_target_pairs={{0,1},{1,0},{2,3},{3,2},{4,5},{5,4},{6,7},{7,6},{8,9},{9,8},{10,11... | collective-permute-start | bytes 786440 | tf_op jit(solution)/shard_map/ppermute | solution.py:79
  78.4 1.7 %collective-permute-start.8 = (bf16[8,128,128]{2,1,0:T(8,128)(2,1)}, bf16[8,128,128]{2,1,0:T(8,128)(2,1)S(1)}, u32[]{:S(2)}, u32[]{:S(2)}) collective-permute-start(bf16[8,128,128]{2,1,0:T(8,128)(2,1)} %collective-permute-done.6.rest_4_), channel_id=1, source_target_pairs={{0,1},{1,0},{2,3},{3,2},{4,5},{5,4},{6,7},{7,6},{8,9},{9,8},{10,11... | collective-permute-start | bytes 786440 | tf_op jit(solution)/shard_map/ppermute | solution.py:79
  78.4 13.4 %copy-start.10 = (bf16[512,128]{1,0:T(8,128)(2,1)S(1)}, bf16[512,128]{1,0:T(8,128)(2,1)}, u32[]{:S(2)}) copy-start(bf16[512,128]{1,0:T(8,128)(2,1)} %param.15) | copy-start | bytes 393220
  84.5 8.4 %collective-permute-start.10 = (f32[136,128]{1,0:T(8,128)S(1)}, f32[136,128]{1,0:T(8,128)S(1)}, u32[]{:S(2)}, u32[]{:S(2)}) collective-permute-start(f32[136,128]{1,0:T(8,128)S(1)} %get-tuple-element.86), channel_id=1, source_target_pairs={{0,2},{2,0},{1,3},{3,1},{4,6},{6,4},{5,7},{7,5},{8,10},{10,8},{9,1... | collective-permute-start | bytes 208904 | tf_op jit(solution)/shard_map/ppermute | solution.py:79
  85.1 17.2 %all-to-all-start.2 = ((bf16[16,2,32,128]{3,2,1,0:T(8,128)(2,1)}), bf16[16,2,32,128]{3,2,1,0:T(8,128)(2,1)S(1)}, u32[]{:S(2)}, u32[]{:S(2)}) async-start(bf16[16,2,32,128]{3,2,1,0:T(8,128)(2,1)} %copy-done.1), calls=%async_computation.2 | async-start | bytes 524288 | tf_op jit(solution)/shard_map/all_to_all | solution.py:462
  91.8 3.3 %collective-permute-start.12 = (bf16[512,128]{1,0:T(8,128)(2,1)S(1)}, bf16[512,128]{1,0:T(8,128)(2,1)S(1)}, u32[]{:S(2)}, u32[]{:S(2)}) collective-permute-start(bf16[512,128]{1,0:T(8,128)(2,1)S(1)} %copy-done.10), channel_id=1, source_target_pairs={{0,1},{1,0},{2,3},{3,2},{4,5},{5,4},{6,7},{7,6},{8,9},{9,8},{10,11... | collective-permute-start | bytes 393224 | tf_op jit(solution)/shard_map/ppermute | solution.py:79
  92.9 2.3 %collective-permute-start.11 = (f32[2,136,128]{2,1,0:T(8,128)S(1)}, f32[2,136,128]{2,1,0:T(8,128)S(1)}, u32[]{:S(2)}, u32[]{:S(2)}) collective-permute-start(f32[2,136,128]{2,1,0:T(8,128)S(1)} %get-tuple-element.84), channel_id=1, source_target_pairs={{0,1},{1,0},{2,3},{3,2},{4,5},{5,4},{6,7},{7,6},{8,9},{9,8},{10,11... | collective-permute-start | bytes 417800 | tf_op jit(solution)/shard_map/ppermute | solution.py:79
  102.3 7.2 %collective-permute-start.9 = (bf16[8,2,2,32,128]{4,3,2,1,0:T(8,128)(2,1)S(1)}, bf16[8,2,2,32,128]{4,3,2,1,0:T(8,128)(2,1)S(1)}, u32[]{:S(2)}, u32[]{:S(2)}) collective-permute-start(bf16[8,2,2,32,128]{4,3,2,1,0:T(8,128)(2,1)S(1)} %bitcast.39), channel_id=1, source_target_pairs={{0,32},{32,0},{1,33},{33,1},{2,34},{34,2},{3,35},{35,3},{4,36},{36... | collective-permute-start | bytes 786440 | tf_op jit(solution)/shard_map/ppermute | solution.py:79
  109.6 10.3 %collective-permute-start.16 = (bf16[2,8,2,2,32,128]{5,4,3,2,1,0:T(8,128)(2,1)S(1)}, bf16[2,8,2,2,32,128]{5,4,3,2,1,0:T(8,128)(2,1)S(1)}, u32[]{:S(2)}, u32[]{:S(2)}) collective-permute-start(bf16[2,8,2,2,32,128]{5,4,3,2,1,0:T(8,128)(2,1)S(1)} %pad_maximum_fusion.refs_0_), channel_id=1, source_target_pairs={{0,192},{64,0},{128,64},{192,128},{1,193},{65,1},{129,65},{193,129... | collective-permute-start | bytes 1572872 | tf_op jit(solution)/shard_map/ppermute | solution.py:491
  109.7 11.5 %collective-permute-start.15 = (bf16[2,8,2,2,32,128]{5,4,3,2,1,0:T(8,128)(2,1)S(1)}, bf16[2,8,2,2,32,128]{5,4,3,2,1,0:T(8,128)(2,1)S(1)}, u32[]{:S(2)}, u32[]{:S(2)}) collective-permute-start(bf16[2,8,2,2,32,128]{5,4,3,2,1,0:T(8,128)(2,1)S(1)} %pad_maximum_fusion.refs_0_), channel_id=1, source_target_pairs={{0,64},{64,128},{128,192},{192,0},{1,65},{65,129},{129,193},{193,1... | collective-permute-start | bytes 1572872 | tf_op jit(solution)/shard_map/ppermute | solution.py:490
  111.2 28.9 %collective-permute-start.14 = (bf16[64,72,128]{2,1,0:T(8,128)(2,1)S(1)}, bf16[64,72,128]{2,1,0:T(8,128)(2,1)S(1)}, u32[]{:S(2)}, u32[]{:S(2)}) collective-permute-start(bf16[64,72,128]{2,1,0:T(8,128)(2,1)S(1)} %all-to-all-done.heavy.h0), channel_id=1, source_target_pairs={{0,2},{2,0},{1,3},{3,1},{4,6},{6,4},{5,7},{7,5},{8,10},{10,8},{9,1... | collective-permute-start | bytes 3538952 | tf_op jit(solution)/shard_map/ppermute | solution.py:79
  124.2 7.6 %collective-permute-start.20 = (bf16[2,32,2,32,128]{4,3,2,1,0:T(8,128)(2,1)S(1)}, bf16[2,32,2,32,128]{4,3,2,1,0:T(8,128)(2,1)S(1)}, u32[]{:S(2)}, u32[]{:S(2)}) collective-permute-start(bf16[2,32,2,32,128]{4,3,2,1,0:T(8,128)(2,1)S(1)} %get-tuple-element.76), channel_id=1, source_target_pairs={{0,1},{1,0},{2,3},{3,2},{4,5},{5,4},{6,7},{7,6},{8,9},{9,8},{10,11... | collective-permute-start | bytes 3145736 | tf_op jit(solution)/shard_map/ppermute | solution.py:79
  128.4 3.0 %collective-permute-start.19 = (bf16[2,16,2,32,128]{4,3,2,1,0:T(8,128)(2,1)S(1)}, bf16[2,16,2,32,128]{4,3,2,1,0:T(8,128)(2,1)S(1)}, u32[]{:S(2)}, u32[]{:S(2)}) collective-permute-start(bf16[2,16,2,32,128]{4,3,2,1,0:T(8,128)(2,1)S(1)} %get-tuple-element.75), channel_id=1, source_target_pairs={{0,1},{1,0},{2,3},{3,2},{4,5},{5,4},{6,7},{7,6},{8,9},{9,8},{10,11... | collective-permute-start | bytes 1572872 | tf_op jit(solution)/shard_map/ppermute | solution.py:79
  128.6 9.6 %collective-permute-start.18 = (bf16[1,8,2,2,32,128]{5,4,3,2,1,0:T(8,128)(2,1)S(1)}, bf16[1,8,2,2,32,128]{5,4,3,2,1,0:T(8,128)(2,1)S(1)}, u32[]{:S(2)}, u32[]{:S(2)}) collective-permute-start(bf16[1,8,2,2,32,128]{5,4,3,2,1,0:T(8,128)(2,1)S(1)} %slice.28), channel_id=1, source_target_pairs={{0,192},{64,0},{128,64},{192,128},{1,193},{65,1},{129,65},{193,129... | collective-permute-start | bytes 786440 | tf_op jit(solution)/shard_map/ppermute | solution.py:496
  128.7 9.5 %collective-permute-start.17 = (bf16[1,8,2,2,32,128]{5,4,3,2,1,0:T(8,128)(2,1)S(1)}, bf16[1,8,2,2,32,128]{5,4,3,2,1,0:T(8,128)(2,1)S(1)}, u32[]{:S(2)}, u32[]{:S(2)}) collective-permute-start(bf16[1,8,2,2,32,128]{5,4,3,2,1,0:T(8,128)(2,1)S(1)} %slice.27), channel_id=1, source_target_pairs={{0,64},{64,128},{128,192},{192,0},{1,65},{65,129},{129,193},{193,1... | collective-permute-start | bytes 786440 | tf_op jit(solution)/shard_map/ppermute | solution.py:495
  131.5 9.3 %collective-permute-start.13 = (bf16[64,72,128]{2,1,0:T(8,128)(2,1)S(1)}, bf16[64,72,128]{2,1,0:T(8,128)(2,1)S(1)}, u32[]{:S(2)}, u32[]{:S(2)}) collective-permute-start(bf16[64,72,128]{2,1,0:T(8,128)(2,1)S(1)} %all-to-all-done.heavy.h0), channel_id=1, source_target_pairs={{0,1},{1,0},{2,3},{3,2},{4,5},{5,4},{6,7},{7,6},{8,9},{9,8},{10,11... | collective-permute-start | bytes 3538952 | tf_op jit(solution)/shard_map/ppermute | solution.py:79
  131.8 12.1 %copy-start.8 = (f32[128]{0:T(128)S(1)}, f32[128]{0:T(128)}, u32[]{:S(2)}) copy-start(f32[128]{0:T(128)} %param.16) | copy-start | bytes 1540
  140.1 3.8 %collective-permute-start.21 = (bf16[64,72,128]{2,1,0:T(8,128)(2,1)S(1)}, bf16[64,72,128]{2,1,0:T(8,128)(2,1)S(1)}, u32[]{:S(2)}, u32[]{:S(2)}) collective-permute-start(bf16[64,72,128]{2,1,0:T(8,128)(2,1)S(1)} %collective-permute-done.14.h2), channel_id=1, source_target_pairs={{0,1},{1,0},{2,3},{3,2},{4,5},{5,4},{6,7},{7,6},{8,9},{9,8},{10,11... | collective-permute-start | bytes 3538952 | tf_op jit(solution)/shard_map/ppermute | solution.py:79
  140.7 3.2 %collective-permute-start.22 = (bf16[2,16,2,32,128]{4,3,2,1,0:T(8,128)(2,1)S(1)}, bf16[2,16,2,32,128]{4,3,2,1,0:T(8,128)(2,1)S(1)}, u32[]{:S(2)}, u32[]{:S(2)}) collective-permute-start(bf16[2,16,2,32,128]{4,3,2,1,0:T(8,128)(2,1)S(1)} %get-tuple-element.80), channel_id=1, source_target_pairs={{0,1},{1,0},{2,3},{3,2},{4,5},{5,4},{6,7},{7,6},{8,9},{9,8},{10,11... | collective-permute-start | bytes 1572872 | tf_op jit(solution)/shard_map/ppermute | solution.py:79
  (7 other events, 47.9 us)
